TPU v7x, 256 devices: a whole 4x4x8 slice. The times are simulated.
256 devices in a mesh: seq: 64 (over y, z, core), tp: 4 (over x).
Axes of the slice: x: 4, y: 4, z: 8, core: 2. Of those that a mesh axis runs over, the one named last changes fastest.
Arguments:
- head_input: bfloat16 [49152, 8192], P('seq', 'tp'), may hold values from -6 to 6
- gate_input: bfloat16 [49152, 8192], P('seq', 'tp'), may hold values from -16 to 16
- step_size: float32 [49152, 64], P('seq', 'tp'), may hold values from 0.01 to 0.04
- input_proj: bfloat16 [49152, 128], P('seq'), may hold values from -6 to 6
- output_proj: bfloat16 [49152, 128], P('seq'), may hold values from -6 to 6
- decay_rate: float32 [64], P('tp'), may hold values from 0.0009765625 to 2, as said below
- skip_gain: float32 [64], P('tp'), may hold values from 0.5 to 1.5
- norm_gain: float32 [8192], P('tp'), may hold values from 0.5 to 1.5
- doc_lengths: int32 [16], replicated, may hold values from 1 to 12288, 49152 in all
Outputs:
- mixed_out: bfloat16 [49152, 8192], P('seq', 'tp')
- group_states: float32 [192, 64, 128, 128], P('seq', 'tp')
Inputs may be any that keep to these rules, and one draw needn't show every extreme that they name: `doc_lengths`: the lengths sum to 49152; the longest is exactly 12288. `decay_rate`: positive rates.
All inputs are finite; a program needn't handle non-finite values.
Results may differ from a plain program's by a relative error of at most 0.0056.
Values sent between devices are 32-bit elements; how exact they have to be, the bound alone decides.
No kernel may reach another device: no remote copies, remote signals or barrier semaphores. Data moves between devices by JAX's collectives and lax.ppermute only.
A program may use at most 192 MiB of HBM per device.

v0:
```python
import functools
import jax
import jax.numpy as jnp
from jax import lax
from jax.experimental import pallas as pl
from jax.experimental.pallas import tpu as pltpu
from jax.sharding import PartitionSpec as P

P_SIZE = 128
N = 128
Q = 256
F32 = jnp.float32
BF16 = jnp.bfloat16
Y_SIZE = 4
Z_SIZE = 8
NT = (((1,), (1,)), ((), ()))
TN = (((0,), (0,)), ((), ()))


def seq_index(y, z, core):
    return ((y % Y_SIZE) * Z_SIZE + (z % Z_SIZE)) * 2 + core


def seq_pairs(move):
    pairs = []
    for y in range(Y_SIZE):
        for z in range(Z_SIZE):
            for core in range(2):
                pairs.append((seq_index(y, z, core), seq_index(*move(y, z, core))))
    return pairs


CORE_SWAP = seq_pairs(lambda y, z, core: (y, z, 1 - core))
NEXT_ROW = seq_pairs(lambda y, z, core: (y + 1, z, core))
RINGS = [
    [seq_index(y, z, core) for z in range(Z_SIZE)] for y in range(Y_SIZE) for core in range(2)
]


def group_bounds(doc_ref, start):
    last = start + (Q - 1)
    doc_first = jnp.int32(0)
    next_end = jnp.int32(2147483647)
    end = jnp.int32(0)
    for k in range(doc_ref.shape[0]):
        end = end + doc_ref[k]
        doc_first = jnp.where(end <= last, end, doc_first)
        next_end = jnp.minimum(next_end, jnp.where(end >= start, end, 2147483647))
    return doc_first, next_end


def split3(values):
    high = values.astype(BF16)
    rest = values - high.astype(F32)
    mid = rest.astype(BF16)
    low = (rest - mid.astype(F32)).astype(BF16)
    return high, mid, low


def column_logs(step, rate_ref):
    head_rows = lax.broadcasted_iota(jnp.int32, step.shape, 0)
    terms = jnp.zeros_like(step)
    for head in range(step.shape[0]):
        terms = jnp.where(head_rows == head, -rate_ref[head] * step, terms)
    rows = lax.broadcasted_iota(jnp.int32, (Q, Q), 0)
    cols = lax.broadcasted_iota(jnp.int32, (Q, Q), 1)
    lower = jnp.where(cols <= rows, 1.0, 0.0).astype(BF16)
    return sum(
        lax.dot_general(lower, part, NT, preferred_element_type=F32) for part in split3(terms)
    )


def head_columns(values, head):
    return jnp.broadcast_to(values[:, head : head + 1], (values.shape[0], P_SIZE))


def scaled_pair(x, scale, pair):
    parts = []
    for head in (2 * pair, 2 * pair + 1):
        columns = x[:, head * P_SIZE : (head + 1) * P_SIZE].astype(F32)
        parts.append((columns * head_columns(scale, head)).astype(BF16))
    return jnp.concatenate(parts, axis=1)


def states_kernel(
    heads,
    groups,
    doc_hbm,
    rate_hbm,
    step_hbm,
    b_hbm,
    x_hbm,
    state_ref,
    before_ref,
    pass_ref,
    doc_ref,
    rate_ref,
    step_ref,
    b_ref,
    x_ref,
    small_sems,
    wide_sems,
):
    small = [
        pltpu.make_async_copy(src, dst, small_sems.at[i])
        for i, (src, dst) in enumerate(
            ((step_hbm, step_ref), (rate_hbm, rate_ref), (doc_hbm, doc_ref), (b_hbm, b_ref))
        )
    ]
    wide = [
        pltpu.make_async_copy(
            x_hbm.at[pl.ds(group * Q, Q), :], x_ref.at[group], wide_sems.at[group]
        )
        for group in range(groups)
    ]
    for copy in small + wide:
        copy.start()
    for copy in small:
        copy.wait()
    pass_ref[...] = jnp.ones_like(pass_ref)
    base = lax.axis_index("seq") * (groups * Q)
    prepared = []
    reach = jnp.ones((1, heads), F32)
    for group in range(groups):
        start = base + group * Q
        doc_first, next_end = group_bounds(doc_ref, start)
        step = step_ref[:, group * Q : (group + 1) * Q]
        logs = column_logs(step, rate_ref)
        scale = jnp.exp(-logs) * step.T
        final = jnp.exp(logs[Q - 1 : Q, :])
        passing = jnp.where(start + (Q - 1) < next_end, final, 0.0)
        positions = lax.broadcasted_iota(jnp.int32, (N, Q), 1) + start
        b_rows = b_ref[group * Q : (group + 1) * Q, :].astype(F32).T
        tail_b = jnp.where(positions >= doc_first, b_rows, 0.0).astype(BF16)
        reach = reach * passing
        pass_ref[group + 1 : group + 2, 0:heads] = reach
        prepared.append((scale, final, passing, tail_b))
    for head in range(heads):
        state_ref[head, N : N + 8, :] = jnp.broadcast_to(reach[:, head : head + 1], (8, P_SIZE))
    for group in range(groups):
        scale, final, passing, tail_b = prepared[group]
        wide[group].wait()
        x = x_ref.at[group]
        for pair in range(heads // 2):
            scaled = scaled_pair(x, scale, pair)
            product = jnp.dot(tail_b, scaled, preferred_element_type=F32)
            for part in range(2):
                head = 2 * pair + part
                state = product[:, part * P_SIZE : (part + 1) * P_SIZE] * final[:, head : head + 1]
                if group > 0:
                    state = state + before_ref[group - 1, head] * passing[:, head : head + 1]
                if group < groups - 1:
                    before_ref[group, head] = state
                else:
                    state_ref[head, 0:N, :] = state


def inside_kernel(
    heads,
    groups,
    doc_ref,
    rate_ref,
    skip_ref,
    step_ref,
    b_ref,
    c_ref,
    x_ref,
    gate_ref,
    after_ref,
    u_ref,
    v_ref,
):
    base = lax.axis_index("seq") * (groups * Q)
    rows = lax.broadcasted_iota(jnp.int32, (Q, Q), 0)
    cols = lax.broadcasted_iota(jnp.int32, (Q, Q), 1)
    for group in range(groups):
        start = base + group * Q
        block = slice(group * Q, (group + 1) * Q)
        _, next_end = group_bounds(doc_ref, start)
        step = step_ref[:, block]
        logs = column_logs(step, rate_ref)
        scale = jnp.exp(-logs) * step.T
        decay = jnp.exp(logs)
        positions = lax.broadcasted_iota(jnp.int32, (Q, heads), 0) + start
        entry = jnp.where(positions < next_end, decay, 0.0)
        first = jnp.zeros((Q, Q), jnp.int32)
        end = jnp.int32(0)
        for k in range(doc_ref.shape[0]):
            end = end + doc_ref[k]
            first = jnp.where(end - start <= rows, end - start, first)
        scores = lax.dot_general(c_ref[block, :], b_ref[block, :], NT, preferred_element_type=F32)
        masked = jnp.where((cols <= rows) & (cols >= first), scores, 0.0).astype(BF16)
        for pair in range(heads // 2):
            scaled = scaled_pair(x_ref.at[block, :], scale, pair)
            product = jnp.dot(masked, scaled, preferred_element_type=F32)
            for part in range(2):
                head = 2 * pair + part
                span = slice(head * P_SIZE, (head + 1) * P_SIZE)
                gate = gate_ref[block, span].astype(F32)
                active = gate / (1.0 + jnp.exp(-gate))
                inside = product[:, part * P_SIZE : (part + 1) * P_SIZE]
                inside = inside * head_columns(decay, head)
                inside = inside + skip_ref[head] * x_ref[block, span].astype(F32)
                u_ref[block, span] = inside * active
                v_ref[block, span] = head_columns(entry, head) * active


def join_cores_kernel(own_ref, other_ref, joined_ref):
    core = lax.rem(lax.axis_index("seq"), 2)
    half = joined_ref.shape[0]
    for slot in range(half):
        head = core * half + slot
        own, other = own_ref[head], other_ref[head]
        earlier = jnp.where(core == 0, own, other)
        later = jnp.where(core == 0, other, own)
        later_pass = later[N : N + 1, :]
        joined_ref[slot, 0:N, :] = later_pass * earlier[0:N, :] + later[0:N, :]
        joined_ref[slot, N : N + 8, :] = later_pass * earlier[N : N + 8, :]


def row_total_kernel(parts_ref, after_ref, total_ref):
    total = parts_ref[0, 0:N, :]
    for chip in range(1, Z_SIZE):
        total = parts_ref[chip, N : N + 1, :] * total + parts_ref[chip, 0:N, :]
    total_ref[...] = total


def entering_kernel(parts_ref, carried_ref, entering_ref):
    row = lax.axis_index("seq") // (2 * Z_SIZE)
    state = jnp.where(row > 0, carried_ref[...], 0.0)
    for chip in range(Z_SIZE):
        entering_ref[chip] = state
        if chip < Z_SIZE - 1:
            state = parts_ref[chip, N : N + 1, :] * state + parts_ref[chip, 0:N, :]


def outputs_kernel(
    heads,
    groups,
    own_ref,
    swapped_ref,
    other_ref,
    before_ref,
    pass_ref,
    c_ref,
    u_ref,
    v_ref,
    gated_ref,
    squares_ref,
    states_hbm,
    first_ref,
    states_ref,
    sems,
):
    core = lax.rem(lax.axis_index("seq"), 2)
    half = heads // 2
    for head in range(heads):
        here = core == (head // half)
        chip_state = jnp.where(here, own_ref[head % half], swapped_ref[head % half])
        joined = other_ref[head, N : N + 1, :] * chip_state + other_ref[head, 0:N, :]
        first_ref[head] = jnp.where(core == 0, chip_state, joined)
    ones = jnp.ones((8, P_SIZE), F32)
    copies = []
    for group in range(groups):
        block = slice(group * Q, (group + 1) * Q)
        reach = pass_ref[group : group + 1, 0:heads]
        squares = jnp.zeros((Q, P_SIZE), F32)
        for pair in range(heads // 2):
            both = []
            for part in range(2):
                head = 2 * pair + part
                state = first_ref[head]
                if group > 0:
                    state = state * reach[:, head : head + 1] + before_ref[group - 1, head]
                states_ref[group, head] = state.T
                both.append(state.astype(BF16))
            carried = jnp.dot(
                c_ref[block, :], jnp.concatenate(both, axis=1), preferred_element_type=F32
            )
            span = slice(2 * pair * P_SIZE, 2 * (pair + 1) * P_SIZE)
            gated = u_ref[block, span] + v_ref[block, span] * carried
            gated_ref[block, span] = gated
            square = gated * gated
            squares = squares + square[:, 0:P_SIZE] + square[:, P_SIZE:]
        copy = pltpu.make_async_copy(states_ref.at[group], states_hbm.at[group], sems.at[group])
        copy.start()
        copies.append(copy)
        squares_ref[:, block] = lax.dot_general(
            ones, squares, NT, precision=lax.Precision.HIGHEST, preferred_element_type=F32
        )
    for copy in copies:
        copy.wait()


SCALE_ROWS = 128


def scale_kernel(inner, gated_ref, gain_ref, own_ref, a_ref, b_ref, c_ref, out_hbm, out_ref, sems):
    mean = (own_ref[...] + a_ref[...] + b_ref[...] + c_ref[...]) * (1.0 / inner)
    scale = lax.rsqrt(mean + 1e-05)
    pick = jnp.where(lax.broadcasted_iota(jnp.int32, (8, P_SIZE), 0) == 0, 1.0, 0.0)
    copies = []
    for chunk in range(gated_ref.shape[0] // SCALE_ROWS):
        block = slice(chunk * SCALE_ROWS, (chunk + 1) * SCALE_ROWS)
        column = lax.dot_general(
            scale[:, block],
            pick,
            TN,
            precision=lax.Precision.HIGHEST,
            preferred_element_type=F32,
        )
        for tile in range(gated_ref.shape[1] // P_SIZE):
            span = slice(tile * P_SIZE, (tile + 1) * P_SIZE)
            out_ref[block, span] = (gated_ref[block, span] * column * gain_ref[:, span]).astype(
                BF16
            )
        copy = pltpu.make_async_copy(
            out_ref.at[pl.ds(chunk * SCALE_ROWS, SCALE_ROWS), :],
            out_hbm.at[pl.ds(chunk * SCALE_ROWS, SCALE_ROWS), :],
            sems.at[chunk],
        )
        copy.start()
        copies.append(copy)
    for copy in copies:
        copy.wait()


def cost(flops, bytes_accessed):
    return pl.CostEstimate(flops=flops, bytes_accessed=bytes_accessed, transcendentals=0)


def params(mebibytes):
    return pltpu.CompilerParams(vmem_limit_bytes=mebibytes * 1024 * 1024)


def local(
    head_input,
    gate_input,
    step_size,
    input_proj,
    output_proj,
    decay_rate,
    skip_gain,
    norm_gain,
    doc_lengths,
):
    row_count, width = head_input.shape
    heads = step_size.shape[1]
    half = heads // 2
    groups = row_count // Q
    sds = jax.ShapeDtypeStruct
    step_rows = step_size.T
    gain = norm_gain.reshape(1, width)
    smem = pl.BlockSpec(memory_space=pltpu.SMEM)
    vmem = pl.BlockSpec(memory_space=pltpu.VMEM)
    hbm = pl.BlockSpec(memory_space=pltpu.HBM)
    anywhere = pl.BlockSpec(memory_space=pl.ANY)
    dma = pltpu.SemaphoreType.DMA

    state, before, passes = pl.pallas_call(
        functools.partial(states_kernel, heads, groups),
        in_specs=[hbm] * 5,
        out_specs=[vmem] * 3,
        out_shape=[
            sds((heads, N + 8, P_SIZE), F32),
            sds((groups - 1, heads, N, P_SIZE), F32),
            sds((8, P_SIZE), F32),
        ],
        scratch_shapes=[
            pltpu.SMEM(doc_lengths.shape, jnp.int32),
            pltpu.SMEM(decay_rate.shape, F32),
            pltpu.VMEM((heads, row_count), F32),
            pltpu.VMEM((row_count, N), BF16),
            pltpu.VMEM((groups, Q, width), BF16),
            dma((4,)),
            dma((groups,)),
        ],
        compiler_params=params(24),
        cost_estimate=cost(400_000_000, 6_000_000),
        name="states",
    )(doc_lengths, decay_rate, step_rows, input_proj, head_input)

    other = lax.ppermute(state, "seq", CORE_SWAP)

    joined = pl.pallas_call(
        join_cores_kernel,
        out_shape=sds((half, N + 8, P_SIZE), F32),
        compiler_params=params(8),
        cost_estimate=cost(1_000_000, 1_700_000),
        name="join_cores",
    )(state, other)

    parts = lax.all_to_all(
        joined, "seq", split_axis=0, concat_axis=0, axis_index_groups=RINGS, tiled=True
    )

    u, v = pl.pallas_call(
        functools.partial(inside_kernel, heads, groups),
        in_specs=[smem, smem, smem, vmem, vmem, vmem, vmem, vmem, anywhere],
        out_specs=[vmem, vmem],
        out_shape=[sds((row_count, width), F32), sds((row_count, width), F32)],
        compiler_params=params(28),
        cost_estimate=cost(8_000_000_000, 20_000_000),
        name="inside",
    )(
        doc_lengths,
        decay_rate,
        skip_gain,
        step_rows,
        input_proj,
        output_proj,
        head_input,
        gate_input,
        joined,
    )

    total = pl.pallas_call(
        row_total_kernel,
        in_specs=[vmem, anywhere],
        out_shape=sds((N, P_SIZE), F32),
        compiler_params=params(8),
        cost_estimate=cost(300_000, 600_000),
        name="row_total",
    )(parts, u)
    carried = lax.ppermute(total, "seq", NEXT_ROW)
    entering = pl.pallas_call(
        entering_kernel,
        out_shape=sds((Z_SIZE, N, P_SIZE), F32),
        compiler_params=params(8),
        cost_estimate=cost(300_000, 1_100_000),
        name="entering",
    )(parts, carried)

    own = lax.all_to_all(
        entering, "seq", split_axis=0, concat_axis=0, axis_index_groups=RINGS, tiled=True
    )
    swapped = lax.ppermute(own, "seq", CORE_SWAP)

    gated, squares, group_states = pl.pallas_call(
        functools.partial(outputs_kernel, heads, groups),
        in_specs=[vmem] * 8,
        out_specs=[vmem, vmem, hbm],
        out_shape=[
            sds((row_count, width), F32),
            sds((8, row_count), F32),
            sds((groups, heads, P_SIZE, N), F32),
        ],
        scratch_shapes=[
            pltpu.VMEM((heads, N, P_SIZE), F32),
            pltpu.VMEM((groups, heads, P_SIZE, N), F32),
            dma((groups,)),
        ],
        compiler_params=params(34),
        cost_estimate=cost(400_000_000, 18_000_000),
        name="outputs",
    )(own, swapped, other, before, passes, output_proj, u, v)

    tp_size = 4
    sums = [
        lax.ppermute(squares, "tp", [(i, (i + k) % tp_size) for i in range(tp_size)])
        for k in range(1, tp_size)
    ]
    mixed_out = pl.pallas_call(
        functools.partial(scale_kernel, width * tp_size),
        in_specs=[vmem] * 6,
        out_specs=hbm,
        out_shape=sds((row_count, width), BF16),
        scratch_shapes=[pltpu.VMEM((row_count, width), BF16), dma((row_count // SCALE_ROWS,))],
        compiler_params=params(16),
        cost_estimate=cost(5_000_000, 6_500_000),
        name="scale",
    )(gated, gain, squares, *sums)
    return (mixed_out, group_states)


def solution(mesh):
    return jax.shard_map(
        local,
        mesh=mesh,
        in_specs=(
            P("seq", "tp"),
            P("seq", "tp"),
            P("seq", "tp"),
            P("seq", None),
            P("seq", None),
            P("tp"),
            P("tp"),
            P("tp"),
            P(),
        ),
        out_specs=(P("seq", "tp"), P("seq", "tp", None, None)),
        check_vma=False,
    )
```

profile of v0, /device:TPU:1, one launch (start us, length us, event | category | flops | bytes accessed | tf_op | source)
XLA Modules:
  0.0 91.7 jit_solution(14044479762151806270)
XLA Ops:
  0.6 0.0 copy-start.4
  0.6 1.9 %copy-done.4 = bf16[768,2048]{1,0:T(8,128)(2,1)S(1)} copy-done((bf16[768,2048]{1,0:T(8,128)(2,1)S(1)}, bf16[768,2048]{1,0:T(8,128)(2,1)}, u32[]{:S(2)}) %copy-start.4) | copy-done | bytes 3145752
  2.5 0.0 copy-start.9
  2.5 0.9 %copy-done.9 = bf16[768,128]{1,0:T(8,128)(2,1)S(1)} copy-done((bf16[768,128]{1,0:T(8,128)(2,1)S(1)}, bf16[768,128]{1,0:T(8,128)(2,1)}, u32[]{:S(2)}) %copy-start.9) | copy-done | bytes 196632
  3.5 0.0 copy-start.11
  3.5 0.8 copy-done.11
  4.3 0.7 copy-done.14
  4.9 0.7 copy-done.16
  5.6 0.0 copy-start.17
  5.6 0.0 copy-start.19
  5.6 4.2 %states.1 = (f32[16,136,128]{2,1,0:T(8,128)S(1)}, f32[2,16,128,128]{3,2,1,0:T(8,128)S(1)}, f32[8,128]{1,0:T(8,128)S(1)}) custom-call(s32[16]{0:T(128)S(1)} %copy-done.14, f32[16]{0:T(128)S(1)} %copy-done.16, f32[16,768]{1,0:T(8,128)S(1)} %bitcast.2, bf16[768,128]{1,0:T(8,128)(2,1)S(1)} %copy-done.9, bf16[768,2048]{1,0:T(8,128)(2,1)S(1)} %copy-done.4), custom_call_target="tpu_custom_call" | custom-call | flops 400000000 | bytes 6000000 | tf_op jit(solution)/shard_map/states/pallas_call | solution.py:360
  9.8 0.0 copy-start.6
  9.8 1.3 %copy-done.6 = f32[2,16,128,128]{3,2,1,0:T(8,128)} copy-done((f32[2,16,128,128]{3,2,1,0:T(8,128)}, f32[2,16,128,128]{3,2,1,0:T(8,128)S(1)}, u32[]{:S(2)}) %copy-start.6) | copy-done | bytes 2097176
  11.1 3.2 %collective-permute-start = (f32[16,136,128]{2,1,0:T(8,128)S(1)}, f32[16,136,128]{2,1,0:T(8,128)S(1)}, u32[]{:S(2)}, u32[]{:S(2)}) collective-permute-start(f32[16,136,128]{2,1,0:T(8,128)S(1)} %get-tuple-element.10.own_ref), channel_id=1, source_target_pairs={{0,4},{4,0},{8,12},{12,8},{16,20},{20,16},{24,28},{28,24},{32,36},... | collective-permute-start | bytes 3342344 | tf_op jit(solution)/shard_map/ppermute | solution.py:383
  14.3 2.4 %collective-permute-done.other_ref = f32[16,136,128]{2,1,0:T(8,128)S(1)} collective-permute-done((f32[16,136,128]{2,1,0:T(8,128)S(1)}, f32[16,136,128]{2,1,0:T(8,128)S(1)}, u32[]{:S(2)}, u32[]{:S(2)}) %collective-permute-start) | collective-permute-done | bytes 1114144 | tf_op jit(solution)/shard_map/ppermute | solution.py:383
  16.7 0.9 join_cores.1.after_ref
  17.6 6.4 %all-to-all-start = ((f32[8,136,128]{2,1,0:T(8,128)}), f32[8,136,128]{2,1,0:T(8,128)S(1)}, u32[]{:S(2)}, u32[]{:S(2)}) async-start(f32[8,136,128]{2,1,0:T(8,128)} %join_cores.1.after_ref), calls=%async_computation | async-start | bytes 1114112 | tf_op jit(solution)/shard_map/all_to_all | solution.py:393
  24.1 0.0 copy-done.8
  24.1 0.0 copy-done.10
  24.1 0.0 copy-done.12
  24.1 0.0 copy-done.15
  24.1 0.0 copy-done.17
  24.1 0.0 copy-done.19
  24.1 0.0 copy-start.5
  24.2 1.9 %copy-done.5 = bf16[768,2048]{1,0:T(8,128)(2,1)S(1)} copy-done((bf16[768,2048]{1,0:T(8,128)(2,1)S(1)}, bf16[768,2048]{1,0:T(8,128)(2,1)}, u32[]{:S(2)}) %copy-start.5) | copy-done | bytes 3145752
  26.0 1.9 %copy-done.18 = bf16[768,2048]{1,0:T(8,128)(2,1)S(1)} copy-done((bf16[768,2048]{1,0:T(8,128)(2,1)S(1)}, bf16[768,2048]{1,0:T(8,128)(2,1)}, u32[]{:S(2)}) %copy-start.18) | copy-done | bytes 3145752
  27.9 9.1 %inside.1 = (f32[768,2048]{1,0:T(8,128)S(1)}, f32[768,2048]{1,0:T(8,128)S(1)}) custom-call(s32[16]{0:T(128)S(1)} %copy-done.15, f32[16]{0:T(128)S(1)} %copy-done.17, f32[16]{0:T(128)S(1)} %copy-done.19, f32[16,768]{1,0:T(8,128)S(1)} %bitcast.3, bf16[768,128]{1,0:T(8,128)(2,1)S(1)} %copy-done.10, bf16[768,128]{1,0:T(8,128)(2,1)S(1)} %copy-done.8, ...), custom_call_target="tpu_custom_call" | custom-call | flops 8000000000 | bytes 20000000 | tf_op jit(solution)/shard_map/inside/pallas_call | solution.py:397
  37.1 0.0 copy-start
  37.1 2.6 %copy-done = f32[768,2048]{1,0:T(8,128)} copy-done((f32[768,2048]{1,0:T(8,128)}, f32[768,2048]{1,0:T(8,128)S(1)}, u32[]{:S(2)}) %copy-start) | copy-done | bytes 6291480
  39.7 2.6 %copy-done.3 = f32[768,2048]{1,0:T(8,128)} copy-done((f32[768,2048]{1,0:T(8,128)}, f32[768,2048]{1,0:T(8,128)S(1)}, u32[]{:S(2)}) %copy-start.3) | copy-done | bytes 6291480
  42.3 0.4 all-to-all-done.parts_ref
  42.8 2.8 %copy-done.1 = f32[768,2048]{1,0:T(8,128)S(1)} copy-done((f32[768,2048]{1,0:T(8,128)S(1)}, f32[768,2048]{1,0:T(8,128)}, u32[]{:S(2)}) %copy-start.1) | copy-done | bytes 6291480
  45.6 1.6 %collective-permute-start.1 = (f32[128,128]{1,0:T(8,128)S(1)}, f32[128,128]{1,0:T(8,128)S(1)}, u32[]{:S(2)}, u32[]{:S(2)}) collective-permute-start(f32[128,128]{1,0:T(8,128)S(1)} %row_total.1), channel_id=1, source_target_pairs={{0,64},{4,68},{8,72},{12,76},{16,80},{20,84},{24,88},{28,92},{32,9... | collective-permute-start | bytes 196616 | tf_op jit(solution)/shard_map/ppermute | solution.py:425
  47.1 3.1 %collective-permute-done.1.carried_ref = f32[128,128]{1,0:T(8,128)S(1)} collective-permute-done((f32[128,128]{1,0:T(8,128)S(1)}, f32[128,128]{1,0:T(8,128)S(1)}, u32[]{:S(2)}, u32[]{:S(2)}) %collective-permute-start.1) | collective-permute-done | bytes 65568 | tf_op jit(solution)/shard_map/ppermute | solution.py:425
  50.3 20.5 %all_to_all.10.own_ref = f32[8,128,128]{2,1,0:T(8,128)S(1)} all-to-all(f32[8,128,128]{2,1,0:T(8,128)S(1)} %entering.1), channel_id=1, replica_groups={{0,8,16,24,32,40,48,56},{4,12,20,28,36,44,52,60},{64,72,80,88,96,104,11..., dimensions={0} | all-to-all | bytes 1048576 | tf_op jit(solution)/shard_map/all_to_all | solution.py:434
  70.7 4.0 %collective-permute-start.2 = (f32[8,128,128]{2,1,0:T(8,128)S(1)}, f32[8,128,128]{2,1,0:T(8,128)S(1)}, u32[]{:S(2)}, u32[]{:S(2)}) collective-permute-start(f32[8,128,128]{2,1,0:T(8,128)S(1)} %all_to_all.10.own_ref), channel_id=1, source_target_pairs={{0,4},{4,0},{8,12},{12,8},{16,20},{20,16},{24,28},{28,24},{32,36},... | collective-permute-start | bytes 1572872 | tf_op jit(solution)/shard_map/ppermute | solution.py:437
  74.7 1.5 %collective-permute-done.2.swapped_ref = f32[8,128,128]{2,1,0:T(8,128)S(1)} collective-permute-done((f32[8,128,128]{2,1,0:T(8,128)S(1)}, f32[8,128,128]{2,1,0:T(8,128)S(1)}, u32[]{:S(2)}, u32[]{:S(2)}) %collective-permute-start.2) | collective-permute-done | bytes 524320 | tf_op jit(solution)/shard_map/ppermute | solution.py:437
  76.3 0.0 copy-done.2
  76.3 0.0 copy-done.7
  76.3 6.2 %outputs.1 = (f32[768,2048]{1,0:T(8,128)S(1)}, f32[8,768]{1,0:T(8,128)S(1)}, f32[3,16,128,128]{3,2,1,0:T(8,128)}) custom-call(f32[8,128,128]{2,1,0:T(8,128)S(1)} %all_to_all.10.own_ref, f32[8,128,128]{2,1,0:T(8,128)S(1)} %collective-permute-done.2.swapped_ref, f32[16,136,128]{2,1,0:T(8,128)S(1)} %collective-permute-done.other_ref, ...), custom_call_target="tpu_custom_call" | custom-call | flops 400000000 | bytes 18000000 | tf_op jit(solution)/shard_map/outputs/pallas_call | solution.py:439
  82.5 2.6 %collective-permute-start.5 = (f32[8,768]{1,0:T(8,128)S(1)}, f32[8,768]{1,0:T(8,128)S(1)}, u32[]{:S(2)}, u32[]{:S(2)}) collective-permute-start(f32[8,768]{1,0:T(8,128)S(1)} %get-tuple-element.16.own_ref), channel_id=1, source_target_pairs={{0,3},{1,0},{2,1},{3,2},{4,7},{5,4},{6,5},{7,6},{8,11},{9,8},{10,9... | collective-permute-start | bytes 73736 | tf_op jit(solution)/shard_map/ppermute | solution.py:460
  85.0 0.5 collective-permute-start.4
  85.5 0.6 collective-permute-start.3
  86.1 0.0 collective-permute-done.5.c_ref
  86.1 3.0 %collective-permute-done.4.b_ref = f32[8,768]{1,0:T(8,128)S(1)} collective-permute-done((f32[8,768]{1,0:T(8,128)S(1)}, f32[8,768]{1,0:T(8,128)S(1)}, u32[]{:S(2)}, u32[]{:S(2)}) %collective-permute-start.4) | collective-permute-done | bytes 24608 | tf_op jit(solution)/shard_map/ppermute | solution.py:460
  89.2 0.3 collective-permute-done.3.a_ref
  89.5 0.0 copy-done.13
  89.5 2.1 %scale.1 = bf16[768,2048]{1,0:T(8,128)(2,1)} custom-call(f32[768,2048]{1,0:T(8,128)S(1)} %get-tuple-element.15.gated_ref, f32[1,2048]{1,0:T(1,128)S(1)} %bitcast.4, f32[8,768]{1,0:T(8,128)S(1)} %get-tuple-element.16.own_ref, f32[8,768]{1,0:T(8,128)S(1)} %collective-permute-done.3.a_ref, f32[8,768]{1,0:T(8,128)S(1)} %collective-permute-done.4.b_ref, ...), custom_call_target="tpu_custom_call" | custom-call | flops 5000000 | bytes 6500000 | tf_op jit(solution)/shard_map/scale/pallas_call | solution.py:463
  (14 shorter events, 0.1 us)
Async XLA Ops:
  0.6 1.9 %copy-start.4 = (bf16[768,2048]{1,0:T(8,128)(2,1)S(1)}, bf16[768,2048]{1,0:T(8,128)(2,1)}, u32[]{:S(2)}) copy-start(bf16[768,2048]{1,0:T(8,128)(2,1)} %x_ref.1) | copy-start | bytes 9437188
  2.5 0.9 %copy-start.9 = (bf16[768,128]{1,0:T(8,128)(2,1)S(1)}, bf16[768,128]{1,0:T(8,128)(2,1)}, u32[]{:S(2)}) copy-start(bf16[768,128]{1,0:T(8,128)(2,1)} %b_ref.1) | copy-start | bytes 589828
  3.5 0.8 copy-start.11
  4.3 0.7 copy-start.14
  4.9 0.7 copy-start.16
  5.6 18.5 %copy-start.8 = (bf16[768,128]{1,0:T(8,128)(2,1)S(1)}, bf16[768,128]{1,0:T(8,128)(2,1)}, u32[]{:S(2)}) copy-start(bf16[768,128]{1,0:T(8,128)(2,1)} %c_ref.3) | copy-start | bytes 589828
  5.6 18.5 %copy-start.10 = (bf16[768,128]{1,0:T(8,128)(2,1)S(1)}, bf16[768,128]{1,0:T(8,128)(2,1)}, u32[]{:S(2)}) copy-start(bf16[768,128]{1,0:T(8,128)(2,1)} %b_ref.1) | copy-start | bytes 589828
  5.6 18.5 %copy-start.12 = (f32[768,16]{0,1:T(8,128)S(1)}, f32[768,16]{0,1:T(8,128)}, u32[]{:S(2)}) copy-start(f32[768,16]{0,1:T(8,128)} %param.11) | copy-start | bytes 147460
  5.6 18.6 %copy-start.15 = (s32[16]{0:T(128)S(1)}, s32[16]{0:T(128)}, u32[]{:S(2)}) copy-start(s32[16]{0:T(128)} %doc_ref.1) | copy-start | bytes 196
  5.6 18.6 %copy-start.17 = (f32[16]{0:T(128)S(1)}, f32[16]{0:T(128)}, u32[]{:S(2)}) copy-start(f32[16]{0:T(128)} %rate_ref.1) | copy-start | bytes 196
  5.6 18.6 %copy-start.19 = (f32[16]{0:T(128)S(1)}, f32[16]{0:T(128)}, u32[]{:S(2)}) copy-start(f32[16]{0:T(128)} %skip_ref.1) | copy-start | bytes 196
  9.8 1.3 %copy-start.6 = (f32[2,16,128,128]{3,2,1,0:T(8,128)}, f32[2,16,128,128]{3,2,1,0:T(8,128)S(1)}, u32[]{:S(2)}) copy-start(f32[2,16,128,128]{3,2,1,0:T(8,128)S(1)} %get-tuple-element.12.before_ref) | copy-start | bytes 6291460
  11.1 5.6 %collective-permute-start = (f32[16,136,128]{2,1,0:T(8,128)S(1)}, f32[16,136,128]{2,1,0:T(8,128)S(1)}, u32[]{:S(2)}, u32[]{:S(2)}) collective-permute-start(f32[16,136,128]{2,1,0:T(8,128)S(1)} %get-tuple-element.10.own_ref), channel_id=1, source_target_pairs={{0,4},{4,0},{8,12},{12,8},{16,20},{20,16},{24,28},{28,24},{32,36},... | collective-permute-start | bytes 3342344 | tf_op jit(solution)/shard_map/ppermute | solution.py:383
  17.6 25.1 %all-to-all-start = ((f32[8,136,128]{2,1,0:T(8,128)}), f32[8,136,128]{2,1,0:T(8,128)S(1)}, u32[]{:S(2)}, u32[]{:S(2)}) async-start(f32[8,136,128]{2,1,0:T(8,128)} %join_cores.1.after_ref), calls=%async_computation | async-start | bytes 1114112 | tf_op jit(solution)/shard_map/all_to_all | solution.py:393
  24.1 1.9 %copy-start.5 = (bf16[768,2048]{1,0:T(8,128)(2,1)S(1)}, bf16[768,2048]{1,0:T(8,128)(2,1)}, u32[]{:S(2)}) copy-start(bf16[768,2048]{1,0:T(8,128)(2,1)} %x_ref.1) | copy-start | bytes 9437188
  26.0 1.9 %copy-start.18 = (bf16[768,2048]{1,0:T(8,128)(2,1)S(1)}, bf16[768,2048]{1,0:T(8,128)(2,1)}, u32[]{:S(2)}) copy-start(bf16[768,2048]{1,0:T(8,128)(2,1)} %gate_ref.1) | copy-start | bytes 9437188
  37.1 2.6 %copy-start = (f32[768,2048]{1,0:T(8,128)}, f32[768,2048]{1,0:T(8,128)S(1)}, u32[]{:S(2)}) copy-start(f32[768,2048]{1,0:T(8,128)S(1)} %get-tuple-element.11.after_ref.u_ref) | copy-start | bytes 18874372
  39.7 2.6 %copy-start.3 = (f32[768,2048]{1,0:T(8,128)}, f32[768,2048]{1,0:T(8,128)S(1)}, u32[]{:S(2)}) copy-start(f32[768,2048]{1,0:T(8,128)S(1)} %get-tuple-element.14.v_ref) | copy-start | bytes 18874372
  42.8 2.8 %copy-start.1 = (f32[768,2048]{1,0:T(8,128)S(1)}, f32[768,2048]{1,0:T(8,128)}, u32[]{:S(2)}) copy-start(f32[768,2048]{1,0:T(8,128)} %copy-done) | copy-start | bytes 18874372
  45.5 30.7 %copy-start.2 = (f32[768,2048]{1,0:T(8,128)S(1)}, f32[768,2048]{1,0:T(8,128)}, u32[]{:S(2)}) copy-start(f32[768,2048]{1,0:T(8,128)} %copy-done) | copy-start | bytes 18874372
  45.5 30.7 %copy-start.7 = (f32[2,16,128,128]{3,2,1,0:T(8,128)S(1)}, f32[2,16,128,128]{3,2,1,0:T(8,128)}, u32[]{:S(2)}) copy-start(f32[2,16,128,128]{3,2,1,0:T(8,128)} %copy-done.6) | copy-start | bytes 6291460
  45.6 4.7 %collective-permute-start.1 = (f32[128,128]{1,0:T(8,128)S(1)}, f32[128,128]{1,0:T(8,128)S(1)}, u32[]{:S(2)}, u32[]{:S(2)}) collective-permute-start(f32[128,128]{1,0:T(8,128)S(1)} %row_total.1), channel_id=1, source_target_pairs={{0,64},{4,68},{8,72},{12,76},{16,80},{20,84},{24,88},{28,92},{32,9... | collective-permute-start | bytes 196616 | tf_op jit(solution)/shard_map/ppermute | solution.py:425
  70.7 5.5 %collective-permute-start.2 = (f32[8,128,128]{2,1,0:T(8,128)S(1)}, f32[8,128,128]{2,1,0:T(8,128)S(1)}, u32[]{:S(2)}, u32[]{:S(2)}) collective-permute-start(f32[8,128,128]{2,1,0:T(8,128)S(1)} %all_to_all.10.own_ref), channel_id=1, source_target_pairs={{0,4},{4,0},{8,12},{12,8},{16,20},{20,16},{24,28},{28,24},{32,36},... | collective-permute-start | bytes 1572872 | tf_op jit(solution)/shard_map/ppermute | solution.py:437
  76.3 13.2 %copy-start.13 = (f32[2048]{0:T(1024)S(1)}, f32[2048]{0:T(1024)}, u32[]{:S(2)}) copy-start(f32[2048]{0:T(1024)} %param.16) | copy-start | bytes 24580
  82.5 3.7 %collective-permute-start.5 = (f32[8,768]{1,0:T(8,128)S(1)}, f32[8,768]{1,0:T(8,128)S(1)}, u32[]{:S(2)}, u32[]{:S(2)}) collective-permute-start(f32[8,768]{1,0:T(8,128)S(1)} %get-tuple-element.16.own_ref), channel_id=1, source_target_pairs={{0,3},{1,0},{2,1},{3,2},{4,7},{5,4},{6,5},{7,6},{8,11},{9,8},{10,9... | collective-permute-start | bytes 73736 | tf_op jit(solution)/shard_map/ppermute | solution.py:460
  85.0 4.2 %collective-permute-start.4 = (f32[8,768]{1,0:T(8,128)S(1)}, f32[8,768]{1,0:T(8,128)S(1)}, u32[]{:S(2)}, u32[]{:S(2)}) collective-permute-start(f32[8,768]{1,0:T(8,128)S(1)} %get-tuple-element.16.own_ref), channel_id=1, source_target_pairs={{0,2},{1,3},{2,0},{3,1},{4,6},{5,7},{6,4},{7,5},{8,10},{9,11},{10,... | collective-permute-start | bytes 73736 | tf_op jit(solution)/shard_map/ppermute | solution.py:460
  85.5 3.9 %collective-permute-start.3 = (f32[8,768]{1,0:T(8,128)S(1)}, f32[8,768]{1,0:T(8,128)S(1)}, u32[]{:S(2)}, u32[]{:S(2)}) collective-permute-start(f32[8,768]{1,0:T(8,128)S(1)} %get-tuple-element.16.own_ref), channel_id=1, source_target_pairs={{0,1},{1,2},{2,3},{3,0},{4,5},{5,6},{6,7},{7,4},{8,9},{9,10},{10,1... | collective-permute-start | bytes 73736 | tf_op jit(solution)/shard_map/ppermute | solution.py:460
where the time goes:
time: 92.2 us; the launch traced here: 91.7 us
  Pallas kernels  22.6 us (25%)
  blocking collectives  20.5 us (22%)
  starting transfers between devices  18.9 us (20%)
  local copies, waits for them, and re-layouts  18.1 us (20%)
  waiting for transfers between devices  10.8 us (12%)
  between operations  0.94 us (1%)
    all_to_all x1, blocking collectives, local(): lax.all_to_all(entering, 'seq', split_axis=0, concat_axis=0, axis_index_g...  20.5 us
    unnamed x40, local copies, waits for them, and re-layouts  18.1 us
    pallas_call x1, Pallas kernels, local(): pl.pallas_call(functools.partial(inside_kernel, heads, groups), in_specs=...  9.12 us
    all_to_all x1, starting transfers between devices, local(): lax.all_to_all(joined, 'seq', split_axis=0, concat_axis=0, axis_index_gro...  6.45 us
    pallas_call x1, Pallas kernels, local(): pl.pallas_call(functools.partial(outputs_kernel, heads, groups), in_specs...  6.15 us
    pallas_call x1, Pallas kernels, local(): pl.pallas_call(functools.partial(states_kernel, heads, groups), in_specs=...  4.18 us
    ppermute x1, starting transfers between devices, local(): swapped = lax.ppermute(own, 'seq', CORE_SWAP)  4 us
    ppermute x3, starting transfers between devices, local(): lax.ppermute(squares, 'tp', [(i, (i + k) % tp_size) for i in range(tp_siz...  3.69 us
  transfers between devices with their start and end apart: 7, of which 6 were waited for; matrix products, arithmetic and copies ran while one was open for 0% of the time, Pallas kernels for 10%

commit v1 on v0

v1 whole, which is shorter than its diff:
```python
import functools
import jax
import jax.numpy as jnp
from jax import lax
from jax.experimental import pallas as pl
from jax.experimental.pallas import tpu as pltpu
from jax.sharding import PartitionSpec as P

P_SIZE = 128
N = 128
Q = 256
F32 = jnp.float32
BF16 = jnp.bfloat16
Y_SIZE = 4
Z_SIZE = 8
NT = (((1,), (1,)), ((), ()))


def seq_index(y, z, core):
    return ((y % Y_SIZE) * Z_SIZE + (z % Z_SIZE)) * 2 + core


def seq_pairs(move):
    pairs = []
    for y in range(Y_SIZE):
        for z in range(Z_SIZE):
            for core in range(2):
                pairs.append((seq_index(y, z, core), seq_index(*move(y, z, core))))
    return pairs


CORE_SWAP = seq_pairs(lambda y, z, core: (y, z, 1 - core))
NEXT_ROW = seq_pairs(lambda y, z, core: (y + 1, z, core))
RINGS = [
    [seq_index(y, z, core) for z in range(Z_SIZE)] for y in range(Y_SIZE) for core in range(2)
]


def group_bounds(doc_ref, start):
    last = start + (Q - 1)
    doc_first = jnp.int32(0)
    next_end = jnp.int32(2147483647)
    end = jnp.int32(0)
    for k in range(doc_ref.shape[0]):
        end = end + doc_ref[k]
        doc_first = jnp.where(end <= last, end, doc_first)
        next_end = jnp.minimum(next_end, jnp.where(end >= start, end, 2147483647))
    return doc_first, next_end


def split3(values):
    high = values.astype(BF16)
    rest = values - high.astype(F32)
    mid = rest.astype(BF16)
    low = (rest - mid.astype(F32)).astype(BF16)
    return high, mid, low


def core_index():
    return lax.rem(lax.axis_index("seq"), 2)


def head_of(slot, heads):
    return lax.rem(slot + core_index() * (heads // 2), heads)


def head_span(slot, heads, count=1):
    return pl.ds(pl.multiple_of(head_of(slot, heads) * P_SIZE, P_SIZE), count * P_SIZE)


def slot_rows(rows):
    half = rows.shape[0] // 2
    turned = jnp.concatenate([rows[half:], rows[:half]], axis=0)
    return jnp.where(core_index() == 0, rows, turned)


def column_logs(step, rate_ref):
    head_rows = lax.broadcasted_iota(jnp.int32, step.shape, 0)
    terms = jnp.zeros_like(step)
    for head in range(step.shape[0]):
        terms = jnp.where(head_rows == head, -rate_ref[head_of(head, step.shape[0])] * step, terms)
    rows = lax.broadcasted_iota(jnp.int32, (Q, Q), 0)
    cols = lax.broadcasted_iota(jnp.int32, (Q, Q), 1)
    lower = jnp.where(cols <= rows, 1.0, 0.0).astype(BF16)
    return sum(
        lax.dot_general(lower, part, NT, preferred_element_type=F32) for part in split3(terms)
    )


def head_columns(values, head):
    return jnp.broadcast_to(values[:, head : head + 1], (values.shape[0], P_SIZE))


def scaled_pair(x, scale, slot, heads):
    parts = []
    for part in range(2):
        columns = x[:, part * P_SIZE : (part + 1) * P_SIZE].astype(F32)
        parts.append((columns * head_columns(scale, slot + part)).astype(BF16))
    return jnp.concatenate(parts, axis=1)


def half_states(groups, first_slot, x_of, scale_of, tail_of, stats_ref, state_ref):
    half = state_ref.shape[0]
    for group in range(groups):
        final = stats_ref[group : group + 1, :]
        passing = stats_ref[8 + group : 9 + group, :]
        tail_b = tail_of(group)
        scale = scale_of(group)
        for pair in range(half // 2):
            slot = first_slot + 2 * pair
            scaled = scaled_pair(x_of(group, pair), scale, slot, 2 * half)
            product = jnp.dot(tail_b, scaled, preferred_element_type=F32)
            for part in range(2):
                lane = slice(slot + part, slot + part + 1)
                index = 2 * pair + part
                state = product[:, part * P_SIZE : (part + 1) * P_SIZE] * final[:, lane]
                if group > 0:
                    state = state + state_ref[index, 0:N, :] * passing[:, lane]
                state_ref[index, 0:N, :] = state
    reach = stats_ref[16 + groups : 17 + groups, :]
    for index in range(half):
        lane = slice(first_slot + index, first_slot + index + 1)
        state_ref[index, N : N + 8, :] = jnp.broadcast_to(reach[:, lane], (8, P_SIZE))


def away_states_kernel(
    heads,
    groups,
    doc_hbm,
    rate_hbm,
    step_hbm,
    b_hbm,
    x_hbm,
    state_ref,
    stats_ref,
    scale_ref,
    tail_ref,
    doc_ref,
    rate_ref,
    step_ref,
    b_ref,
    x_ref,
    small_sems,
    wide_sems,
):
    half = heads // 2
    small = [
        pltpu.make_async_copy(src, dst, small_sems.at[i])
        for i, (src, dst) in enumerate(
            ((step_hbm, step_ref), (rate_hbm, rate_ref), (doc_hbm, doc_ref), (b_hbm, b_ref))
        )
    ]
    wide = [
        pltpu.make_async_copy(
            x_hbm.at[pl.ds(group * Q, Q), head_span(half, heads, half)],
            x_ref.at[group],
            wide_sems.at[group],
        )
        for group in range(groups)
    ]
    for copy in small + wide:
        copy.start()
    for copy in small:
        copy.wait()
    stats_ref[...] = jnp.zeros_like(stats_ref)
    base = lax.axis_index("seq") * (groups * Q)
    reach = jnp.ones((1, heads), F32)
    stats_ref[16:17, 0:heads] = reach
    for group in range(groups):
        start = base + group * Q
        doc_first, next_end = group_bounds(doc_ref, start)
        step = slot_rows(step_ref[:, group * Q : (group + 1) * Q])
        logs = column_logs(step, rate_ref)
        scale_ref[group] = jnp.exp(-logs) * step.T
        final = jnp.exp(logs[Q - 1 : Q, :])
        passing = jnp.where(start + (Q - 1) < next_end, final, 0.0)
        positions = lax.broadcasted_iota(jnp.int32, (N, Q), 1) + start
        b_rows = b_ref[group * Q : (group + 1) * Q, :].astype(F32).T
        tail_ref[group] = jnp.where(positions >= doc_first, b_rows, 0.0).astype(BF16)
        reach = reach * passing
        stats_ref[group : group + 1, 0:heads] = final
        stats_ref[8 + group : 9 + group, 0:heads] = passing
        stats_ref[17 + group : 18 + group, 0:heads] = reach

    def x_of(group, pair):
        if pair == 0:
            wide[group].wait()
        return x_ref[group, :, 2 * pair * P_SIZE : 2 * (pair + 1) * P_SIZE]

    half_states(
        groups,
        half,
        x_of,
        lambda group: scale_ref[group],
        lambda group: tail_ref[group],
        stats_ref,
        state_ref,
    )


def own_states_kernel(heads, groups, stats_ref, scale_ref, tail_ref, x_ref, state_ref):
    half_states(
        groups,
        0,
        lambda group, pair: x_ref[group * Q : (group + 1) * Q, head_span(2 * pair, heads, 2)],
        lambda group: scale_ref[group],
        lambda group: tail_ref[group],
        stats_ref,
        state_ref,
    )


def inside_kernel(
    heads,
    groups,
    doc_hbm,
    rate_hbm,
    skip_hbm,
    step_hbm,
    b_hbm,
    c_hbm,
    x_hbm,
    gate_hbm,
    after_ref,
    own_u_hbm,
    own_v_hbm,
    away_u_hbm,
    away_v_hbm,
    own_before_hbm,
    away_before_hbm,
    entry_c_hbm,
    token_ref,
    own_u_ref,
    own_v_ref,
    away_u_ref,
    away_v_ref,
    own_before_ref,
    away_before_ref,
    entry_c_ref,
    out_sems,
    doc_ref,
    rate_ref,
    skip_ref,
    step_ref,
    b_ref,
    c_ref,
    x_ref,
    gate_ref,
    small_sems,
    wide_sems,
):
    small = [
        pltpu.make_async_copy(src, dst, small_sems.at[i])
        for i, (src, dst) in enumerate(
            (
                (step_hbm, step_ref),
                (rate_hbm, rate_ref),
                (doc_hbm, doc_ref),
                (skip_hbm, skip_ref),
                (b_hbm, b_ref),
                (c_hbm, c_ref),
            )
        )
    ]
    wide = []
    for group in range(groups):
        for side, (src, dst) in enumerate(((x_hbm, x_ref), (gate_hbm, gate_ref))):
            wide.append(
                pltpu.make_async_copy(
                    src.at[pl.ds(group * Q, Q), :],
                    dst.at[pl.ds(group * Q, Q), :],
                    wide_sems.at[group, side],
                )
            )
    for copy in small + wide:
        copy.start()
    for copy in small:
        copy.wait()
    half = heads // 2
    copies, results = [], []
    base = lax.axis_index("seq") * (groups * Q)
    rows = lax.broadcasted_iota(jnp.int32, (Q, Q), 0)
    cols = lax.broadcasted_iota(jnp.int32, (Q, Q), 1)
    for group in range(groups):
        start = base + group * Q
        block = slice(group * Q, (group + 1) * Q)
        doc_first, next_end = group_bounds(doc_ref, start)
        step = slot_rows(step_ref[:, block])
        logs = column_logs(step, rate_ref)
        scale = jnp.exp(-logs) * step.T
        decay = jnp.exp(logs)
        final = decay[Q - 1 : Q, :]
        passing = jnp.where(start + (Q - 1) < next_end, final, 0.0)
        positions = lax.broadcasted_iota(jnp.int32, (Q, N), 0) + start
        entry_c = jnp.where(positions < next_end, c_ref[block, :].astype(F32), 0.0)
        entry_c_ref[block, :] = entry_c.astype(BF16)
        first = jnp.zeros((Q, Q), jnp.int32)
        end = jnp.int32(0)
        for k in range(doc_ref.shape[0]):
            end = end + doc_ref[k]
            first = jnp.where(end - start <= rows, end - start, first)
        scores = lax.dot_general(c_ref[block, :], b_ref[block, :], NT, preferred_element_type=F32)
        masked = jnp.where((cols <= rows) & (cols >= first), scores, 0.0).astype(BF16)
        lanes = lax.broadcasted_iota(jnp.int32, (N, Q), 1) + start
        tail_b = jnp.where(lanes >= doc_first, b_ref[block, :].astype(F32).T, 0.0).astype(BF16)
        wide[2 * group].wait()
        wide[2 * group + 1].wait()
        for pair in range(half):
            x = x_ref[block, head_span(2 * pair, heads, 2)]
            gates = gate_ref[block, head_span(2 * pair, heads, 2)]
            scaled = scaled_pair(x, scale, 2 * pair, heads)
            product = jnp.dot(masked, scaled, preferred_element_type=F32)
            if pair < half // 2:
                u_ref, v_ref, before_ref = own_u_ref, own_v_ref, own_before_ref
            else:
                u_ref, v_ref, before_ref = away_u_ref, away_v_ref, away_before_ref
            if group < groups - 1:
                states = jnp.dot(tail_b, scaled, preferred_element_type=F32)
            for part in range(2):
                slot = 2 * pair + part
                here = slice(part * P_SIZE, (part + 1) * P_SIZE)
                place = slot % half
                span = slice(place * P_SIZE, (place + 1) * P_SIZE)
                gate = 0.5 * gates[:, here].astype(F32)
                active = gate + gate * jnp.tanh(gate)
                carry = head_columns(decay, slot) * active
                direct = skip_ref[head_of(slot, heads)] * x[:, here].astype(F32)
                u_ref[block, span] = product[:, here] * carry + direct * active
                v_ref[block, span] = carry
                if group < groups - 1:
                    state = states[:, here] * final[:, slot : slot + 1]
                    if group > 0:
                        earlier = before_ref[group - 1, place]
                        state = state + earlier * passing[:, slot : slot + 1]
                    before_ref[group, place] = state
            if pair == half // 2 - 1:
                results.append((own_u_ref, own_u_hbm, 0))
                results.append((own_v_ref, own_v_hbm, 1))
                results.append((own_before_ref, own_before_hbm, 2))
            if pair == half - 1:
                results.append((away_u_ref, away_u_hbm, 3))
                results.append((away_v_ref, away_v_hbm, 4))
                results.append((away_before_ref, away_before_hbm, 5))
                results.append((entry_c_ref, entry_c_hbm, 6))
            for src, dst, index in results:
                if len(dst.shape) == 2:
                    where = pl.ds(group * Q, Q)
                elif group < groups - 1:
                    where = group
                else:
                    continue
                copy = pltpu.make_async_copy(
                    src.at[where], dst.at[where], out_sems.at[group, index]
                )
                copy.start()
                copies.append(copy)
            results = []
    for copy in copies:
        copy.wait()
    token_ref[...] = jnp.zeros_like(token_ref)


def join_cores_kernel(own_ref, other_ref, joined_ref, token_ref):
    core = core_index()
    for slot in range(joined_ref.shape[0]):
        own, other = own_ref[slot], other_ref[slot]
        earlier = jnp.where(core == 0, own, other)
        later = jnp.where(core == 0, other, own)
        later_pass = later[N : N + 1, :]
        joined_ref[slot, 0:N, :] = later_pass * earlier[0:N, :] + later[0:N, :]
        joined_ref[slot, N : N + 8, :] = later_pass * earlier[N : N + 8, :]
    token_ref[...] = jnp.zeros_like(token_ref)


def row_total_kernel(parts_ref, inside_ref, swap_ref, total_ref):
    total = parts_ref[0, 0:N, :]
    for chip in range(1, Z_SIZE):
        total = parts_ref[chip, N : N + 1, :] * total + parts_ref[chip, 0:N, :]
    total_ref[...] = total


def entering_kernel(parts_ref, carried_ref, entering_ref):
    row = lax.axis_index("seq") // (2 * Z_SIZE)
    state = jnp.where(row > 0, carried_ref[...], 0.0)
    for chip in range(Z_SIZE):
        entering_ref[chip] = state
        if chip < Z_SIZE - 1:
            state = parts_ref[chip, N : N + 1, :] * state + parts_ref[chip, 0:N, :]


def half_outputs_kernel(
    groups,
    first_slot,
    last,
    chip_ref,
    other_ref,
    before_ref,
    stats_ref,
    c_ref,
    u_ref,
    v_ref,
    sums_ref,
    gated_ref,
    squares_ref,
    first_ref,
):
    core = core_index()
    half = chip_ref.shape[0]
    for index in range(half):
        chip_state = chip_ref[index]
        joined = other_ref[index, N : N + 1, :] * chip_state + other_ref[index, 0:N, :]
        first_ref[index] = jnp.where(core == 0, chip_state, joined)
    for group in range(groups):
        block = slice(group * Q, (group + 1) * Q)
        reach = stats_ref[16 + group : 17 + group, :]
        squares = sums_ref[block, :] if last else jnp.zeros((Q, P_SIZE), F32)
        for pair in range(half // 2):
            both = []
            for index in (2 * pair, 2 * pair + 1):
                state = first_ref[index]
                if group > 0:
                    lane = slice(first_slot + index, first_slot + index + 1)
                    state = state * reach[:, lane] + before_ref[group - 1, index]
                both.append(state.astype(BF16))
            carried = jnp.dot(
                c_ref[block, :], jnp.concatenate(both, axis=1), preferred_element_type=F32
            )
            span = slice(2 * pair * P_SIZE, 2 * (pair + 1) * P_SIZE)
            gated = u_ref[block, span] + v_ref[block, span] * carried
            gated_ref[block, span] = gated
            square = gated * gated
            squares = squares + square[:, 0:P_SIZE] + square[:, P_SIZE:]
        if last:
            squares_ref[:, block] = jnp.broadcast_to(
                jnp.sum(squares.T, axis=0, keepdims=True), (8, Q)
            )
        else:
            squares_ref[block, :] = squares


def write_states_kernel(
    heads,
    groups,
    own_first_ref,
    away_first_ref,
    own_before_ref,
    away_before_ref,
    stats_ref,
    after_ref,
    states_hbm,
    token_ref,
    states_ref,
    sems,
):
    half = heads // 2
    copies = []
    for group in range(groups):
        reach = stats_ref[16 + group : 17 + group, :]
        for side, (first_ref, before_ref) in enumerate(
            ((own_first_ref, own_before_ref), (away_first_ref, away_before_ref))
        ):
            for index in range(half):
                state = first_ref[index]
                if group > 0:
                    slot = side * half + index
                    state = state * reach[:, slot : slot + 1] + before_ref[group - 1, index]
                states_ref[group, side, index] = state.T
            copy = pltpu.make_async_copy(
                states_ref.at[group, side],
                states_hbm.at[group, pl.ds(head_of(side * half, heads), half)],
                sems.at[group, side],
            )
            copy.start()
            copies.append(copy)
    for copy in copies:
        copy.wait()
    token_ref[...] = jnp.zeros_like(token_ref)


SCALE_ROWS = 128


def scale_kernel(
    inner, heads, own_ref, away_ref, gain_ref, sum_ref, a_ref, b_ref, c_ref, after_ref, out_hbm, out_ref, sems
):
    mean = (sum_ref[...] + a_ref[...] + b_ref[...] + c_ref[...]) * (1.0 / inner)
    scale = lax.rsqrt(mean + 1e-05)
    half = heads // 2
    copies = []
    for chunk in range(own_ref.shape[0] // SCALE_ROWS):
        block = slice(chunk * SCALE_ROWS, (chunk + 1) * SCALE_ROWS)
        column = jnp.broadcast_to(scale[0:1, block], (P_SIZE, SCALE_ROWS)).T
        for side, gated_ref in enumerate((own_ref, away_ref)):
            for index in range(half):
                span = slice(index * P_SIZE, (index + 1) * P_SIZE)
                gain = gain_ref[:, head_span(side * half + index, heads)]
                out_ref[side, block, span] = (gated_ref[block, span] * column * gain).astype(BF16)
            copy = pltpu.make_async_copy(
                out_ref.at[side, pl.ds(chunk * SCALE_ROWS, SCALE_ROWS), :],
                out_hbm.at[
                    pl.ds(chunk * SCALE_ROWS, SCALE_ROWS), head_span(side * half, heads, half)
                ],
                sems.at[side, chunk],
            )
            copy.start()
            copies.append(copy)
    for copy in copies:
        copy.wait()


def cost(flops, bytes_accessed):
    return pl.CostEstimate(flops=flops, bytes_accessed=bytes_accessed, transcendentals=0)


def params(mebibytes):
    return pltpu.CompilerParams(vmem_limit_bytes=mebibytes * 1024 * 1024)


def local(
    head_input,
    gate_input,
    step_size,
    input_proj,
    output_proj,
    decay_rate,
    skip_gain,
    norm_gain,
    doc_lengths,
):
    row_count, width = head_input.shape
    heads = step_size.shape[1]
    half = heads // 2
    groups = row_count // Q
    sds = jax.ShapeDtypeStruct
    step_rows = step_size.T
    gain = norm_gain.reshape(1, width)
    smem = pl.BlockSpec(memory_space=pltpu.SMEM)
    vmem = pl.BlockSpec(memory_space=pltpu.VMEM)
    hbm = pl.BlockSpec(memory_space=pltpu.HBM)
    anywhere = pl.BlockSpec(memory_space=pl.ANY)
    dma = pltpu.SemaphoreType.DMA

    token = sds((8, P_SIZE), F32)
    half_state = sds((half, N + 8, P_SIZE), F32)
    half_before = sds((groups - 1, half, N, P_SIZE), F32)
    half_wide = sds((row_count, width // 2), F32)
    half_first = sds((half, N, P_SIZE), F32)

    def in_hbm(*arrays):
        return [pltpu.with_memory_space_constraint(array, pltpu.HBM) for array in arrays]

    away_state, stats, scale, tail = pl.pallas_call(
        functools.partial(away_states_kernel, heads, groups),
        in_specs=[hbm] * 5,
        out_specs=[vmem] * 4,
        out_shape=[
            half_state,
            sds((24, P_SIZE), F32),
            sds((groups, Q, heads), F32),
            sds((groups, N, Q), BF16),
        ],
        scratch_shapes=[
            pltpu.SMEM(doc_lengths.shape, jnp.int32),
            pltpu.SMEM(decay_rate.shape, F32),
            pltpu.VMEM((heads, row_count), F32),
            pltpu.VMEM((row_count, N), BF16),
            pltpu.VMEM((groups, Q, width // 2), BF16),
            dma((4,)),
            dma((groups,)),
        ],
        compiler_params=params(16),
        cost_estimate=cost(200_000_000, 4_000_000),
        name="away_states",
    )(*in_hbm(doc_lengths, decay_rate, step_rows, input_proj, head_input))
    own_other = lax.ppermute(away_state, "seq", CORE_SWAP)

    own_state = pl.pallas_call(
        functools.partial(own_states_kernel, heads, groups),
        in_specs=[vmem] * 4,
        out_specs=vmem,
        out_shape=half_state,
        compiler_params=params(16),
        cost_estimate=cost(2_000_000_000, 4_000_000),
        name="own_states",
    )(stats, scale, tail, head_input)

    joined, joined_token = pl.pallas_call(
        join_cores_kernel,
        out_shape=[half_state, token],
        compiler_params=params(8),
        cost_estimate=cost(1_000_000, 1_700_000),
        name="join_cores",
    )(own_state, own_other)
    parts = lax.all_to_all(
        joined, "seq", split_axis=0, concat_axis=0, axis_index_groups=RINGS, tiled=True
    )
    away_other = lax.ppermute(own_state, "seq", CORE_SWAP)

    own_u, own_v, away_u, away_v, own_before, away_before, entry_c, inside_token = pl.pallas_call(
        functools.partial(inside_kernel, heads, groups),
        in_specs=[hbm] * 8 + [anywhere],
        out_specs=[hbm] * 7 + [vmem],
        out_shape=[pltpu.HBM(half_wide.shape, F32)] * 4
        + [pltpu.HBM(half_before.shape, F32)] * 2
        + [pltpu.HBM((row_count, N), BF16), token],
        scratch_shapes=[pltpu.VMEM(half_wide.shape, F32)] * 4
        + [pltpu.VMEM(half_before.shape, F32)] * 2
        + [pltpu.VMEM((row_count, N), BF16), dma((groups, 7))]
        + [
            pltpu.SMEM(doc_lengths.shape, jnp.int32),
            pltpu.SMEM(decay_rate.shape, F32),
            pltpu.SMEM(skip_gain.shape, F32),
            pltpu.VMEM((heads, row_count), F32),
            pltpu.VMEM((row_count, N), BF16),
            pltpu.VMEM((row_count, N), BF16),
            pltpu.VMEM((row_count, width), BF16),
            pltpu.VMEM((row_count, width), BF16),
            dma((6,)),
            dma((groups, 2)),
        ],
        compiler_params=params(36),
        cost_estimate=cost(8_000_000_000, 20_000_000),
        name="inside",
    )(
        *in_hbm(
            doc_lengths,
            decay_rate,
            skip_gain,
            step_rows,
            input_proj,
            output_proj,
            head_input,
            gate_input,
        ),
        joined_token,
    )
    total = pl.pallas_call(
        row_total_kernel,
        in_specs=[vmem, anywhere, anywhere],
        out_shape=sds((N, P_SIZE), F32),
        compiler_params=params(8),
        cost_estimate=cost(300_000, 600_000),
        name="row_total",
    )(parts, inside_token, away_other)
    carried = lax.ppermute(total, "seq", NEXT_ROW)
    entering = pl.pallas_call(
        entering_kernel,
        out_shape=sds((Z_SIZE, N, P_SIZE), F32),
        compiler_params=params(8),
        cost_estimate=cost(20_000_000_000, 1_100_000),
        name="entering",
    )(parts, carried)

    own_chip = lax.all_to_all(
        entering, "seq", split_axis=0, concat_axis=0, axis_index_groups=RINGS, tiled=True
    )

    away_chip = lax.ppermute(own_chip, "seq", CORE_SWAP)

    def half_outputs(first_slot, last, *operands):
        sums = sds((8, row_count), F32) if last else sds((row_count, P_SIZE), F32)
        return pl.pallas_call(
            functools.partial(half_outputs_kernel, groups, first_slot, last),
            in_specs=[vmem] * 7 + [vmem if last else anywhere],
            out_specs=[vmem] * 3,
            out_shape=[half_wide, sums, half_first],
            compiler_params=params(20),
            cost_estimate=cost(2_000_000_000, 9_000_000),
            name="away_outputs" if last else "own_outputs",
        )(*operands)

    own_gated, own_squares, own_first = half_outputs(
        0, False, own_chip, own_other, own_before, stats, entry_c, own_u, own_v, stats
    )
    away_gated, squares, away_first = half_outputs(
        half,
        True,
        away_chip,
        away_other,
        away_before,
        stats,
        entry_c,
        away_u,
        away_v,
        own_squares,
    )

    tp_size = 4
    sums = [
        lax.ppermute(squares, "tp", [(i, (i + k) % tp_size) for i in range(tp_size)])
        for k in range(1, tp_size)
    ]
    group_states, states_token = pl.pallas_call(
        functools.partial(write_states_kernel, heads, groups),
        in_specs=[vmem] * 5 + [anywhere],
        out_specs=[hbm, vmem],
        out_shape=[sds((groups, heads, P_SIZE, N), F32), token],
        scratch_shapes=[
            pltpu.VMEM((groups, 2, half, P_SIZE, N), F32),
            dma((groups, 2)),
        ],
        compiler_params=params(16),
        cost_estimate=cost(4_000_000_000, 9_000_000),
        name="write_states",
    )(own_first, away_first, own_before, away_before, stats, squares)
    mixed_out = pl.pallas_call(
        functools.partial(scale_kernel, width * tp_size, heads),
        in_specs=[vmem] * 7 + [anywhere],
        out_specs=hbm,
        out_shape=sds((row_count, width), BF16),
        scratch_shapes=[
            pltpu.VMEM((2, row_count, width // 2), BF16),
            dma((2, row_count // SCALE_ROWS)),
        ],
        compiler_params=params(16),
        cost_estimate=cost(5_000_000, 6_500_000),
        name="scale",
    )(own_gated, away_gated, gain, squares, *sums, states_token)
    return (mixed_out, group_states)


def solution(mesh):
    return jax.shard_map(
        local,
        mesh=mesh,
        in_specs=(
            P("seq", "tp"),
            P("seq", "tp"),
            P("seq", "tp"),
            P("seq", None),
            P("seq", None),
            P("tp"),
            P("tp"),
            P("tp"),
            P(),
        ),
        out_specs=(P("seq", "tp"), P("seq", "tp", None, None)),
        check_vma=False,
    )
```

time: 92.2 us -> 74.8 us (0.81)
  local copies, waits for them, and re-layouts: 18.1 us -> 2.4 us
  blocking collectives: 20.5 us -> 17.6 us
  waiting for transfers between devices: 10.8 us -> 12.5 us
    unnamed x40 -> x22, local copies, waits for them, and re-layouts: 18.1 us -> 2.4 us
    all_to_all x1, waiting for transfers between devices: 0.43 us -> 7.06 us  [local(): lax.all_to_all(joined, 'seq', split_axis=0, concat_axis=0, axis_index_gro...]
    ppermute x2 -> x3, waiting for transfers between devices: 3.92 us -> 1.03 us  [the longest x1 0.76 us: local(): away_chip = lax.ppermute(own_chip, 'seq', CORE_SWAP)]
    all_to_all x1, blocking collectives: 20.5 us -> 17.6 us  [local(): lax.all_to_all(entering, 'seq', split_axis=0, concat_axis=0, axis_index_g...]
    pallas_call x5 -> x8, Pallas kernels: 13.4 us -> 11.4 us  [the longest x1 3.56 us: local(): pl.pallas_call(functools.partial(away_states_kernel, heads, groups), in_s...]
    ppermute x3, waiting for transfers between devices: 3.31 us -> 1.34 us  [local(): lax.ppermute(squares, 'tp', [(i, (i + k) % tp_size) for i in range(tp_siz...]
    pallas_call x1, Pallas kernels: 9.12 us -> 10.9 us  [local(): pl.pallas_call(functools.partial(inside_kernel, heads, groups), in_specs=...]
    ppermute x2 -> x3, starting transfers between devices: 7.25 us -> 7.21 us  [the longest x1 3.33 us: local(): own_other = lax.ppermute(away_state, 'seq', CORE_SWAP)]
  transfers between devices with their start and end apart: 7 -> 8, of which waited for: 6 -> 6; matrix products, arithmetic and copies ran while one was open for 0% -> 0% of each run, Pallas kernels for 10% -> 20%
where the time goes in v1:
time: 74.8 us; the launch traced here: 74.6 us
  Pallas kernels  22.4 us (30%)
  starting transfers between devices  18.7 us (25%)
  blocking collectives  17.6 us (24%)
  waiting for transfers between devices  12.5 us (17%)
  local copies, waits for them, and re-layouts  2.4 us (3%)
  between operations  0.94 us (1%)
    all_to_all x1, blocking collectives, local(): lax.all_to_all(entering, 'seq', split_axis=0, concat_axis=0, axis_index_g...  17.6 us
    pallas_call x1, Pallas kernels, local(): pl.pallas_call(functools.partial(inside_kernel, heads, groups), in_specs=...  10.9 us
    all_to_all x1, waiting for transfers between devices, local(): lax.all_to_all(joined, 'seq', split_axis=0, concat_axis=0, axis_index_gro...  7.06 us
    all_to_all x1, starting transfers between devices, local(): lax.all_to_all(joined, 'seq', split_axis=0, concat_axis=0, axis_index_gro...  6.45 us
    ppermute x3, starting transfers between devices, local(): lax.ppermute(squares, 'tp', [(i, (i + k) % tp_size) for i in range(tp_siz...  3.68 us
    pallas_call x1, Pallas kernels, local(): pl.pallas_call(functools.partial(away_states_kernel, heads, groups), in_s...  3.56 us
    ppermute x1, starting transfers between devices, local(): own_other = lax.ppermute(away_state, 'seq', CORE_SWAP)  3.33 us
    ppermute x1, starting transfers between devices, local(): away_chip = lax.ppermute(own_chip, 'seq', CORE_SWAP)  3.23 us
  transfers between devices with their start and end apart: 8, of which 6 were waited for; matrix products, arithmetic and copies ran while one was open for 0% of the time, Pallas kernels for 20%

profile of v1, /device:TPU:1, one launch (start us, length us, event | category | flops | bytes accessed | tf_op | source)
XLA Modules:
  0.0 74.6 jit_solution(5563445227959663762)
XLA Ops:
  0.6 0.0 copy-start.2
  0.6 3.6 %away_states.1 = (f32[8,136,128]{2,1,0:T(8,128)S(1)}, f32[24,128]{1,0:T(8,128)S(1)}, f32[3,256,16]{2,1,0:T(8,128)S(1)}, bf16[3,128,256]{2,1,0:T(8,128)(2,1)S(1)}) custom-call(s32[16]{0:T(128)} %doc_hbm.3, f32[16]{0:T(128)} %rate_hbm.3, f32[16,768]{1,0:T(8,128)} %bitcast.3, bf16[768,128]{1,0:T(8,128)(2,1)} %b_hbm.3, bf16[768,2048]{1,0:T(8,128)(2,1)} %x_hbm.3), custom_call_target="tpu_custom_call" | custom-call | flops 200000000 | bytes 4000000 | tf_op jit(solution)/shard_map/away_states/pallas_call | solution.py:552
  4.2 3.3 %collective-permute-start = (f32[8,136,128]{2,1,0:T(8,128)S(1)}, f32[8,136,128]{2,1,0:T(8,128)S(1)}, u32[]{:S(2)}, u32[]{:S(2)}) collective-permute-start(f32[8,136,128]{2,1,0:T(8,128)S(1)} %get-tuple-element.27), channel_id=1, source_target_pairs={{0,4},{4,0},{8,12},{12,8},{16,20},{20,16},{24,28},{28,24},{32,36},... | collective-permute-start | bytes 1671176 | tf_op jit(solution)/shard_map/ppermute | solution.py:575
  7.5 0.0 copy-done.2
  7.5 1.3 %own_states.1.own_ref = f32[8,136,128]{2,1,0:T(8,128)S(1)} custom-call(f32[24,128]{1,0:T(8,128)S(1)} %get-tuple-element.24.stats_ref.sums_ref, f32[3,256,16]{2,1,0:T(8,128)S(1)} %get-tuple-element.25.scale_ref, bf16[3,128,256]{2,1,0:T(8,128)(2,1)S(1)} %get-tuple-element.26.tail_ref, bf16[768,2048]{1,0:T(8,128)(2,1)S(1)} %copy-done.2), custom_call_target="tpu_custom_call" | custom-call | flops 2000000000 | bytes 4000000 | tf_op jit(solution)/shard_map/own_states/pallas_call | solution.py:577
  8.9 0.3 collective-permute-done.other_ref
  9.1 1.0 %join_cores.1 = (f32[8,136,128]{2,1,0:T(8,128)}, f32[8,128]{1,0:T(8,128)S(1)}) custom-call(f32[8,136,128]{2,1,0:T(8,128)S(1)} %own_states.1.own_ref, f32[8,136,128]{2,1,0:T(8,128)S(1)} %collective-permute-done.other_ref), custom_call_target="tpu_custom_call" | custom-call | flops 1000000 | bytes 1700000 | tf_op jit(solution)/shard_map/join_cores/pallas_call | solution.py:587
  10.1 0.0 copy-start.5
  10.1 0.8 %copy-done.5 = f32[8,136,128]{2,1,0:T(8,128)} copy-done((f32[8,136,128]{2,1,0:T(8,128)}, f32[8,136,128]{2,1,0:T(8,128)S(1)}, u32[]{:S(2)}) %copy-start.5) | copy-done | bytes 557080
  10.9 6.4 %all-to-all-start = ((f32[8,136,128]{2,1,0:T(8,128)}), f32[8,136,128]{2,1,0:T(8,128)S(1)}, u32[]{:S(2)}, u32[]{:S(2)}) async-start(f32[8,136,128]{2,1,0:T(8,128)} %get-tuple-element.28), calls=%async_computation | async-start | bytes 1114112 | tf_op jit(solution)/shard_map/all_to_all | solution.py:594
  17.3 0.7 collective-permute-start.1
  18.0 10.9 %inside.1 = (f32[768,1024]{1,0:T(8,128)}, f32[768,1024]{1,0:T(8,128)}, f32[768,1024]{1,0:T(8,128)}, f32[768,1024]{1,0:T(8,128)}, f32[2,8,128,128]{3,2,1,0:T(8,12...) custom-call(s32[16]{0:T(128)} %doc_hbm.3, f32[16]{0:T(128)} %rate_hbm.3, ...), custom_call_target="tpu_custom_call" | custom-call | flops 8000000000 | bytes 20000000 | tf_op jit(solution)/shard_map/inside/pallas_call | solution.py:599
  28.9 0.0 collective-permute-done.1.swap_ref.other_ref
  28.9 7.1 %all-to-all-done.parts_ref = f32[8,136,128]{2,1,0:T(8,128)S(1)} async-done(((f32[8,136,128]{2,1,0:T(8,128)}), f32[8,136,128]{2,1,0:T(8,128)S(1)}, u32[]{:S(2)}, u32[]{:S(2)}) %all-to-all-start) | async-done | bytes 557088 | tf_op jit(solution)/shard_map/all_to_all | solution.py:594
  36.0 0.0 copy-start
  36.0 0.0 copy-start.1
  36.1 0.0 copy-start.6
  36.1 0.0 copy-start.7
  36.1 0.0 copy-start.9
  36.1 1.4 %collective-permute-start.2 = (f32[128,128]{1,0:T(8,128)S(1)}, f32[128,128]{1,0:T(8,128)S(1)}, u32[]{:S(2)}, u32[]{:S(2)}) collective-permute-start(f32[128,128]{1,0:T(8,128)S(1)} %row_total.1), channel_id=1, source_target_pairs={{0,64},{4,68},{8,72},{12,76},{16,80},{20,84},{24,88},{28,92},{32,9... | collective-permute-start | bytes 196616 | tf_op jit(solution)/shard_map/ppermute | solution.py:645
  37.5 3.1 %collective-permute-done.2.carried_ref = f32[128,128]{1,0:T(8,128)S(1)} collective-permute-done((f32[128,128]{1,0:T(8,128)S(1)}, f32[128,128]{1,0:T(8,128)S(1)}, u32[]{:S(2)}, u32[]{:S(2)}) %collective-permute-start.2) | collective-permute-done | bytes 65568 | tf_op jit(solution)/shard_map/ppermute | solution.py:645
  40.6 17.6 %all_to_all.10.chip_ref = f32[8,128,128]{2,1,0:T(8,128)S(1)} all-to-all(f32[8,128,128]{2,1,0:T(8,128)S(1)} %entering.1), channel_id=1, replica_groups={{0,8,16,24,32,40,48,56},{4,12,20,28,36,44,52,60},{64,72,80,88,96,104,11..., dimensions={0} | all-to-all | bytes 1048576 | tf_op jit(solution)/shard_map/all_to_all | solution.py:654
  58.2 3.2 %collective-permute-start.3 = (f32[8,128,128]{2,1,0:T(8,128)S(1)}, f32[8,128,128]{2,1,0:T(8,128)S(1)}, u32[]{:S(2)}, u32[]{:S(2)}) collective-permute-start(f32[8,128,128]{2,1,0:T(8,128)S(1)} %all_to_all.10.chip_ref), channel_id=1, source_target_pairs={{0,4},{4,0},{8,12},{12,8},{16,20},{20,16},{24,28},{28,24},{32,36},... | collective-permute-start | bytes 1572872 | tf_op jit(solution)/shard_map/ppermute | solution.py:658
  61.5 0.0 copy-done
  61.5 0.0 copy-done.1
  61.5 0.0 copy-done.6
  61.5 0.0 copy-done.7
  61.5 0.0 copy-done.9
  61.5 0.0 copy-start.3
  61.5 0.0 copy-start.4
  61.5 0.0 copy-start.8
  61.5 0.7 own_outputs.1
  62.2 0.8 %collective-permute-done.3.chip_ref = f32[8,128,128]{2,1,0:T(8,128)S(1)} collective-permute-done((f32[8,128,128]{2,1,0:T(8,128)S(1)}, f32[8,128,128]{2,1,0:T(8,128)S(1)}, u32[]{:S(2)}, u32[]{:S(2)}) %collective-permute-start.3) | collective-permute-done | bytes 524320 | tf_op jit(solution)/shard_map/ppermute | solution.py:658
  63.0 0.4 copy-done.3
  63.4 1.0 %copy-done.4 = f32[768,1024]{1,0:T(8,128)S(1)} copy-done((f32[768,1024]{1,0:T(8,128)S(1)}, f32[768,1024]{1,0:T(8,128)}, u32[]{:S(2)}) %copy-start.4) | copy-done | bytes 3145752
  64.3 0.2 copy-done.8
  64.6 0.8 %away_outputs.1 = (f32[768,1024]{1,0:T(8,128)S(1)}, f32[8,768]{1,0:T(8,128)S(1)}, f32[8,128,128]{2,1,0:T(8,128)S(1)}) custom-call(f32[8,128,128]{2,1,0:T(8,128)S(1)} %collective-permute-done.3.chip_ref, f32[8,136,128]{2,1,0:T(8,128)S(1)} %collective-permute-done.1.swap_ref.other_ref, f32[2,8,128,128]{3,2,1,0:T(8,128)S(1)} %copy-done.8, ...), custom_call_target="tpu_custom_call" | custom-call | flops 2000000000 | bytes 9000000 | tf_op jit(solution)/shard_map/away_outputs/pallas_call | solution.py:662
  65.4 2.6 %collective-permute-start.6 = (f32[8,768]{1,0:T(8,128)S(1)}, f32[8,768]{1,0:T(8,128)S(1)}, u32[]{:S(2)}, u32[]{:S(2)}) collective-permute-start(f32[8,768]{1,0:T(8,128)S(1)} %get-tuple-element.41.after_ref.sum_ref), channel_id=1, source_target_pairs={{0,3},{1,0},{2,1},{3,2},{4,7},{5,4},{6,5},{7,6},{8,11},{9,8},{10,9... | collective-permute-start | bytes 73736 | tf_op jit(solution)/shard_map/ppermute | solution.py:690
  67.9 0.5 collective-permute-start.5
  68.5 0.6 collective-permute-start.4
  69.1 0.0 copy-start.10
  69.1 2.0 %write_states.1 = (f32[3,16,128,128]{3,2,1,0:T(8,128)}, f32[8,128]{1,0:T(8,128)S(1)}) custom-call(f32[8,128,128]{2,1,0:T(8,128)S(1)} %get-tuple-element.42.own_first_ref, f32[8,128,128]{2,1,0:T(8,128)S(1)} %get-tuple-element.43.away_first_ref, f32[2,8,128,128]{3,2,1,0:T(8,128)S(1)} %copy-done.7, f32[2,8,128,128]{3,2,1,0:T(8,128)S(1)} %copy-done.8, ...), custom_call_target="tpu_custom_call" | custom-call | flops 4000000000 | bytes 9000000 | tf_op jit(solution)/shard_map/write_states/pallas_call | solution.py:693
  71.0 0.0 collective-permute-done.6.c_ref
  71.1 1.1 %collective-permute-done.5.b_ref = f32[8,768]{1,0:T(8,128)S(1)} collective-permute-done((f32[8,768]{1,0:T(8,128)S(1)}, f32[8,768]{1,0:T(8,128)S(1)}, u32[]{:S(2)}, u32[]{:S(2)}) %collective-permute-start.5) | collective-permute-done | bytes 24608 | tf_op jit(solution)/shard_map/ppermute | solution.py:690
  72.1 0.3 collective-permute-done.4.a_ref
  72.4 0.0 copy-done.10
  72.4 2.0 %scale.1 = bf16[768,2048]{1,0:T(8,128)(2,1)} custom-call(f32[768,1024]{1,0:T(8,128)S(1)} %get-tuple-element.35.own_ref, f32[768,1024]{1,0:T(8,128)S(1)} %get-tuple-element.40.away_ref, f32[1,2048]{1,0:T(1,128)S(1)} %bitcast.2, f32[8,768]{1,0:T(8,128)S(1)} %get-tuple-element.41.after_ref.sum_ref, f32[8,768]{1,0:T(8,128)S(1)} %collective-permute-done.4.a_ref, ...), custom_call_target="tpu_custom_call" | custom-call | flops 5000000 | bytes 6500000 | tf_op jit(solution)/shard_map/scale/pallas_call | solution.py:706
  (2 shorter events, 0.1 us)
Async XLA Ops:
  0.6 6.9 %copy-start.2 = (bf16[768,2048]{1,0:T(8,128)(2,1)S(1)}, bf16[768,2048]{1,0:T(8,128)(2,1)}, u32[]{:S(2)}) copy-start(bf16[768,2048]{1,0:T(8,128)(2,1)} %x_hbm.3) | copy-start | bytes 9437188
  4.2 4.9 %collective-permute-start = (f32[8,136,128]{2,1,0:T(8,128)S(1)}, f32[8,136,128]{2,1,0:T(8,128)S(1)}, u32[]{:S(2)}, u32[]{:S(2)}) collective-permute-start(f32[8,136,128]{2,1,0:T(8,128)S(1)} %get-tuple-element.27), channel_id=1, source_target_pairs={{0,4},{4,0},{8,12},{12,8},{16,20},{20,16},{24,28},{28,24},{32,36},... | collective-permute-start | bytes 1671176 | tf_op jit(solution)/shard_map/ppermute | solution.py:575
  10.1 0.8 %copy-start.5 = (f32[8,136,128]{2,1,0:T(8,128)}, f32[8,136,128]{2,1,0:T(8,128)S(1)}, u32[]{:S(2)}) copy-start(f32[8,136,128]{2,1,0:T(8,128)S(1)} %collective-permute-done.other_ref) | copy-start | bytes 1671172
  10.9 25.1 %all-to-all-start = ((f32[8,136,128]{2,1,0:T(8,128)}), f32[8,136,128]{2,1,0:T(8,128)S(1)}, u32[]{:S(2)}, u32[]{:S(2)}) async-start(f32[8,136,128]{2,1,0:T(8,128)} %get-tuple-element.28), calls=%async_computation | async-start | bytes 1114112 | tf_op jit(solution)/shard_map/all_to_all | solution.py:594
  17.3 11.6 %collective-permute-start.1 = (f32[8,136,128]{2,1,0:T(8,128)S(1)}, f32[8,136,128]{2,1,0:T(8,128)S(1)}, u32[]{:S(2)}, u32[]{:S(2)}) collective-permute-start(f32[8,136,128]{2,1,0:T(8,128)S(1)} %own_states.1.own_ref), channel_id=1, source_target_pairs={{0,4},{4,0},{8,12},{12,8},{16,20},{20,16},{24,28},{28,24},{32,36},... | collective-permute-start | bytes 1671176 | tf_op jit(solution)/shard_map/ppermute | solution.py:597
  36.0 25.4 %copy-start = (f32[768,1024]{1,0:T(8,128)S(1)}, f32[768,1024]{1,0:T(8,128)}, u32[]{:S(2)}) copy-start(f32[768,1024]{1,0:T(8,128)} %get-tuple-element.33.u_ref) | copy-start | bytes 9437188
  36.0 25.4 %copy-start.1 = (f32[768,1024]{1,0:T(8,128)S(1)}, f32[768,1024]{1,0:T(8,128)}, u32[]{:S(2)}) copy-start(f32[768,1024]{1,0:T(8,128)} %get-tuple-element.34.v_ref) | copy-start | bytes 9437188
  36.1 25.4 %copy-start.6 = (f32[8,136,128]{2,1,0:T(8,128)S(1)}, f32[8,136,128]{2,1,0:T(8,128)}, u32[]{:S(2)}) copy-start(f32[8,136,128]{2,1,0:T(8,128)} %copy-done.5) | copy-start | bytes 1671172
  36.1 25.4 %copy-start.7 = (f32[2,8,128,128]{3,2,1,0:T(8,128)S(1)}, f32[2,8,128,128]{3,2,1,0:T(8,128)}, u32[]{:S(2)}) copy-start(f32[2,8,128,128]{3,2,1,0:T(8,128)} %get-tuple-element.31.before_ref.own_before_ref) | copy-start | bytes 3145732
  36.1 25.4 %copy-start.9 = (bf16[768,128]{1,0:T(8,128)(2,1)S(1)}, bf16[768,128]{1,0:T(8,128)(2,1)}, u32[]{:S(2)}) copy-start(bf16[768,128]{1,0:T(8,128)(2,1)} %get-tuple-element.32.c_ref) | copy-start | bytes 589828
  36.1 4.5 %collective-permute-start.2 = (f32[128,128]{1,0:T(8,128)S(1)}, f32[128,128]{1,0:T(8,128)S(1)}, u32[]{:S(2)}, u32[]{:S(2)}) collective-permute-start(f32[128,128]{1,0:T(8,128)S(1)} %row_total.1), channel_id=1, source_target_pairs={{0,64},{4,68},{8,72},{12,76},{16,80},{20,84},{24,88},{28,92},{32,9... | collective-permute-start | bytes 196616 | tf_op jit(solution)/shard_map/ppermute | solution.py:645
  58.2 4.8 %collective-permute-start.3 = (f32[8,128,128]{2,1,0:T(8,128)S(1)}, f32[8,128,128]{2,1,0:T(8,128)S(1)}, u32[]{:S(2)}, u32[]{:S(2)}) collective-permute-start(f32[8,128,128]{2,1,0:T(8,128)S(1)} %all_to_all.10.chip_ref), channel_id=1, source_target_pairs={{0,4},{4,0},{8,12},{12,8},{16,20},{20,16},{24,28},{28,24},{32,36},... | collective-permute-start | bytes 1572872 | tf_op jit(solution)/shard_map/ppermute | solution.py:658
  61.5 1.9 %copy-start.3 = (f32[768,1024]{1,0:T(8,128)S(1)}, f32[768,1024]{1,0:T(8,128)}, u32[]{:S(2)}) copy-start(f32[768,1024]{1,0:T(8,128)} %get-tuple-element.37.u_ref) | copy-start | bytes 9437188
  61.5 2.8 %copy-start.4 = (f32[768,1024]{1,0:T(8,128)S(1)}, f32[768,1024]{1,0:T(8,128)}, u32[]{:S(2)}) copy-start(f32[768,1024]{1,0:T(8,128)} %get-tuple-element.38.v_ref) | copy-start | bytes 9437188
  61.5 3.1 %copy-start.8 = (f32[2,8,128,128]{3,2,1,0:T(8,128)S(1)}, f32[2,8,128,128]{3,2,1,0:T(8,128)}, u32[]{:S(2)}) copy-start(f32[2,8,128,128]{3,2,1,0:T(8,128)} %get-tuple-element.36.before_ref.away_before_ref) | copy-start | bytes 3145732
  65.4 5.7 %collective-permute-start.6 = (f32[8,768]{1,0:T(8,128)S(1)}, f32[8,768]{1,0:T(8,128)S(1)}, u32[]{:S(2)}, u32[]{:S(2)}) collective-permute-start(f32[8,768]{1,0:T(8,128)S(1)} %get-tuple-element.41.after_ref.sum_ref), channel_id=1, source_target_pairs={{0,3},{1,0},{2,1},{3,2},{4,7},{5,4},{6,5},{7,6},{8,11},{9,8},{10,9... | collective-permute-start | bytes 73736 | tf_op jit(solution)/shard_map/ppermute | solution.py:690
  67.9 4.2 %collective-permute-start.5 = (f32[8,768]{1,0:T(8,128)S(1)}, f32[8,768]{1,0:T(8,128)S(1)}, u32[]{:S(2)}, u32[]{:S(2)}) collective-permute-start(f32[8,768]{1,0:T(8,128)S(1)} %get-tuple-element.41.after_ref.sum_ref), channel_id=1, source_target_pairs={{0,2},{1,3},{2,0},{3,1},{4,6},{5,7},{6,4},{7,5},{8,10},{9,11},{10,... | collective-permute-start | bytes 73736 | tf_op jit(solution)/shard_map/ppermute | solution.py:690
  68.5 3.9 %collective-permute-start.4 = (f32[8,768]{1,0:T(8,128)S(1)}, f32[8,768]{1,0:T(8,128)S(1)}, u32[]{:S(2)}, u32[]{:S(2)}) collective-permute-start(f32[8,768]{1,0:T(8,128)S(1)} %get-tuple-element.41.after_ref.sum_ref), channel_id=1, source_target_pairs={{0,1},{1,2},{2,3},{3,0},{4,5},{5,6},{6,7},{7,4},{8,9},{9,10},{10,1... | collective-permute-start | bytes 73736 | tf_op jit(solution)/shard_map/ppermute | solution.py:690
  69.1 3.3 %copy-start.10 = (f32[2048]{0:T(1024)S(1)}, f32[2048]{0:T(1024)}, u32[]{:S(2)}) copy-start(f32[2048]{0:T(1024)} %param.16) | copy-start | bytes 24580

commit v2 on v1

--- a/solution.py
+++ b/solution.py
@@ -31,6 +31,11 @@
 
 CORE_SWAP = seq_pairs(lambda y, z, core: (y, z, 1 - core))
 NEXT_ROW = seq_pairs(lambda y, z, core: (y + 1, z, core))
+NEXT_ROW_SWAP = seq_pairs(lambda y, z, core: (y + 1, z, 1 - core))
+AROUND = [
+    seq_pairs(lambda y, z, core, step=step: (y, z + (step if core == 0 else -step), core))
+    for step in range(1, 5)
+]
 RINGS = [
     [seq_index(y, z, core) for z in range(Z_SIZE)] for y in range(Y_SIZE) for core in range(2)
 ]
@@ -74,16 +79,22 @@
     return jnp.where(core_index() == 0, rows, turned)
 
 
-def column_logs(step, rate_ref):
-    head_rows = lax.broadcasted_iota(jnp.int32, step.shape, 0)
-    terms = jnp.zeros_like(step)
-    for head in range(step.shape[0]):
-        terms = jnp.where(head_rows == head, -rate_ref[head_of(head, step.shape[0])] * step, terms)
+def stacked_groups(rows):
+    groups = rows.shape[1] // Q
+    return jnp.concatenate([rows[:, g * Q : (g + 1) * Q] for g in range(groups)], axis=0)
+
+
+def column_logs(step, rate_ref, heads):
+    head_rows = lax.rem(lax.broadcasted_iota(jnp.int32, step.shape, 0), heads)
+    rates = jnp.zeros_like(step)
+    for slot in range(heads):
+        rates = jnp.where(head_rows == slot, -rate_ref[head_of(slot, heads)], rates)
     rows = lax.broadcasted_iota(jnp.int32, (Q, Q), 0)
     cols = lax.broadcasted_iota(jnp.int32, (Q, Q), 1)
     lower = jnp.where(cols <= rows, 1.0, 0.0).astype(BF16)
     return sum(
-        lax.dot_general(lower, part, NT, preferred_element_type=F32) for part in split3(terms)
+        lax.dot_general(lower, part, NT, preferred_element_type=F32)
+        for part in split3(rates * step)
     )
 
 
@@ -99,13 +110,13 @@
     return jnp.concatenate(parts, axis=1)
 
 
-def half_states(groups, first_slot, x_of, scale_of, tail_of, stats_ref, state_ref):
+def half_states(groups, first_slot, x_of, scale_ref, tail_of, stats_ref, state_ref):
     half = state_ref.shape[0]
     for group in range(groups):
         final = stats_ref[group : group + 1, :]
         passing = stats_ref[8 + group : 9 + group, :]
         tail_b = tail_of(group)
-        scale = scale_of(group)
+        scale = scale_ref[:, group * 2 * half : (group + 1) * 2 * half]
         for pair in range(half // 2):
             slot = first_slot + 2 * pair
             scaled = scaled_pair(x_of(group, pair), scale, slot, 2 * half)
@@ -166,13 +177,14 @@
     base = lax.axis_index("seq") * (groups * Q)
     reach = jnp.ones((1, heads), F32)
     stats_ref[16:17, 0:heads] = reach
+    step = stacked_groups(slot_rows(step_ref[...]))
+    logs = column_logs(step, rate_ref, heads)
+    scale_ref[...] = jnp.exp(-logs) * step.T
+    finals = jnp.exp(logs[Q - 1 : Q, :])
     for group in range(groups):
         start = base + group * Q
         doc_first, next_end = group_bounds(doc_ref, start)
-        step = slot_rows(step_ref[:, group * Q : (group + 1) * Q])
-        logs = column_logs(step, rate_ref)
-        scale_ref[group] = jnp.exp(-logs) * step.T
-        final = jnp.exp(logs[Q - 1 : Q, :])
+        final = finals[:, group * heads : (group + 1) * heads]
         passing = jnp.where(start + (Q - 1) < next_end, final, 0.0)
         positions = lax.broadcasted_iota(jnp.int32, (N, Q), 1) + start
         b_rows = b_ref[group * Q : (group + 1) * Q, :].astype(F32).T
@@ -191,7 +203,7 @@
         groups,
         half,
         x_of,
-        lambda group: scale_ref[group],
+        scale_ref,
         lambda group: tail_ref[group],
         stats_ref,
         state_ref,
@@ -203,7 +215,7 @@
         groups,
         0,
         lambda group, pair: x_ref[group * Q : (group + 1) * Q, head_span(2 * pair, heads, 2)],
-        lambda group: scale_ref[group],
+        scale_ref,
         lambda group: tail_ref[group],
         stats_ref,
         state_ref,
@@ -281,14 +293,16 @@
     base = lax.axis_index("seq") * (groups * Q)
     rows = lax.broadcasted_iota(jnp.int32, (Q, Q), 0)
     cols = lax.broadcasted_iota(jnp.int32, (Q, Q), 1)
+    step = stacked_groups(slot_rows(step_ref[...]))
+    logs = column_logs(step, rate_ref, heads)
+    scales = jnp.exp(-logs) * step.T
+    decays = jnp.exp(logs)
     for group in range(groups):
         start = base + group * Q
         block = slice(group * Q, (group + 1) * Q)
         doc_first, next_end = group_bounds(doc_ref, start)
-        step = slot_rows(step_ref[:, block])
-        logs = column_logs(step, rate_ref)
-        scale = jnp.exp(-logs) * step.T
-        decay = jnp.exp(logs)
+        scale = scales[:, group * heads : (group + 1) * heads]
+        decay = decays[:, group * heads : (group + 1) * heads]
         final = decay[Q - 1 : Q, :]
         passing = jnp.where(start + (Q - 1) < next_end, final, 0.0)
         positions = lax.broadcasted_iota(jnp.int32, (Q, N), 0) + start
@@ -360,89 +374,158 @@
     token_ref[...] = jnp.zeros_like(token_ref)
 
 
-def join_cores_kernel(own_ref, other_ref, joined_ref, token_ref):
+def join_cores_kernel(
+    own_ref, other_ref, joined_hbm, kept_hbm, token_ref, joined_ref, sems
+):
     core = core_index()
-    for slot in range(joined_ref.shape[0]):
+    half = own_ref.shape[0]
+    copies = [pltpu.make_async_copy(other_ref, kept_hbm, sems.at[half])]
+    copies[0].start()
+    for slot in range(half):
         own, other = own_ref[slot], other_ref[slot]
         earlier = jnp.where(core == 0, own, other)
         later = jnp.where(core == 0, other, own)
         later_pass = later[N : N + 1, :]
         joined_ref[slot, 0:N, :] = later_pass * earlier[0:N, :] + later[0:N, :]
         joined_ref[slot, N : N + 8, :] = later_pass * earlier[N : N + 8, :]
+        if slot % 2 == 1:
+            part = pl.ds(slot - 1, 2)
+            copies.append(
+                pltpu.make_async_copy(joined_ref.at[part], joined_hbm.at[part], sems.at[slot])
+            )
+            copies[-1].start()
     token_ref[...] = jnp.zeros_like(token_ref)
-
-
-def row_total_kernel(parts_ref, inside_ref, swap_ref, total_ref):
+    for copy in copies:
+        copy.wait()
+
+
+def row_total_kernel(parts_ref, inside_ref, swap_ref, total_ref, copy_ref):
     total = parts_ref[0, 0:N, :]
     for chip in range(1, Z_SIZE):
         total = parts_ref[chip, N : N + 1, :] * total + parts_ref[chip, 0:N, :]
     total_ref[...] = total
-
-
-def entering_kernel(parts_ref, carried_ref, entering_ref):
-    row = lax.axis_index("seq") // (2 * Z_SIZE)
-    state = jnp.where(row > 0, carried_ref[...], 0.0)
-    for chip in range(Z_SIZE):
-        entering_ref[chip] = state
-        if chip < Z_SIZE - 1:
-            state = parts_ref[chip, N : N + 1, :] * state + parts_ref[chip, 0:N, :]
-
-
-def half_outputs_kernel(
+    copy_ref[...] = parts_ref[...]
+
+
+def entering_kernel(
+    parts_ref,
+    other_parts_ref,
+    carried_ref,
+    other_carried_ref,
+    step1_ref,
+    step2_ref,
+    step3_ref,
+    step4_ref,
+    here_ref,
+    all_ref,
+):
+    seq = lax.axis_index("seq")
+    row = seq // (2 * Z_SIZE)
+    z = lax.rem(seq // 2, Z_SIZE)
+    core = core_index()
+    for which, (chips_ref, before_row_ref) in enumerate(
+        ((parts_ref, carried_ref), (other_parts_ref, other_carried_ref))
+    ):
+        state = jnp.where(row > 0, before_row_ref[...], 0.0)
+        for chip in range(Z_SIZE):
+            all_ref[which, chip] = state
+            if chip < Z_SIZE - 1:
+                state = chips_ref[chip, N : N + 1, :] * state + chips_ref[chip, 0:N, :]
+    for step, pair_ref in ((0, here_ref), (1, step1_ref), (2, step2_ref), (3, step3_ref)):
+        chip = lax.rem(z + jnp.where(core == 0, step, Z_SIZE - step), Z_SIZE)
+        pair_ref[0] = all_ref[core, chip]
+        pair_ref[1] = all_ref[1 - core, chip]
+    step4_ref[0] = all_ref[0, lax.rem(z + 4, Z_SIZE)]
+
+
+def outputs_kernel(
+    heads,
     groups,
-    first_slot,
-    last,
-    chip_ref,
-    other_ref,
-    before_ref,
+    here_ref,
+    step1_ref,
+    step2_ref,
+    step3_ref,
+    step4_ref,
+    swapped1_ref,
+    swapped2_ref,
+    swapped3_ref,
+    swapped4_ref,
+    own_other_ref,
+    away_other_ref,
+    own_before_ref,
+    away_before_ref,
     stats_ref,
     c_ref,
-    u_ref,
-    v_ref,
-    sums_ref,
-    gated_ref,
+    own_u_ref,
+    own_v_ref,
+    away_u_ref,
+    away_v_ref,
+    own_gated_ref,
+    away_gated_ref,
     squares_ref,
     first_ref,
 ):
     core = core_index()
-    half = chip_ref.shape[0]
-    for index in range(half):
-        chip_state = chip_ref[index]
-        joined = other_ref[index, N : N + 1, :] * chip_state + other_ref[index, 0:N, :]
-        first_ref[index] = jnp.where(core == 0, chip_state, joined)
+    z = lax.rem(lax.axis_index("seq") // 2, Z_SIZE)
+    half = heads // 2
+
+    def place(chip_state, owner, earlier_ref, slot):
+        earlier = earlier_ref[owner]
+        joined = earlier[N : N + 1, :] * chip_state + earlier[0:N, :]
+        first_ref[slot] = jnp.where(core == 0, chip_state, joined)
+
+    up, down = jnp.where(core == 0, 1, Z_SIZE - 1), jnp.where(core == 0, Z_SIZE - 1, 1)
+    for pair_ref, distance in (
+        (here_ref, 0 * up),
+        (step1_ref, down),
+        (step2_ref, 2 * down),
+        (step3_ref, 3 * down),
+        (swapped1_ref, up),
+        (swapped2_ref, 2 * up),
+        (swapped3_ref, 3 * up),
+    ):
+        owner = lax.rem(z + distance, Z_SIZE)
+        place(pair_ref[0], owner, away_other_ref, owner + core * half)
+        place(pair_ref[1], owner, own_other_ref, owner + (1 - core) * half)
+    owner = lax.rem(z + 4, Z_SIZE)
+    place(step4_ref[0], owner, own_other_ref, owner)
+    place(swapped4_ref[0], owner, away_other_ref, half + owner)
+
     for group in range(groups):
         block = slice(group * Q, (group + 1) * Q)
         reach = stats_ref[16 + group : 17 + group, :]
-        squares = sums_ref[block, :] if last else jnp.zeros((Q, P_SIZE), F32)
-        for pair in range(half // 2):
-            both = []
-            for index in (2 * pair, 2 * pair + 1):
-                state = first_ref[index]
-                if group > 0:
-                    lane = slice(first_slot + index, first_slot + index + 1)
-                    state = state * reach[:, lane] + before_ref[group - 1, index]
-                both.append(state.astype(BF16))
-            carried = jnp.dot(
-                c_ref[block, :], jnp.concatenate(both, axis=1), preferred_element_type=F32
+        squares = jnp.zeros((Q, P_SIZE), F32)
+        for side, (u_ref, v_ref, before_ref, gated_ref) in enumerate(
+            (
+                (own_u_ref, own_v_ref, own_before_ref, own_gated_ref),
+                (away_u_ref, away_v_ref, away_before_ref, away_gated_ref),
             )
-            span = slice(2 * pair * P_SIZE, 2 * (pair + 1) * P_SIZE)
-            gated = u_ref[block, span] + v_ref[block, span] * carried
-            gated_ref[block, span] = gated
-            square = gated * gated
-            squares = squares + square[:, 0:P_SIZE] + square[:, P_SIZE:]
-        if last:
-            squares_ref[:, block] = jnp.broadcast_to(
-                jnp.sum(squares.T, axis=0, keepdims=True), (8, Q)
-            )
-        else:
-            squares_ref[block, :] = squares
+        ):
+            for pair in range(half // 2):
+                both = []
+                for index in (2 * pair, 2 * pair + 1):
+                    slot = side * half + index
+                    state = first_ref[slot]
+                    if group > 0:
+                        state = state * reach[:, slot : slot + 1] + before_ref[group - 1, index]
+                    both.append(state.astype(BF16))
+                carried = jnp.dot(
+                    c_ref[block, :], jnp.concatenate(both, axis=1), preferred_element_type=F32
+                )
+                span = slice(2 * pair * P_SIZE, 2 * (pair + 1) * P_SIZE)
+                gated = u_ref[block, span] + v_ref[block, span] * carried
+                gated_ref[block, span] = gated
+                square = gated * gated
+                squares = squares + square[:, 0:P_SIZE] + square[:, P_SIZE:]
+        squares_ref[:, block] = jnp.broadcast_to(
+            jnp.sum(squares.T, axis=0, keepdims=True), (8, Q)
+        )
 
 
 def write_states_kernel(
     heads,
     groups,
-    own_first_ref,
-    away_first_ref,
+    first_ref,
     own_before_ref,
     away_before_ref,
     stats_ref,
@@ -456,13 +539,11 @@
     copies = []
     for group in range(groups):
         reach = stats_ref[16 + group : 17 + group, :]
-        for side, (first_ref, before_ref) in enumerate(
-            ((own_first_ref, own_before_ref), (away_first_ref, away_before_ref))
-        ):
+        for side, before_ref in enumerate((own_before_ref, away_before_ref)):
             for index in range(half):
-                state = first_ref[index]
+                slot = side * half + index
+                state = first_ref[slot]
                 if group > 0:
-                    slot = side * half + index
                     state = state * reach[:, slot : slot + 1] + before_ref[group - 1, index]
                 states_ref[group, side, index] = state.T
             copy = pltpu.make_async_copy(
@@ -544,7 +625,6 @@
     half_state = sds((half, N + 8, P_SIZE), F32)
     half_before = sds((groups - 1, half, N, P_SIZE), F32)
     half_wide = sds((row_count, width // 2), F32)
-    half_first = sds((half, N, P_SIZE), F32)
 
     def in_hbm(*arrays):
         return [pltpu.with_memory_space_constraint(array, pltpu.HBM) for array in arrays]
@@ -556,7 +636,7 @@
         out_shape=[
             half_state,
             sds((24, P_SIZE), F32),
-            sds((groups, Q, heads), F32),
+            sds((Q, groups * heads), F32),
             sds((groups, N, Q), BF16),
         ],
         scratch_shapes=[
@@ -584,9 +664,12 @@
         name="own_states",
     )(stats, scale, tail, head_input)
 
-    joined, joined_token = pl.pallas_call(
+    joined, own_kept, joined_token = pl.pallas_call(
         join_cores_kernel,
-        out_shape=[half_state, token],
+        in_specs=[vmem, vmem],
+        out_specs=[hbm, hbm, vmem],
+        out_shape=[pltpu.HBM(half_state.shape, F32)] * 2 + [token],
+        scratch_shapes=[pltpu.VMEM(half_state.shape, F32), dma((half + 1,))],
         compiler_params=params(8),
         cost_estimate=cost(1_000_000, 1_700_000),
         name="join_cores",
@@ -634,55 +717,51 @@
         ),
         joined_token,
     )
-    total = pl.pallas_call(
+    total, parts = pl.pallas_call(
         row_total_kernel,
         in_specs=[vmem, anywhere, anywhere],
-        out_shape=sds((N, P_SIZE), F32),
+        out_shape=[sds((N, P_SIZE), F32), half_state],
         compiler_params=params(8),
         cost_estimate=cost(300_000, 600_000),
         name="row_total",
     )(parts, inside_token, away_other)
     carried = lax.ppermute(total, "seq", NEXT_ROW)
-    entering = pl.pallas_call(
+    other_carried = lax.ppermute(total, "seq", NEXT_ROW_SWAP)
+    other_parts = lax.ppermute(parts, "seq", CORE_SWAP)
+    pair_state = sds((2, N, P_SIZE), F32)
+    *steps, here = pl.pallas_call(
         entering_kernel,
-        out_shape=sds((Z_SIZE, N, P_SIZE), F32),
+        out_shape=[pair_state] * 3 + [sds((1, N, P_SIZE), F32), pair_state],
+        scratch_shapes=[pltpu.VMEM((2, Z_SIZE, N, P_SIZE), F32)],
         compiler_params=params(8),
         cost_estimate=cost(20_000_000_000, 1_100_000),
         name="entering",
-    )(parts, carried)
-
-    own_chip = lax.all_to_all(
-        entering, "seq", split_axis=0, concat_axis=0, axis_index_groups=RINGS, tiled=True
-    )
-
-    away_chip = lax.ppermute(own_chip, "seq", CORE_SWAP)
-
-    def half_outputs(first_slot, last, *operands):
-        sums = sds((8, row_count), F32) if last else sds((row_count, P_SIZE), F32)
-        return pl.pallas_call(
-            functools.partial(half_outputs_kernel, groups, first_slot, last),
-            in_specs=[vmem] * 7 + [vmem if last else anywhere],
-            out_specs=[vmem] * 3,
-            out_shape=[half_wide, sums, half_first],
-            compiler_params=params(20),
-            cost_estimate=cost(2_000_000_000, 9_000_000),
-            name="away_outputs" if last else "own_outputs",
-        )(*operands)
-
-    own_gated, own_squares, own_first = half_outputs(
-        0, False, own_chip, own_other, own_before, stats, entry_c, own_u, own_v, stats
-    )
-    away_gated, squares, away_first = half_outputs(
-        half,
-        True,
-        away_chip,
+    )(parts, other_parts, carried, other_carried)
+    arrived = [lax.ppermute(sent, "seq", pairs) for sent, pairs in zip(steps, AROUND)]
+    swapped = [lax.ppermute(state, "seq", CORE_SWAP) for state in arrived]
+
+    own_gated, away_gated, squares, first = pl.pallas_call(
+        functools.partial(outputs_kernel, heads, groups),
+        in_specs=[vmem] * 19,
+        out_specs=[vmem] * 4,
+        out_shape=[half_wide] * 2 + [sds((8, row_count), F32), sds((heads, N, P_SIZE), F32)],
+        compiler_params=params(30),
+        cost_estimate=cost(2_000_000, 9_000),
+        name="outputs",
+    )(
+        here,
+        *arrived,
+        *swapped,
+        own_kept,
         away_other,
+        own_before,
         away_before,
         stats,
         entry_c,
+        own_u,
+        own_v,
         away_u,
         away_v,
-        own_squares,
     )
 
     tp_size = 4
@@ -692,7 +771,7 @@
     ]
     group_states, states_token = pl.pallas_call(
         functools.partial(write_states_kernel, heads, groups),
-        in_specs=[vmem] * 5 + [anywhere],
+        in_specs=[vmem] * 4 + [anywhere],
         out_specs=[hbm, vmem],
         out_shape=[sds((groups, heads, P_SIZE, N), F32), token],
         scratch_shapes=[
@@ -702,7 +781,7 @@
         compiler_params=params(16),
         cost_estimate=cost(4_000_000_000, 9_000_000),
         name="write_states",
-    )(own_first, away_first, own_before, away_before, stats, squares)
+    )(first, own_before, away_before, stats, squares)
     mixed_out = pl.pallas_call(
         functools.partial(scale_kernel, width * tp_size, heads),
         in_specs=[vmem] * 7 + [anywhere],

time: 74.8 us -> 71.4 us (0.955); the launches traced: 74.6 us -> 70.2 us
  blocking collectives: 17.6 us -> 0 us
  starting transfers between devices: 18.7 us -> 32.3 us
  local copies, waits for them, and re-layouts: 2.4 us -> 0.04 us
  waiting for transfers between devices: 12.5 us -> 13.9 us
    all_to_all x1 -> x0, blocking collectives: 17.6 us -> none  [local(): lax.all_to_all(entering, 'seq', split_axis=0, concat_axis=0, axis_index_g...]
    ppermute x1 -> x10, starting transfers between devices: 3.23 us -> 16.9 us  [the longest x4 9.22 us: local(): swapped = [lax.ppermute(state, 'seq', CORE_SWAP) for state in arrived]]
    ppermute x1 -> x10, waiting for transfers between devices: 0.76 us -> 4.48 us  [the longest x1 2.85 us: local(): other_carried = lax.ppermute(total, 'seq', NEXT_ROW_SWAP)]
    unnamed x22 -> x20, local copies, waits for them, and re-layouts: 2.4 us -> 0.04 us
    ppermute x1, waiting for transfers between devices: 3.1 us -> 0.74 us  [local(): carried = lax.ppermute(total, 'seq', NEXT_ROW)]
    pallas_call x4 -> x3, Pallas kernels: 2.55 us -> 3.22 us  [the longest x1 1.98 us: local(): pl.pallas_call(functools.partial(outputs_kernel, heads, groups), in_specs...]
  transfers between devices with their start and end apart: 8 -> 17, of which waited for: 6 -> 8; matrix products, arithmetic and copies ran while one was open for 0% -> 0% of each run, Pallas kernels for 20% -> 20%
where the time goes in v2:
time: 71.4 us; the launch traced here: 70.2 us
  starting transfers between devices  32.3 us (45%)
  Pallas kernels  22.9 us (32%)
  waiting for transfers between devices  13.9 us (19%)
  between operations  0.99 us (1%)
    pallas_call x1, Pallas kernels, local(): pl.pallas_call(functools.partial(inside_kernel, heads, groups), in_specs=...  10.9 us
    ppermute x4, starting transfers between devices, local(): swapped = [lax.ppermute(state, 'seq', CORE_SWAP) for state in arrived]  9.22 us
    all_to_all x1, waiting for transfers between devices, local(): lax.all_to_all(joined, 'seq', split_axis=0, concat_axis=0, axis_index_gro...  7.07 us
    all_to_all x1, starting transfers between devices, local(): lax.all_to_all(joined, 'seq', split_axis=0, concat_axis=0, axis_index_gro...  6.46 us
    ppermute x4, starting transfers between devices, local(): lax.ppermute(sent, 'seq', pairs)  5.79 us
    ppermute x3, starting transfers between devices, local(): lax.ppermute(squares, 'tp', [(i, (i + k) % tp_size) for i in range(tp_siz...  3.68 us
    pallas_call x1, Pallas kernels, local(): pl.pallas_call(functools.partial(away_states_kernel, heads, groups), in_s...  3.43 us
    ppermute x1, starting transfers between devices, local(): own_other = lax.ppermute(away_state, 'seq', CORE_SWAP)  3.33 us
  transfers between devices with their start and end apart: 17, of which 8 were waited for; matrix products, arithmetic and copies ran while one was open for 0% of the time, Pallas kernels for 20%

profile of v2, /device:TPU:1, one launch (start us, length us, event | category | flops | bytes accessed | tf_op | source)
XLA Modules:
  0.0 70.2 jit_solution(7868082187115406668)
XLA Ops:
  0.6 0.0 copy-start.4
  0.6 3.4 %away_states.1 = (f32[8,136,128]{2,1,0:T(8,128)S(1)}, f32[24,128]{1,0:T(8,128)S(1)}, f32[256,48]{1,0:T(8,128)S(1)}, bf16[3,128,256]{2,1,0:T(8,128)(2,1)S(1)}) custom-call(s32[16]{0:T(128)} %doc_hbm.3, f32[16]{0:T(128)} %rate_hbm.3, f32[16,768]{1,0:T(8,128)} %bitcast.3, bf16[768,128]{1,0:T(8,128)(2,1)} %b_hbm.3, bf16[768,2048]{1,0:T(8,128)(2,1)} %x_hbm.3), custom_call_target="tpu_custom_call" | custom-call | flops 200000000 | bytes 4000000 | tf_op jit(solution)/shard_map/away_states/pallas_call | solution.py:632
  4.1 3.3 %collective-permute-start = (f32[8,136,128]{2,1,0:T(8,128)S(1)}, f32[8,136,128]{2,1,0:T(8,128)S(1)}, u32[]{:S(2)}, u32[]{:S(2)}) collective-permute-start(f32[8,136,128]{2,1,0:T(8,128)S(1)} %get-tuple-element.33), channel_id=1, source_target_pairs={{0,4},{4,0},{8,12},{12,8},{16,20},{20,16},{24,28},{28,24},{32,36},... | collective-permute-start | bytes 1671176 | tf_op jit(solution)/shard_map/ppermute | solution.py:655
  7.4 0.0 copy-done.4
  7.4 1.3 %own_states.1.own_ref = f32[8,136,128]{2,1,0:T(8,128)S(1)} custom-call(f32[24,128]{1,0:T(8,128)S(1)} %get-tuple-element.30.stats_ref, f32[256,48]{1,0:T(8,128)S(1)} %get-tuple-element.31.scale_ref, bf16[3,128,256]{2,1,0:T(8,128)(2,1)S(1)} %get-tuple-element.32.tail_ref, bf16[768,2048]{1,0:T(8,128)(2,1)S(1)} %copy-done.4), custom_call_target="tpu_custom_call" | custom-call | flops 2000000000 | bytes 4000000 | tf_op jit(solution)/shard_map/own_states/pallas_call | solution.py:657
  8.7 0.3 collective-permute-done.other_ref
  9.0 1.1 %join_cores.1 = (f32[8,136,128]{2,1,0:T(8,128)}, f32[8,136,128]{2,1,0:T(8,128)}, f32[8,128]{1,0:T(8,128)S(1)}) custom-call(f32[8,136,128]{2,1,0:T(8,128)S(1)} %own_states.1.own_ref, f32[8,136,128]{2,1,0:T(8,128)S(1)} %collective-permute-done.other_ref), custom_call_target="tpu_custom_call" | custom-call | flops 1000000 | bytes 1700000 | tf_op jit(solution)/shard_map/join_cores/pallas_call | solution.py:667
  10.1 6.5 %all-to-all-start = ((f32[8,136,128]{2,1,0:T(8,128)}), f32[8,136,128]{2,1,0:T(8,128)S(1)}, u32[]{:S(2)}, u32[]{:S(2)}) async-start(f32[8,136,128]{2,1,0:T(8,128)} %get-tuple-element.34), calls=%async_computation | async-start | bytes 1114112 | tf_op jit(solution)/shard_map/all_to_all | solution.py:677
  16.6 0.7 collective-permute-start.1
  17.2 10.9 %inside.1 = (f32[768,1024]{1,0:T(8,128)}, f32[768,1024]{1,0:T(8,128)}, f32[768,1024]{1,0:T(8,128)}, f32[768,1024]{1,0:T(8,128)}, f32[2,8,128,128]{3,2,1,0:T(8,12...) custom-call(s32[16]{0:T(128)} %doc_hbm.3, f32[16]{0:T(128)} %rate_hbm.3, ...), custom_call_target="tpu_custom_call" | custom-call | flops 8000000000 | bytes 20000000 | tf_op jit(solution)/shard_map/inside/pallas_call | solution.py:682
  28.1 0.0 collective-permute-done.1.swap_ref.away_other_ref
  28.2 7.1 %all-to-all-done.parts_ref = f32[8,136,128]{2,1,0:T(8,128)S(1)} async-done(((f32[8,136,128]{2,1,0:T(8,128)}), f32[8,136,128]{2,1,0:T(8,128)S(1)}, u32[]{:S(2)}, u32[]{:S(2)}) %all-to-all-start) | async-done | bytes 557088 | tf_op jit(solution)/shard_map/all_to_all | solution.py:677
  35.2 0.1 row_total.1
  35.3 0.6 collective-permute-start.2
  35.9 0.0 copy-start.5
  35.9 0.0 copy-start.6
  35.9 0.0 copy-start.7
  35.9 1.3 %collective-permute-start.4 = (f32[128,128]{1,0:T(8,128)S(1)}, f32[128,128]{1,0:T(8,128)S(1)}, u32[]{:S(2)}, u32[]{:S(2)}) collective-permute-start(f32[128,128]{1,0:T(8,128)S(1)} %get-tuple-element.38), channel_id=1, source_target_pairs={{0,68},{4,64},{8,76},{12,72},{16,84},{20,80},{24,92},{28,88},{32,1... | collective-permute-start | bytes 196616 | tf_op jit(solution)/shard_map/ppermute | solution.py:729
  37.2 1.3 %collective-permute-start.3 = (f32[128,128]{1,0:T(8,128)S(1)}, f32[128,128]{1,0:T(8,128)S(1)}, u32[]{:S(2)}, u32[]{:S(2)}) collective-permute-start(f32[128,128]{1,0:T(8,128)S(1)} %get-tuple-element.38), channel_id=1, source_target_pairs={{0,64},{4,68},{8,72},{12,76},{16,80},{20,84},{24,88},{28,92},{32,9... | collective-permute-start | bytes 196616 | tf_op jit(solution)/shard_map/ppermute | solution.py:728
  38.5 2.9 %collective-permute-done.4.other_carried_ref = f32[128,128]{1,0:T(8,128)S(1)} collective-permute-done((f32[128,128]{1,0:T(8,128)S(1)}, f32[128,128]{1,0:T(8,128)S(1)}, u32[]{:S(2)}, u32[]{:S(2)}) %collective-permute-start.4) | collective-permute-done | bytes 65568 | tf_op jit(solution)/shard_map/ppermute | solution.py:729
  41.4 0.7 %collective-permute-done.3.carried_ref = f32[128,128]{1,0:T(8,128)S(1)} collective-permute-done((f32[128,128]{1,0:T(8,128)S(1)}, f32[128,128]{1,0:T(8,128)S(1)}, u32[]{:S(2)}, u32[]{:S(2)}) %collective-permute-start.3) | collective-permute-done | bytes 65568 | tf_op jit(solution)/shard_map/ppermute | solution.py:728
  42.1 0.0 collective-permute-done.2.other_parts_ref
  42.1 0.1 entering.1
  42.3 0.1 collective-permute-start.5
  42.3 0.6 collective-permute-start.6
  42.9 2.5 %collective-permute-start.7 = (f32[2,128,128]{2,1,0:T(8,128)S(1)}, f32[2,128,128]{2,1,0:T(8,128)S(1)}, u32[]{:S(2)}, u32[]{:S(2)}) collective-permute-start(f32[2,128,128]{2,1,0:T(8,128)S(1)} %get-tuple-element.42), channel_id=1, source_target_pairs={{0,24},{4,44},{8,32},{12,52},{16,40},{20,60},{24,48},{28,4},{32,56... | collective-permute-start | bytes 393224 | tf_op jit(solution)/shard_map/ppermute | solution.py:740
  45.4 2.6 %collective-permute-start.8 = (f32[1,128,128]{2,1,0:T(8,128)S(1)}, f32[1,128,128]{2,1,0:T(8,128)S(1)}, u32[]{:S(2)}, u32[]{:S(2)}) collective-permute-start(f32[1,128,128]{2,1,0:T(8,128)S(1)} %get-tuple-element.43), channel_id=1, source_target_pairs={{0,32},{4,36},{8,40},{12,44},{16,48},{20,52},{24,56},{28,60},{32,0... | collective-permute-start | bytes 196616 | tf_op jit(solution)/shard_map/ppermute | solution.py:740
  48.1 0.0 collective-permute-done.5.step1_ref
  48.1 1.9 %collective-permute-start.9 = (f32[2,128,128]{2,1,0:T(8,128)S(1)}, f32[2,128,128]{2,1,0:T(8,128)S(1)}, u32[]{:S(2)}, u32[]{:S(2)}) collective-permute-start(f32[2,128,128]{2,1,0:T(8,128)S(1)} %collective-permute-done.5.step1_ref), channel_id=1, source_target_pairs={{0,4},{4,0},{8,12},{12,8},{16,20},{20,16},{24,28},{28,24},{32,36},... | collective-permute-start | bytes 393224 | tf_op jit(solution)/shard_map/ppermute | solution.py:741
  50.0 0.4 collective-permute-done.6.step2_ref
  50.4 6.7 %collective-permute-start.10 = (f32[2,128,128]{2,1,0:T(8,128)S(1)}, f32[2,128,128]{2,1,0:T(8,128)S(1)}, u32[]{:S(2)}, u32[]{:S(2)}) collective-permute-start(f32[2,128,128]{2,1,0:T(8,128)S(1)} %collective-permute-done.6.step2_ref), channel_id=1, source_target_pairs={{0,4},{4,0},{8,12},{12,8},{16,20},{20,16},{24,28},{28,24},{32,36},... | collective-permute-start | bytes 393224 | tf_op jit(solution)/shard_map/ppermute | solution.py:741
  57.1 0.0 collective-permute-done.7.step3_ref
  57.1 0.5 collective-permute-start.11
  57.6 0.0 collective-permute-done.8.step4_ref
  57.6 0.0 collective-permute-start.12
  57.6 1.3 %collective-permute-done.12.swapped4_ref = f32[1,128,128]{2,1,0:T(8,128)S(1)} collective-permute-done((f32[1,128,128]{2,1,0:T(8,128)S(1)}, f32[1,128,128]{2,1,0:T(8,128)S(1)}, u32[]{:S(2)}, u32[]{:S(2)}) %collective-permute-start.12) | collective-permute-done | bytes 65568 | tf_op jit(solution)/shard_map/ppermute | solution.py:741
  58.9 0.0 collective-permute-done.9.swapped1_ref
  58.9 0.0 collective-permute-done.10.swapped2_ref
  58.9 0.0 collective-permute-done.11.swapped3_ref
  59.0 2.0 %outputs.1 = (f32[768,1024]{1,0:T(8,128)S(1)}, f32[768,1024]{1,0:T(8,128)S(1)}, f32[8,768]{1,0:T(8,128)S(1)}, f32[16,128,128]{2,1,0:T(8,128)S(1)}) custom-call(f32[2,128,128]{2,1,0:T(8,128)S(1)} %get-tuple-element.39.here_ref, f32[2,128,128]{2,1,0:T(8,128)S(1)} %collective-permute-done.5.step1_ref, f32[2,128,128]{2,1,0:T(8,128)S(1)} %collective-permute-done.6.step2_ref, ...), custom_call_target="tpu_custom_call" | custom-call | flops 2000000 | bytes 9000 | tf_op jit(solution)/shard_map/outputs/pallas_call | solution.py:743
  61.0 2.5 %collective-permute-start.15 = (f32[8,768]{1,0:T(8,128)S(1)}, f32[8,768]{1,0:T(8,128)S(1)}, u32[]{:S(2)}, u32[]{:S(2)}) collective-permute-start(f32[8,768]{1,0:T(8,128)S(1)} %get-tuple-element.54.after_ref.sum_ref), channel_id=1, source_target_pairs={{0,3},{1,0},{2,1},{3,2},{4,7},{5,4},{6,5},{7,6},{8,11},{9,8},{10,9... | collective-permute-start | bytes 73736 | tf_op jit(solution)/shard_map/ppermute | solution.py:769
  63.5 0.5 collective-permute-start.14
  64.0 0.6 collective-permute-start.13
  64.7 2.0 %write_states.1 = (f32[3,16,128,128]{3,2,1,0:T(8,128)}, f32[8,128]{1,0:T(8,128)S(1)}) custom-call(f32[16,128,128]{2,1,0:T(8,128)S(1)} %get-tuple-element.55.first_ref, f32[2,8,128,128]{3,2,1,0:T(8,128)S(1)} %copy-done.5, f32[2,8,128,128]{3,2,1,0:T(8,128)S(1)} %copy-done.6, f32[24,128]{1,0:T(8,128)S(1)} %get-tuple-element.30.stats_ref, ...), custom_call_target="tpu_custom_call" | custom-call | flops 4000000000 | bytes 9000000 | tf_op jit(solution)/shard_map/write_states/pallas_call | solution.py:772
  66.6 0.0 collective-permute-done.15.c_ref
  66.6 1.1 %collective-permute-done.14.b_ref = f32[8,768]{1,0:T(8,128)S(1)} collective-permute-done((f32[8,768]{1,0:T(8,128)S(1)}, f32[8,768]{1,0:T(8,128)S(1)}, u32[]{:S(2)}, u32[]{:S(2)}) %collective-permute-start.14) | collective-permute-done | bytes 24608 | tf_op jit(solution)/shard_map/ppermute | solution.py:769
  67.7 0.3 collective-permute-done.13.a_ref
  68.0 2.0 %scale.1 = bf16[768,2048]{1,0:T(8,128)(2,1)} custom-call(f32[768,1024]{1,0:T(8,128)S(1)} %get-tuple-element.52.own_ref, f32[768,1024]{1,0:T(8,128)S(1)} %get-tuple-element.53.away_ref, f32[1,2048]{1,0:T(1,128)S(1)} %bitcast.2, f32[8,768]{1,0:T(8,128)S(1)} %get-tuple-element.54.after_ref.sum_ref, f32[8,768]{1,0:T(8,128)S(1)} %collective-permute-done.13.a_ref, ...), custom_call_target="tpu_custom_call" | custom-call | flops 5000000 | bytes 6500000 | tf_op jit(solution)/shard_map/scale/pallas_call | solution.py:785
  (15 shorter events, 0.0 us)
Async XLA Ops:
  0.6 6.8 %copy-start.4 = (bf16[768,2048]{1,0:T(8,128)(2,1)S(1)}, bf16[768,2048]{1,0:T(8,128)(2,1)}, u32[]{:S(2)}) copy-start(bf16[768,2048]{1,0:T(8,128)(2,1)} %x_hbm.3) | copy-start | bytes 9437188
  4.1 4.9 %collective-permute-start = (f32[8,136,128]{2,1,0:T(8,128)S(1)}, f32[8,136,128]{2,1,0:T(8,128)S(1)}, u32[]{:S(2)}, u32[]{:S(2)}) collective-permute-start(f32[8,136,128]{2,1,0:T(8,128)S(1)} %get-tuple-element.33), channel_id=1, source_target_pairs={{0,4},{4,0},{8,12},{12,8},{16,20},{20,16},{24,28},{28,24},{32,36},... | collective-permute-start | bytes 1671176 | tf_op jit(solution)/shard_map/ppermute | solution.py:655
  10.1 25.1 %all-to-all-start = ((f32[8,136,128]{2,1,0:T(8,128)}), f32[8,136,128]{2,1,0:T(8,128)S(1)}, u32[]{:S(2)}, u32[]{:S(2)}) async-start(f32[8,136,128]{2,1,0:T(8,128)} %get-tuple-element.34), calls=%async_computation | async-start | bytes 1114112 | tf_op jit(solution)/shard_map/all_to_all | solution.py:677
  16.6 11.6 %collective-permute-start.1 = (f32[8,136,128]{2,1,0:T(8,128)S(1)}, f32[8,136,128]{2,1,0:T(8,128)S(1)}, u32[]{:S(2)}, u32[]{:S(2)}) collective-permute-start(f32[8,136,128]{2,1,0:T(8,128)S(1)} %own_states.1.own_ref), channel_id=1, source_target_pairs={{0,4},{4,0},{8,12},{12,8},{16,20},{20,16},{24,28},{28,24},{32,36},... | collective-permute-start | bytes 1671176 | tf_op jit(solution)/shard_map/ppermute | solution.py:680
  35.3 6.8 %collective-permute-start.2 = (f32[8,136,128]{2,1,0:T(8,128)S(1)}, f32[8,136,128]{2,1,0:T(8,128)S(1)}, u32[]{:S(2)}, u32[]{:S(2)}) collective-permute-start(f32[8,136,128]{2,1,0:T(8,128)S(1)} %get-tuple-element.37.parts_ref), channel_id=1, source_target_pairs={{0,4},{4,0},{8,12},{12,8},{16,20},{20,16},{24,28},{28,24},{32,36},... | collective-permute-start | bytes 1671176 | tf_op jit(solution)/shard_map/ppermute | solution.py:730
  35.9 23.0 %copy-start = (f32[768,1024]{1,0:T(8,128)S(1)}, f32[768,1024]{1,0:T(8,128)}, u32[]{:S(2)}) copy-start(f32[768,1024]{1,0:T(8,128)} %get-tuple-element.48.own_u_ref) | copy-start | bytes 9437188
  35.9 23.1 %copy-start.1 = (f32[768,1024]{1,0:T(8,128)S(1)}, f32[768,1024]{1,0:T(8,128)}, u32[]{:S(2)}) copy-start(f32[768,1024]{1,0:T(8,128)} %get-tuple-element.49.own_v_ref) | copy-start | bytes 9437188
  35.9 23.1 %copy-start.2 = (f32[768,1024]{1,0:T(8,128)S(1)}, f32[768,1024]{1,0:T(8,128)}, u32[]{:S(2)}) copy-start(f32[768,1024]{1,0:T(8,128)} %get-tuple-element.50.away_u_ref) | copy-start | bytes 9437188
  35.9 23.1 %copy-start.3 = (f32[768,1024]{1,0:T(8,128)S(1)}, f32[768,1024]{1,0:T(8,128)}, u32[]{:S(2)}) copy-start(f32[768,1024]{1,0:T(8,128)} %get-tuple-element.51.away_v_ref) | copy-start | bytes 9437188
  35.9 23.1 %copy-start.5 = (f32[2,8,128,128]{3,2,1,0:T(8,128)S(1)}, f32[2,8,128,128]{3,2,1,0:T(8,128)}, u32[]{:S(2)}) copy-start(f32[2,8,128,128]{3,2,1,0:T(8,128)} %get-tuple-element.45.own_before_ref) | copy-start | bytes 3145732
  35.9 23.1 %copy-start.6 = (f32[2,8,128,128]{3,2,1,0:T(8,128)S(1)}, f32[2,8,128,128]{3,2,1,0:T(8,128)}, u32[]{:S(2)}) copy-start(f32[2,8,128,128]{3,2,1,0:T(8,128)} %get-tuple-element.46.away_before_ref) | copy-start | bytes 3145732
  35.9 23.1 %copy-start.7 = (f32[8,136,128]{2,1,0:T(8,128)S(1)}, f32[8,136,128]{2,1,0:T(8,128)}, u32[]{:S(2)}) copy-start(f32[8,136,128]{2,1,0:T(8,128)} %get-tuple-element.44.own_other_ref) | copy-start | bytes 1671172
  35.9 23.1 %copy-start.8 = (bf16[768,128]{1,0:T(8,128)(2,1)S(1)}, bf16[768,128]{1,0:T(8,128)(2,1)}, u32[]{:S(2)}) copy-start(bf16[768,128]{1,0:T(8,128)(2,1)} %get-tuple-element.47.c_ref) | copy-start | bytes 589828
  35.9 5.5 %collective-permute-start.4 = (f32[128,128]{1,0:T(8,128)S(1)}, f32[128,128]{1,0:T(8,128)S(1)}, u32[]{:S(2)}, u32[]{:S(2)}) collective-permute-start(f32[128,128]{1,0:T(8,128)S(1)} %get-tuple-element.38), channel_id=1, source_target_pairs={{0,68},{4,64},{8,76},{12,72},{16,84},{20,80},{24,92},{28,88},{32,1... | collective-permute-start | bytes 196616 | tf_op jit(solution)/shard_map/ppermute | solution.py:729
  37.2 4.9 %collective-permute-start.3 = (f32[128,128]{1,0:T(8,128)S(1)}, f32[128,128]{1,0:T(8,128)S(1)}, u32[]{:S(2)}, u32[]{:S(2)}) collective-permute-start(f32[128,128]{1,0:T(8,128)S(1)} %get-tuple-element.38), channel_id=1, source_target_pairs={{0,64},{4,68},{8,72},{12,76},{16,80},{20,84},{24,88},{28,92},{32,9... | collective-permute-start | bytes 196616 | tf_op jit(solution)/shard_map/ppermute | solution.py:728
  42.3 5.8 %collective-permute-start.5 = (f32[2,128,128]{2,1,0:T(8,128)S(1)}, f32[2,128,128]{2,1,0:T(8,128)S(1)}, u32[]{:S(2)}, u32[]{:S(2)}) collective-permute-start(f32[2,128,128]{2,1,0:T(8,128)S(1)} %get-tuple-element.40), channel_id=1, source_target_pairs={{0,8},{4,60},{8,16},{12,4},{16,24},{20,12},{24,32},{28,20},{32,40}... | collective-permute-start | bytes 393224 | tf_op jit(solution)/shard_map/ppermute | solution.py:740
  42.3 8.0 %collective-permute-start.6 = (f32[2,128,128]{2,1,0:T(8,128)S(1)}, f32[2,128,128]{2,1,0:T(8,128)S(1)}, u32[]{:S(2)}, u32[]{:S(2)}) collective-permute-start(f32[2,128,128]{2,1,0:T(8,128)S(1)} %get-tuple-element.41), channel_id=1, source_target_pairs={{0,16},{4,52},{8,24},{12,60},{16,32},{20,4},{24,40},{28,12},{32,48... | collective-permute-start | bytes 393224 | tf_op jit(solution)/shard_map/ppermute | solution.py:740
  42.9 14.2 %collective-permute-start.7 = (f32[2,128,128]{2,1,0:T(8,128)S(1)}, f32[2,128,128]{2,1,0:T(8,128)S(1)}, u32[]{:S(2)}, u32[]{:S(2)}) collective-permute-start(f32[2,128,128]{2,1,0:T(8,128)S(1)} %get-tuple-element.42), channel_id=1, source_target_pairs={{0,24},{4,44},{8,32},{12,52},{16,40},{20,60},{24,48},{28,4},{32,56... | collective-permute-start | bytes 393224 | tf_op jit(solution)/shard_map/ppermute | solution.py:740
  45.4 12.2 %collective-permute-start.8 = (f32[1,128,128]{2,1,0:T(8,128)S(1)}, f32[1,128,128]{2,1,0:T(8,128)S(1)}, u32[]{:S(2)}, u32[]{:S(2)}) collective-permute-start(f32[1,128,128]{2,1,0:T(8,128)S(1)} %get-tuple-element.43), channel_id=1, source_target_pairs={{0,32},{4,36},{8,40},{12,44},{16,48},{20,52},{24,56},{28,60},{32,0... | collective-permute-start | bytes 196616 | tf_op jit(solution)/shard_map/ppermute | solution.py:740
  48.1 10.8 %collective-permute-start.9 = (f32[2,128,128]{2,1,0:T(8,128)S(1)}, f32[2,128,128]{2,1,0:T(8,128)S(1)}, u32[]{:S(2)}, u32[]{:S(2)}) collective-permute-start(f32[2,128,128]{2,1,0:T(8,128)S(1)} %collective-permute-done.5.step1_ref), channel_id=1, source_target_pairs={{0,4},{4,0},{8,12},{12,8},{16,20},{20,16},{24,28},{28,24},{32,36},... | collective-permute-start | bytes 393224 | tf_op jit(solution)/shard_map/ppermute | solution.py:741
  50.4 8.5 %collective-permute-start.10 = (f32[2,128,128]{2,1,0:T(8,128)S(1)}, f32[2,128,128]{2,1,0:T(8,128)S(1)}, u32[]{:S(2)}, u32[]{:S(2)}) collective-permute-start(f32[2,128,128]{2,1,0:T(8,128)S(1)} %collective-permute-done.6.step2_ref), channel_id=1, source_target_pairs={{0,4},{4,0},{8,12},{12,8},{16,20},{20,16},{24,28},{28,24},{32,36},... | collective-permute-start | bytes 393224 | tf_op jit(solution)/shard_map/ppermute | solution.py:741
  57.1 1.8 %collective-permute-start.11 = (f32[2,128,128]{2,1,0:T(8,128)S(1)}, f32[2,128,128]{2,1,0:T(8,128)S(1)}, u32[]{:S(2)}, u32[]{:S(2)}) collective-permute-start(f32[2,128,128]{2,1,0:T(8,128)S(1)} %collective-permute-done.7.step3_ref), channel_id=1, source_target_pairs={{0,4},{4,0},{8,12},{12,8},{16,20},{20,16},{24,28},{28,24},{32,36},... | collective-permute-start | bytes 393224 | tf_op jit(solution)/shard_map/ppermute | solution.py:741
  57.6 1.3 %collective-permute-start.12 = (f32[1,128,128]{2,1,0:T(8,128)S(1)}, f32[1,128,128]{2,1,0:T(8,128)S(1)}, u32[]{:S(2)}, u32[]{:S(2)}) collective-permute-start(f32[1,128,128]{2,1,0:T(8,128)S(1)} %collective-permute-done.8.step4_ref), channel_id=1, source_target_pairs={{0,4},{4,0},{8,12},{12,8},{16,20},{20,16},{24,28},{28,24},{32,36},... | collective-permute-start | bytes 196616 | tf_op jit(solution)/shard_map/ppermute | solution.py:741
  61.0 5.7 %collective-permute-start.15 = (f32[8,768]{1,0:T(8,128)S(1)}, f32[8,768]{1,0:T(8,128)S(1)}, u32[]{:S(2)}, u32[]{:S(2)}) collective-permute-start(f32[8,768]{1,0:T(8,128)S(1)} %get-tuple-element.54.after_ref.sum_ref), channel_id=1, source_target_pairs={{0,3},{1,0},{2,1},{3,2},{4,7},{5,4},{6,5},{7,6},{8,11},{9,8},{10,9... | collective-permute-start | bytes 73736 | tf_op jit(solution)/shard_map/ppermute | solution.py:769
  63.5 4.2 %collective-permute-start.14 = (f32[8,768]{1,0:T(8,128)S(1)}, f32[8,768]{1,0:T(8,128)S(1)}, u32[]{:S(2)}, u32[]{:S(2)}) collective-permute-start(f32[8,768]{1,0:T(8,128)S(1)} %get-tuple-element.54.after_ref.sum_ref), channel_id=1, source_target_pairs={{0,2},{1,3},{2,0},{3,1},{4,6},{5,7},{6,4},{7,5},{8,10},{9,11},{10,... | collective-permute-start | bytes 73736 | tf_op jit(solution)/shard_map/ppermute | solution.py:769
  64.0 3.9 %collective-permute-start.13 = (f32[8,768]{1,0:T(8,128)S(1)}, f32[8,768]{1,0:T(8,128)S(1)}, u32[]{:S(2)}, u32[]{:S(2)}) collective-permute-start(f32[8,768]{1,0:T(8,128)S(1)} %get-tuple-element.54.after_ref.sum_ref), channel_id=1, source_target_pairs={{0,1},{1,2},{2,3},{3,0},{4,5},{5,6},{6,7},{7,4},{8,9},{9,10},{10,1... | collective-permute-start | bytes 73736 | tf_op jit(solution)/shard_map/ppermute | solution.py:769
  64.7 3.3 %copy-start.9 = (f32[2048]{0:T(1024)S(1)}, f32[2048]{0:T(1024)}, u32[]{:S(2)}) copy-start(f32[2048]{0:T(1024)} %param.16) | copy-start | bytes 24580

commit v3 on v2

v3 whole, which is shorter than its diff:
```python
import functools
import jax
import jax.numpy as jnp
from jax import lax
from jax.experimental import pallas as pl
from jax.experimental.pallas import tpu as pltpu
from jax.sharding import PartitionSpec as P

P_SIZE = 128
N = 128
Q = 256
F32 = jnp.float32
BF16 = jnp.bfloat16
Y_SIZE = 4
Z_SIZE = 8
NT = (((1,), (1,)), ((), ()))


def seq_index(y, z, core):
    return ((y % Y_SIZE) * Z_SIZE + (z % Z_SIZE)) * 2 + core


def seq_pairs(move):
    pairs = []
    for y in range(Y_SIZE):
        for z in range(Z_SIZE):
            for core in range(2):
                pairs.append((seq_index(y, z, core), seq_index(*move(y, z, core))))
    return pairs


CORE_SWAP = seq_pairs(lambda y, z, core: (y, z, 1 - core))
NEXT_ROW = seq_pairs(lambda y, z, core: (y + 1, z, core))
AROUND = [
    seq_pairs(lambda y, z, core, step=step: (y, z + (step if core == 0 else -step), core))
    for step in range(1, 5)
]


def group_bounds(doc_ref, start):
    last = start + (Q - 1)
    doc_first = jnp.int32(0)
    next_end = jnp.int32(2147483647)
    end = jnp.int32(0)
    for k in range(doc_ref.shape[0]):
        end = end + doc_ref[k]
        doc_first = jnp.where(end <= last, end, doc_first)
        next_end = jnp.minimum(next_end, jnp.where(end >= start, end, 2147483647))
    return doc_first, next_end


def split3(values):
    high = values.astype(BF16)
    rest = values - high.astype(F32)
    mid = rest.astype(BF16)
    low = (rest - mid.astype(F32)).astype(BF16)
    return high, mid, low


def core_index():
    return lax.axis_index("seq") & 1


def ring_index():
    return (lax.axis_index("seq") // 2) & (Z_SIZE - 1)


def chip_at(core, step):
    return (ring_index() + jnp.where(core == 0, step, Z_SIZE - step)) & (Z_SIZE - 1)


def head_of(slot, heads):
    half = heads // 2
    core = core_index() if slot < half else 1 - core_index()
    place = slot % half
    if place < 6:
        return chip_at(core, place // 2 + 1) + half * (place % 2)
    return core * half + chip_at(core, 4 if place == 6 else 0)


def head_spans(heads):
    return [
        pl.ds(pl.multiple_of(head_of(slot, heads) * P_SIZE, P_SIZE), P_SIZE)
        for slot in range(heads)
    ]


def slot_rows(rows_ref):
    heads = rows_ref.shape[0]
    return jnp.concatenate(
        [rows_ref[pl.ds(head_of(slot, heads), 1), :] for slot in range(heads)], axis=0
    )


def stacked_groups(rows):
    groups = rows.shape[1] // Q
    return jnp.concatenate([rows[:, g * Q : (g + 1) * Q] for g in range(groups)], axis=0)


def column_logs(step, rate_ref, heads):
    head_rows = lax.rem(lax.broadcasted_iota(jnp.int32, step.shape, 0), heads)
    rates = jnp.zeros_like(step)
    for slot in range(heads):
        rates = jnp.where(head_rows == slot, -rate_ref[head_of(slot, heads)], rates)
    rows = lax.broadcasted_iota(jnp.int32, (Q, Q), 0)
    cols = lax.broadcasted_iota(jnp.int32, (Q, Q), 1)
    lower = jnp.where(cols <= rows, 1.0, 0.0).astype(BF16)
    return sum(
        lax.dot_general(lower, part, NT, preferred_element_type=F32)
        for part in split3(rates * step)
    )


def head_columns(values, head):
    return jnp.broadcast_to(values[:, head : head + 1], (values.shape[0], P_SIZE))


def scaled_pair(columns, scale, slot):
    parts = [
        (columns[part].astype(F32) * head_columns(scale, slot + part)).astype(BF16)
        for part in range(2)
    ]
    return jnp.concatenate(parts, axis=1)


def half_states(groups, first_slot, x_ref, scale_ref, tail_of, stats_ref, state_ref, ready):
    half = state_ref.shape[0]
    spans = head_spans(2 * half)
    for group in range(groups):
        final = stats_ref[group : group + 1, :]
        passing = stats_ref[8 + group : 9 + group, :]
        tail_b = tail_of(group)
        ready(group)
        block = slice(group * Q, (group + 1) * Q)
        scale = scale_ref[:, group * 2 * half : (group + 1) * 2 * half]
        for pair in range(half // 2):
            slot = first_slot + 2 * pair
            columns = [x_ref[block, spans[slot + part]] for part in range(2)]
            scaled = scaled_pair(columns, scale, slot)
            product = jnp.dot(tail_b, scaled, preferred_element_type=F32)
            for part in range(2):
                lane = slice(slot + part, slot + part + 1)
                index = 2 * pair + part
                state = product[:, part * P_SIZE : (part + 1) * P_SIZE] * final[:, lane]
                if group > 0:
                    state = state + state_ref[index, 0:N, :] * passing[:, lane]
                state_ref[index, 0:N, :] = state
    reach = stats_ref[16 + groups : 17 + groups, :]
    for index in range(half):
        lane = slice(first_slot + index, first_slot + index + 1)
        state_ref[index, N : N + 8, :] = jnp.broadcast_to(reach[:, lane], (8, P_SIZE))


def away_states_kernel(
    heads,
    groups,
    doc_hbm,
    rate_hbm,
    step_hbm,
    b_hbm,
    x_hbm,
    state_ref,
    stats_ref,
    scale_ref,
    tail_ref,
    logs_ref,
    x_ref,
    doc_ref,
    rate_ref,
    step_ref,
    b_ref,
    small_sems,
    wide_sems,
):
    half = heads // 2
    small = [
        pltpu.make_async_copy(src, dst, small_sems.at[i])
        for i, (src, dst) in enumerate(
            ((step_hbm, step_ref), (rate_hbm, rate_ref), (doc_hbm, doc_ref), (b_hbm, b_ref))
        )
    ]
    wide = [
        pltpu.make_async_copy(
            x_hbm.at[pl.ds(group * Q, Q), :],
            x_ref.at[pl.ds(group * Q, Q), :],
            wide_sems.at[group],
        )
        for group in range(groups)
    ]
    for copy in small + wide:
        copy.start()
    for copy in small:
        copy.wait()
    stats_ref[...] = jnp.zeros_like(stats_ref)
    base = lax.axis_index("seq") * (groups * Q)
    reach = jnp.ones((1, heads), F32)
    stats_ref[16:17, 0:heads] = reach
    step = stacked_groups(slot_rows(step_ref))
    logs = column_logs(step, rate_ref, heads)
    logs_ref[...] = logs
    scale_ref[...] = jnp.exp(-logs) * step.T
    finals = jnp.exp(logs[Q - 1 : Q, :])
    for group in range(groups):
        start = base + group * Q
        doc_first, next_end = group_bounds(doc_ref, start)
        final = finals[:, group * heads : (group + 1) * heads]
        passing = jnp.where(start + (Q - 1) < next_end, final, 0.0)
        positions = lax.broadcasted_iota(jnp.int32, (N, Q), 1) + start
        b_rows = b_ref[group * Q : (group + 1) * Q, :].astype(F32).T
        tail_ref[group] = jnp.where(positions >= doc_first, b_rows, 0.0).astype(BF16)
        reach = reach * passing
        stats_ref[group : group + 1, 0:heads] = final
        stats_ref[8 + group : 9 + group, 0:heads] = passing
        stats_ref[17 + group : 18 + group, 0:heads] = reach

    half_states(
        groups,
        half,
        x_ref,
        scale_ref,
        lambda group: tail_ref[group],
        stats_ref,
        state_ref,
        lambda group: wide[group].wait(),
    )


def own_states_kernel(heads, groups, stats_ref, scale_ref, tail_ref, x_ref, state_ref):
    half_states(
        groups,
        0,
        x_ref,
        scale_ref,
        lambda group: tail_ref[group],
        stats_ref,
        state_ref,
        lambda group: None,
    )


def half_inside(
    heads,
    groups,
    first_slot,
    skip_ref,
    stats_ref,
    scale_ref,
    tail_ref,
    decay_ref,
    masked_ref,
    x_ref,
    gate_ref,
    u_ref,
    v_ref,
    before_ref,
):
    half = heads // 2
    spans = head_spans(heads)
    skips = [skip_ref[head_of(first_slot + place, heads)] for place in range(half)]
    for group in range(groups):
        block = slice(group * Q, (group + 1) * Q)
        lanes = slice(group * heads, (group + 1) * heads)
        scale = scale_ref[:, lanes]
        decay = decay_ref[:, lanes]
        final = stats_ref[group : group + 1, :]
        passing = stats_ref[8 + group : 9 + group, :]
        masked = masked_ref[group]
        for pair in range(half // 2):
            slot = first_slot + 2 * pair
            columns = [x_ref[block, spans[slot + part]] for part in range(2)]
            scaled = scaled_pair(columns, scale, slot)
            product = jnp.dot(masked, scaled, preferred_element_type=F32)
            if group < groups - 1:
                states = jnp.dot(tail_ref[group], scaled, preferred_element_type=F32)
            for part in range(2):
                here = slice(part * P_SIZE, (part + 1) * P_SIZE)
                place = 2 * pair + part
                span = slice(place * P_SIZE, (place + 1) * P_SIZE)
                gate = 0.5 * gate_ref[block, spans[slot + part]].astype(F32)
                active = gate + gate * jnp.tanh(gate)
                carry = head_columns(decay, slot + part) * active
                direct = skips[place] * columns[part].astype(F32)
                u_ref[block, span] = product[:, here] * carry + direct * active
                v_ref[block, span] = carry
                if group < groups - 1:
                    lane = slice(slot + part, slot + part + 1)
                    state = states[:, here] * final[:, lane]
                    if group > 0:
                        state = state + before_ref[group - 1, place] * passing[:, lane]
                    before_ref[group, place] = state


def away_inside_kernel(
    heads,
    groups,
    doc_ref,
    skip_ref,
    logs_ref,
    b_ref,
    c_ref,
    stats_ref,
    scale_ref,
    tail_ref,
    x_ref,
    gate_ref,
    after_ref,
    u_ref,
    v_ref,
    before_ref,
    entry_c_ref,
    decay_ref,
    masked_ref,
    token_ref,
):
    base = lax.axis_index("seq") * (groups * Q)
    rows = lax.broadcasted_iota(jnp.int32, (Q, Q), 0)
    cols = lax.broadcasted_iota(jnp.int32, (Q, Q), 1)
    decay_ref[...] = jnp.exp(logs_ref[...])
    for group in range(groups):
        start = base + group * Q
        block = slice(group * Q, (group + 1) * Q)
        _, next_end = group_bounds(doc_ref, start)
        positions = lax.broadcasted_iota(jnp.int32, (Q, N), 0) + start
        entry_c = jnp.where(positions < next_end, c_ref[block, :].astype(F32), 0.0)
        entry_c_ref[block, :] = entry_c.astype(BF16)
        first = jnp.zeros((Q, Q), jnp.int32)
        end = jnp.int32(0)
        for k in range(doc_ref.shape[0]):
            end = end + doc_ref[k]
            first = jnp.where(end - start <= rows, end - start, first)
        scores = lax.dot_general(c_ref[block, :], b_ref[block, :], NT, preferred_element_type=F32)
        masked = jnp.where((cols <= rows) & (cols >= first), scores, 0.0)
        masked_ref[group] = masked.astype(BF16)
    half_inside(
        heads,
        groups,
        heads // 2,
        skip_ref,
        stats_ref,
        scale_ref,
        tail_ref,
        decay_ref,
        masked_ref,
        x_ref,
        gate_ref,
        u_ref,
        v_ref,
        before_ref,
    )
    token_ref[...] = jnp.zeros_like(token_ref)


def own_inside_kernel(
    heads,
    groups,
    skip_ref,
    stats_ref,
    scale_ref,
    tail_ref,
    decay_ref,
    masked_ref,
    x_ref,
    gate_ref,
    after_ref,
    u_ref,
    v_ref,
    before_ref,
    token_ref,
):
    half_inside(
        heads,
        groups,
        0,
        skip_ref,
        stats_ref,
        scale_ref,
        tail_ref,
        decay_ref,
        masked_ref,
        x_ref,
        gate_ref,
        u_ref,
        v_ref,
        before_ref,
    )
    token_ref[...] = jnp.zeros_like(token_ref)


def join_cores_kernel(
    own_ref, other_ref, step1_ref, step2_ref, step3_ref, step4_ref, here_ref, token_ref
):
    core = core_index()
    places = [(ref, part) for ref in (step1_ref, step2_ref, step3_ref) for part in range(2)]
    for slot, (joined_ref, part) in enumerate(places + [(step4_ref, 0), (here_ref, 0)]):
        own, other = own_ref[slot], other_ref[slot]
        earlier = jnp.where(core == 0, own, other)
        later = jnp.where(core == 0, other, own)
        later_pass = later[N : N + 1, :]
        joined_ref[part, 0:N, :] = later_pass * earlier[0:N, :] + later[0:N, :]
        joined_ref[part, N : N + 8, :] = later_pass * earlier[N : N + 8, :]
    token_ref[...] = jnp.zeros_like(token_ref)


def pack_kernel(step1_ref, step2_ref, step3_ref, step4_ref, last_ref, after_ref, packed_ref):
    for step, ref in enumerate((step1_ref, step2_ref, step3_ref)):
        packed_ref[2 * step] = ref[0]
        packed_ref[2 * step + 1] = ref[1]
    packed_ref[6] = step4_ref[0]
    packed_ref[7] = last_ref[0]


def row_total_kernel(packed_ref, swapped_ref, after_ref, total_ref, parts_ref):
    core = core_index()
    for ref, arrived_on in ((packed_ref, core), (swapped_ref, 1 - core)):
        for step in (1, 2, 3):
            chip = chip_at(1 - arrived_on, step)
            parts_ref[0, chip] = ref[2 * step - 2]
            parts_ref[1, chip] = ref[2 * step - 1]
        parts_ref[arrived_on, chip_at(core, 4)] = ref[6]
        parts_ref[arrived_on, chip_at(core, 0)] = ref[7]
    for which in range(2):
        total = parts_ref[which, 0, 0:N, :]
        for chip in range(1, Z_SIZE):
            total = parts_ref[which, chip, N : N + 1, :] * total + parts_ref[which, chip, 0:N, :]
        total_ref[which] = total


def entering_kernel(
    parts_ref,
    carried_ref,
    step1_ref,
    step2_ref,
    step3_ref,
    step4_ref,
    here_ref,
    token_ref,
    all_ref,
):
    row = lax.axis_index("seq") // (2 * Z_SIZE)
    core = core_index()
    for which in range(2):
        state = jnp.where(row > 0, carried_ref[which], 0.0)
        for chip in range(Z_SIZE):
            all_ref[which, chip] = state
            if chip < Z_SIZE - 1:
                state = parts_ref[which, chip, N : N + 1, :] * state + parts_ref[which, chip, 0:N, :]
    for step, pair_ref in ((1, step1_ref), (2, step2_ref), (3, step3_ref)):
        chip = chip_at(core, step)
        pair_ref[0] = all_ref[0, chip]
        pair_ref[1] = all_ref[1, chip]
    step4_ref[0] = all_ref[core, chip_at(core, 4)]
    here_ref[0] = all_ref[core, chip_at(core, 0)]
    here_ref[1] = all_ref[1 - core, chip_at(core, 0)]
    token_ref[...] = jnp.zeros_like(token_ref)


def outputs_kernel(
    heads,
    groups,
    here_ref,
    packed_ref,
    swapped_ref,
    own_other_ref,
    away_other_ref,
    own_before_ref,
    away_before_ref,
    stats_ref,
    c_ref,
    own_u_ref,
    own_v_ref,
    away_u_ref,
    away_v_ref,
    own_gated_ref,
    away_gated_ref,
    squares_ref,
    first_ref,
):
    core = core_index()
    half = heads // 2
    for side, earlier_ref in enumerate((own_other_ref, away_other_ref)):
        for place in range(half):
            if place < 6:
                chip_state = (swapped_ref, packed_ref)[side][place]
            elif place == 6:
                chip_state = (packed_ref, swapped_ref)[side][place]
            else:
                chip_state = here_ref[side]
            joined = earlier_ref[place, N : N + 1, :] * chip_state + earlier_ref[place, 0:N, :]
            first_ref[side * half + place] = jnp.where(core == 0, chip_state, joined)

    for group in range(groups):
        block = slice(group * Q, (group + 1) * Q)
        reach = stats_ref[16 + group : 17 + group, :]
        squares = jnp.zeros((Q, P_SIZE), F32)
        for side, (u_ref, v_ref, before_ref, gated_ref) in enumerate(
            (
                (own_u_ref, own_v_ref, own_before_ref, own_gated_ref),
                (away_u_ref, away_v_ref, away_before_ref, away_gated_ref),
            )
        ):
            for pair in range(half // 2):
                both = []
                for index in (2 * pair, 2 * pair + 1):
                    slot = side * half + index
                    state = first_ref[slot]
                    if group > 0:
                        state = state * reach[:, slot : slot + 1] + before_ref[group - 1, index]
                    both.append(state.astype(BF16))
                carried = jnp.dot(
                    c_ref[block, :], jnp.concatenate(both, axis=1), preferred_element_type=F32
                )
                span = slice(2 * pair * P_SIZE, 2 * (pair + 1) * P_SIZE)
                gated = u_ref[block, span] + v_ref[block, span] * carried
                gated_ref[block, span] = gated
                square = gated * gated
                squares = squares + square[:, 0:P_SIZE] + square[:, P_SIZE:]
        squares_ref[:, block] = jnp.broadcast_to(
            jnp.sum(squares.T, axis=0, keepdims=True), (8, Q)
        )


def write_states_kernel(
    heads,
    groups,
    first_ref,
    own_before_ref,
    away_before_ref,
    stats_ref,
    after_ref,
    states_hbm,
    token_ref,
    states_ref,
    sems,
):
    half = heads // 2
    copies = []
    places = [head_of(slot, heads) for slot in range(heads)]
    for group in range(groups):
        reach = stats_ref[16 + group : 17 + group, :]
        for side, before_ref in enumerate((own_before_ref, away_before_ref)):
            for index in range(half):
                slot = side * half + index
                state = first_ref[slot]
                if group > 0:
                    state = state * reach[:, slot : slot + 1] + before_ref[group - 1, index]
                states_ref[group, slot] = state.T
                copy = pltpu.make_async_copy(
                    states_ref.at[group, slot],
                    states_hbm.at[group, places[slot]],
                    sems.at[group, slot],
                )
                copy.start()
                copies.append(copy)
    for copy in copies:
        copy.wait()
    token_ref[...] = jnp.zeros_like(token_ref)


SCALE_ROWS = 128


def scale_kernel(
    inner, heads, own_ref, away_ref, gain_ref, sum_ref, a_ref, b_ref, c_ref, after_ref, out_hbm, out_ref, sems
):
    mean = (sum_ref[...] + a_ref[...] + b_ref[...] + c_ref[...]) * (1.0 / inner)
    scale = lax.rsqrt(mean + 1e-05)
    half = heads // 2
    spans = head_spans(heads)
    copies = []
    for chunk in range(own_ref.shape[0] // SCALE_ROWS):
        block = slice(chunk * SCALE_ROWS, (chunk + 1) * SCALE_ROWS)
        column = jnp.broadcast_to(scale[0:1, block], (P_SIZE, SCALE_ROWS)).T
        for slot in range(heads):
            gated_ref = own_ref if slot < half else away_ref
            span = slice(slot % half * P_SIZE, (slot % half + 1) * P_SIZE)
            place = spans[slot]
            out_ref[block, place] = (
                gated_ref[block, span] * column * gain_ref[:, place]
            ).astype(BF16)
        rows = pl.ds(chunk * SCALE_ROWS, SCALE_ROWS)
        copy = pltpu.make_async_copy(
            out_ref.at[rows, :], out_hbm.at[rows, :], sems.at[chunk]
        )
        copy.start()
        copies.append(copy)
    for copy in copies:
        copy.wait()


def cost(flops, bytes_accessed):
    return pl.CostEstimate(flops=flops, bytes_accessed=bytes_accessed, transcendentals=0)


def params(mebibytes):
    return pltpu.CompilerParams(vmem_limit_bytes=mebibytes * 1024 * 1024)


def local(
    head_input,
    gate_input,
    step_size,
    input_proj,
    output_proj,
    decay_rate,
    skip_gain,
    norm_gain,
    doc_lengths,
):
    row_count, width = head_input.shape
    heads = step_size.shape[1]
    half = heads // 2
    groups = row_count // Q
    sds = jax.ShapeDtypeStruct
    step_rows = step_size.T
    gain = norm_gain.reshape(1, width)
    smem = pl.BlockSpec(memory_space=pltpu.SMEM)
    vmem = pl.BlockSpec(memory_space=pltpu.VMEM)
    hbm = pl.BlockSpec(memory_space=pltpu.HBM)
    anywhere = pl.BlockSpec(memory_space=pl.ANY)
    dma = pltpu.SemaphoreType.DMA

    token = sds((8, P_SIZE), F32)
    half_state = sds((half, N + 8, P_SIZE), F32)
    half_before = sds((groups - 1, half, N, P_SIZE), F32)
    half_wide = sds((row_count, width // 2), F32)

    def in_hbm(*arrays):
        return [pltpu.with_memory_space_constraint(array, pltpu.HBM) for array in arrays]

    pair_state = sds((2, N + 8, P_SIZE), F32)
    one_state = sds((1, N + 8, P_SIZE), F32)
    pair_first = sds((2, N, P_SIZE), F32)
    one_first = sds((1, N, P_SIZE), F32)
    lanes = groups * heads

    away_state, stats, scale, tail, logs, input_copy = pl.pallas_call(
        functools.partial(away_states_kernel, heads, groups),
        in_specs=[hbm] * 5,
        out_specs=[vmem] * 6,
        out_shape=[
            half_state,
            sds((24, P_SIZE), F32),
            sds((Q, lanes), F32),
            sds((groups, N, Q), BF16),
            sds((Q, lanes), F32),
            sds((row_count, width), BF16),
        ],
        scratch_shapes=[
            pltpu.SMEM(doc_lengths.shape, jnp.int32),
            pltpu.SMEM(decay_rate.shape, F32),
            pltpu.VMEM((heads, row_count), F32),
            pltpu.VMEM((row_count, N), BF16),
            dma((4,)),
            dma((groups,)),
        ],
        compiler_params=params(16),
        cost_estimate=cost(200_000_000, 4_000_000),
        name="away_states",
    )(*in_hbm(doc_lengths, decay_rate, step_rows, input_proj, head_input))
    own_other = lax.ppermute(away_state, "seq", CORE_SWAP)

    own_state = pl.pallas_call(
        functools.partial(own_states_kernel, heads, groups),
        in_specs=[vmem] * 4,
        out_specs=vmem,
        out_shape=half_state,
        compiler_params=params(16),
        cost_estimate=cost(2_000_000_000, 4_000_000),
        name="own_states",
    )(stats, scale, tail, input_copy)

    *joined, joined_token = pl.pallas_call(
        join_cores_kernel,
        out_shape=[pair_state] * 3 + [one_state] * 2 + [token],
        compiler_params=params(8),
        cost_estimate=cost(1_000_000, 1_700_000),
        name="join_cores",
    )(own_state, own_other)
    here_part = joined.pop()
    arrived = [lax.ppermute(sent, "seq", pairs) for sent, pairs in zip(joined, AROUND)]
    away_other = lax.ppermute(own_state, "seq", CORE_SWAP)

    away_u, away_v, away_before, entry_c, decay, masked, away_token = pl.pallas_call(
        functools.partial(away_inside_kernel, heads, groups),
        in_specs=[smem] * 2 + [vmem] * 8 + [anywhere],
        out_specs=[vmem] * 7,
        out_shape=[half_wide] * 2
        + [
            half_before,
            sds((row_count, N), BF16),
            sds((Q, lanes), F32),
            sds((groups, Q, Q), BF16),
            token,
        ],
        compiler_params=params(24),
        cost_estimate=cost(8_000_000_000, 20_000_000),
        name="away_inside",
    )(
        doc_lengths,
        skip_gain,
        logs,
        input_proj,
        output_proj,
        stats,
        scale,
        tail,
        input_copy,
        gate_input,
        joined_token,
    )

    def pack(states, last, after, name):
        return pl.pallas_call(
            pack_kernel,
            in_specs=[vmem] * 5 + [anywhere],
            out_specs=vmem,
            out_shape=sds((8,) + last.shape[1:], F32),
            compiler_params=params(8),
            cost_estimate=cost(300_000, 1_100_000),
            name=name,
        )(*states, last, after)

    packed_parts = pack(arrived, here_part, away_token, "pack_parts")
    swapped_parts = lax.ppermute(packed_parts, "seq", CORE_SWAP)
    total, parts = pl.pallas_call(
        row_total_kernel,
        in_specs=[vmem, vmem, anywhere],
        out_shape=[pair_first, sds((2, Z_SIZE, N + 8, P_SIZE), F32)],
        compiler_params=params(8),
        cost_estimate=cost(300_000, 600_000),
        name="row_total",
    )(packed_parts, swapped_parts, away_other)
    carried = lax.ppermute(total, "seq", NEXT_ROW)
    *steps, here, entering_token = pl.pallas_call(
        entering_kernel,
        out_shape=[pair_first] * 3 + [one_first, pair_first, token],
        scratch_shapes=[pltpu.VMEM((2, Z_SIZE, N, P_SIZE), F32)],
        compiler_params=params(8),
        cost_estimate=cost(1_000_000, 1_100_000),
        name="entering",
    )(parts, carried)
    returned = [lax.ppermute(sent, "seq", pairs) for sent, pairs in zip(steps, AROUND)]

    own_u, own_v, own_before, own_token = pl.pallas_call(
        functools.partial(own_inside_kernel, heads, groups),
        in_specs=[smem] + [vmem] * 7 + [anywhere],
        out_specs=[vmem] * 4,
        out_shape=[half_wide] * 2 + [half_before, token],
        compiler_params=params(20),
        cost_estimate=cost(8_000_000_000, 20_000_000),
        name="own_inside",
    )(skip_gain, stats, scale, tail, decay, masked, input_copy, gate_input, entering_token)
    packed = pack(returned, here, own_token, "pack_states")
    swapped = lax.ppermute(packed, "seq", CORE_SWAP)

    own_gated, away_gated, squares, first = pl.pallas_call(
        functools.partial(outputs_kernel, heads, groups),
        in_specs=[vmem] * 13,
        out_specs=[vmem] * 4,
        out_shape=[half_wide] * 2 + [sds((8, row_count), F32), sds((heads, N, P_SIZE), F32)],
        compiler_params=params(30),
        cost_estimate=cost(2_000_000, 9_000),
        name="outputs",
    )(
        here,
        packed,
        swapped,
        own_other,
        away_other,
        own_before,
        away_before,
        stats,
        entry_c,
        own_u,
        own_v,
        away_u,
        away_v,
    )

    tp_size = 4
    sums = [
        lax.ppermute(squares, "tp", [(i, (i + k) % tp_size) for i in range(tp_size)])
        for k in range(1, tp_size)
    ]
    group_states, states_token = pl.pallas_call(
        functools.partial(write_states_kernel, heads, groups),
        in_specs=[vmem] * 4 + [anywhere],
        out_specs=[hbm, vmem],
        out_shape=[sds((groups, heads, P_SIZE, N), F32), token],
        scratch_shapes=[
            pltpu.VMEM((groups, heads, P_SIZE, N), F32),
            dma((groups, heads)),
        ],
        compiler_params=params(16),
        cost_estimate=cost(4_000_000_000, 9_000_000),
        name="write_states",
    )(first, own_before, away_before, stats, squares)
    mixed_out = pl.pallas_call(
        functools.partial(scale_kernel, width * tp_size, heads),
        in_specs=[vmem] * 7 + [anywhere],
        out_specs=hbm,
        out_shape=sds((row_count, width), BF16),
        scratch_shapes=[
            pltpu.VMEM((row_count, width), BF16),
            dma((row_count // SCALE_ROWS,)),
        ],
        compiler_params=params(16),
        cost_estimate=cost(5_000_000, 6_500_000),
        name="scale",
    )(own_gated, away_gated, gain, squares, *sums, states_token)
    return (mixed_out, group_states)


def solution(mesh):
    return jax.shard_map(
        local,
        mesh=mesh,
        in_specs=(
            P("seq", "tp"),
            P("seq", "tp"),
            P("seq", "tp"),
            P("seq", None),
            P("seq", None),
            P("tp"),
            P("tp"),
            P("tp"),
            P(),
        ),
        out_specs=(P("seq", "tp"), P("seq", "tp", None, None)),
        check_vma=False,
    )
```

time: 71.4 us -> 70.2 us (0.983); the launches traced: 70.2 us -> 70.1 us
  waiting for transfers between devices: 13.9 us -> 19.2 us
  Pallas kernels: 22.9 us -> 19.4 us
  starting transfers between devices: 32.3 us -> 30.5 us
    ppermute x4 -> x8, starting transfers between devices: 5.79 us -> 19.5 us  [local(): lax.ppermute(sent, 'seq', pairs)]
    ppermute x4 -> x8, waiting for transfers between devices: 0.37 us -> 9.5 us  [local(): lax.ppermute(sent, 'seq', pairs)]
    ppermute x6 -> x2, starting transfers between devices: 11.1 us -> 2.48 us  [the longest x1 2.36 us: local(): swapped = lax.ppermute(packed, 'seq', CORE_SWAP)]
    all_to_all x1 -> x0, waiting for transfers between devices: 7.07 us -> none  [local(): lax.all_to_all(joined, 'seq', split_axis=0, concat_axis=0, axis_index_gro...]
    all_to_all x1 -> x0, starting transfers between devices: 6.46 us -> none  [local(): lax.all_to_all(joined, 'seq', split_axis=0, concat_axis=0, axis_index_gro...]
    pallas_call x4 -> x7, Pallas kernels: 12.2 us -> 7.9 us  [the longest x1 4.06 us: local(): pl.pallas_call(functools.partial(away_inside_kernel, heads, groups), in_s...]
    ppermute x1, waiting for transfers between devices: 0.74 us -> 5.01 us  [local(): carried = lax.ppermute(total, 'seq', NEXT_ROW)]
    ppermute x6 -> x2, waiting for transfers between devices: 4.11 us -> 3.46 us  [the longest x1 1.93 us: local(): swapped_parts = lax.ppermute(packed_parts, 'seq', CORE_SWAP)]
  transfers between devices with their start and end apart: 17 -> 16, of which waited for: 8 -> 10; matrix products, arithmetic and copies ran while one was open for 0% -> 0% of each run, Pallas kernels for 20% -> 16%
where the time goes in v3:
time: 70.2 us; the launch traced here: 70.1 us
  starting transfers between devices  30.5 us (43%)
  Pallas kernels  19.4 us (28%)
  waiting for transfers between devices  19.2 us (27%)
  between operations  0.92 us (1%)
    ppermute x8, starting transfers between devices, local(): lax.ppermute(sent, 'seq', pairs)  19.5 us
    ppermute x8, waiting for transfers between devices, local(): lax.ppermute(sent, 'seq', pairs)  9.5 us
    ppermute x1, waiting for transfers between devices, local(): carried = lax.ppermute(total, 'seq', NEXT_ROW)  5.01 us
    pallas_call x1, Pallas kernels, local(): pl.pallas_call(functools.partial(away_inside_kernel, heads, groups), in_s...  4.06 us
    pallas_call x1, Pallas kernels, local(): pl.pallas_call(functools.partial(away_states_kernel, heads, groups), in_s...  3.95 us
    ppermute x3, starting transfers between devices, local(): lax.ppermute(squares, 'tp', [(i, (i + k) % tp_size) for i in range(tp_siz...  3.69 us
    pallas_call x1, Pallas kernels, local(): pl.pallas_call(functools.partial(own_inside_kernel, heads, groups), in_sp...  3.38 us
    ppermute x1, starting transfers between devices, local(): own_other = lax.ppermute(away_state, 'seq', CORE_SWAP)  3.33 us
  transfers between devices with their start and end apart: 16, of which 10 were waited for; matrix products, arithmetic and copies ran while one was open for 0% of the time, Pallas kernels for 16%

profile of v3, /device:TPU:1, one launch (start us, length us, event | category | flops | bytes accessed | tf_op | source)
XLA Modules:
  0.0 70.1 jit_solution(9988363982900078113)
XLA Ops:
  0.6 4.0 %away_states.1 = (f32[8,136,128]{2,1,0:T(8,128)S(1)}, f32[24,128]{1,0:T(8,128)S(1)}, f32[256,48]{1,0:T(8,128)S(1)}, bf16[3,128,256]{2,1,0:T(8,128)(2,1)S(1)}, f3...) custom-call(s32[16]{0:T(128)} %doc_ref.1, f32[16]{0:T(128)} %rate_hbm.1, f32[16,768]{1,0:T(8,128)} %bitcast.3, ...), custom_call_target="tpu_custom_call" | custom-call | flops 200000000 | bytes 4000000 | tf_op jit(solution)/shard_map/away_states/pallas_call | solution.py:636
  4.6 3.3 %collective-permute-start = (f32[8,136,128]{2,1,0:T(8,128)S(1)}, f32[8,136,128]{2,1,0:T(8,128)S(1)}, u32[]{:S(2)}, u32[]{:S(2)}) collective-permute-start(f32[8,136,128]{2,1,0:T(8,128)S(1)} %get-tuple-element.43), channel_id=1, source_target_pairs={{0,4},{4,0},{8,12},{12,8},{16,20},{20,16},{24,28},{28,24},{32,36},... | collective-permute-start | bytes 1671176 | tf_op jit(solution)/shard_map/ppermute | solution.py:660
  7.9 0.0 copy-start.5
  7.9 1.3 %own_states.1.own_ref = f32[8,136,128]{2,1,0:T(8,128)S(1)} custom-call(f32[24,128]{1,0:T(8,128)S(1)} %get-tuple-element.39.stats_ref, f32[256,48]{1,0:T(8,128)S(1)} %get-tuple-element.40.scale_ref, bf16[3,128,256]{2,1,0:T(8,128)(2,1)S(1)} %get-tuple-element.41.tail_ref, bf16[768,2048]{1,0:T(8,128)(2,1)S(1)} %get-tuple-element.42.x_ref), custom_call_target="tpu_custom_call" | custom-call | flops 2000000000 | bytes 4000000 | tf_op jit(solution)/shard_map/own_states/pallas_call | solution.py:662
  9.3 0.1 collective-permute-start.6
  9.4 0.1 collective-permute-done.other_ref.own_other_ref
  9.5 0.1 join_cores.1
  9.6 5.3 %collective-permute-start.4 = (f32[1,136,128]{2,1,0:T(8,128)S(1)}, f32[1,136,128]{2,1,0:T(8,128)S(1)}, u32[]{:S(2)}, u32[]{:S(2)}) collective-permute-start(f32[1,136,128]{2,1,0:T(8,128)S(1)} %get-tuple-element.47), channel_id=1, source_target_pairs={{0,32},{4,36},{8,40},{12,44},{16,48},{20,52},{24,56},{28,60},{32,0... | collective-permute-start | bytes 208904 | tf_op jit(solution)/shard_map/ppermute | solution.py:680
  14.8 0.0 collective-permute-start.1
  14.8 0.0 collective-permute-start.2
  14.9 4.8 %collective-permute-start.3 = (f32[2,136,128]{2,1,0:T(8,128)S(1)}, f32[2,136,128]{2,1,0:T(8,128)S(1)}, u32[]{:S(2)}, u32[]{:S(2)}) collective-permute-start(f32[2,136,128]{2,1,0:T(8,128)S(1)} %get-tuple-element.46), channel_id=1, source_target_pairs={{0,24},{4,44},{8,32},{12,52},{16,40},{20,60},{24,48},{28,4},{32,56... | collective-permute-start | bytes 417800 | tf_op jit(solution)/shard_map/ppermute | solution.py:680
  19.6 0.0 copy-done
  19.6 0.0 copy-done.2
  19.6 0.0 copy-done.3
  19.6 0.0 copy-done.4
  19.6 4.1 %away_inside.1 = (f32[768,1024]{1,0:T(8,128)S(1)}, f32[768,1024]{1,0:T(8,128)S(1)}, f32[2,8,128,128]{3,2,1,0:T(8,128)S(1)}, bf16[768,128]{1,0:T(8,128)(2,1)S(1)}...) custom-call(s32[16]{0:T(128)S(1)} %copy-done.2, f32[16]{0:T(128)S(1)} %copy-done.5, ...), custom_call_target="tpu_custom_call" | custom-call | flops 8000000000 | bytes 20000000 | tf_op jit(solution)/shard_map/away_inside/pallas_call | solution.py:683
  23.7 0.0 collective-permute-done.4.step4_ref
  23.7 0.0 collective-permute-done.1.step1_ref
  23.7 1.0 %collective-permute-done.2.step2_ref = f32[2,136,128]{2,1,0:T(8,128)S(1)} collective-permute-done((f32[2,136,128]{2,1,0:T(8,128)S(1)}, f32[2,136,128]{2,1,0:T(8,128)S(1)}, u32[]{:S(2)}, u32[]{:S(2)}) %collective-permute-start.2) | collective-permute-done | bytes 139296 | tf_op jit(solution)/shard_map/ppermute | solution.py:680
  24.8 3.4 %collective-permute-done.3.step3_ref = f32[2,136,128]{2,1,0:T(8,128)S(1)} collective-permute-done((f32[2,136,128]{2,1,0:T(8,128)S(1)}, f32[2,136,128]{2,1,0:T(8,128)S(1)}, u32[]{:S(2)}, u32[]{:S(2)}) %collective-permute-start.3) | collective-permute-done | bytes 139296 | tf_op jit(solution)/shard_map/ppermute | solution.py:680
  28.3 0.1 collective-permute-start.5
  28.4 0.0 collective-permute-done.6.after_ref.away_other_ref
  28.4 1.9 %collective-permute-done.5.swapped_ref = f32[8,136,128]{2,1,0:T(8,128)S(1)} collective-permute-done((f32[8,136,128]{2,1,0:T(8,128)S(1)}, f32[8,136,128]{2,1,0:T(8,128)S(1)}, u32[]{:S(2)}, u32[]{:S(2)}) %collective-permute-start.5) | collective-permute-done | bytes 557088 | tf_op jit(solution)/shard_map/ppermute | solution.py:724
  30.3 0.2 row_total.1
  30.5 1.4 %collective-permute-start.7 = (f32[2,128,128]{2,1,0:T(8,128)S(1)}, f32[2,128,128]{2,1,0:T(8,128)S(1)}, u32[]{:S(2)}, u32[]{:S(2)}) collective-permute-start(f32[2,128,128]{2,1,0:T(8,128)S(1)} %get-tuple-element.53), channel_id=1, source_target_pairs={{0,64},{4,68},{8,72},{12,76},{16,80},{20,84},{24,88},{28,92},{32,9... | collective-permute-start | bytes 393224 | tf_op jit(solution)/shard_map/ppermute | solution.py:733
  31.8 5.0 %collective-permute-done.7.carried_ref = f32[2,128,128]{2,1,0:T(8,128)S(1)} collective-permute-done((f32[2,128,128]{2,1,0:T(8,128)S(1)}, f32[2,128,128]{2,1,0:T(8,128)S(1)}, u32[]{:S(2)}, u32[]{:S(2)}) %collective-permute-start.7) | collective-permute-done | bytes 131104 | tf_op jit(solution)/shard_map/ppermute | solution.py:733
  36.8 0.1 entering.1
  37.0 4.7 %collective-permute-start.11 = (f32[1,128,128]{2,1,0:T(8,128)S(1)}, f32[1,128,128]{2,1,0:T(8,128)S(1)}, u32[]{:S(2)}, u32[]{:S(2)}) collective-permute-start(f32[1,128,128]{2,1,0:T(8,128)S(1)} %get-tuple-element.58), channel_id=1, source_target_pairs={{0,32},{4,36},{8,40},{12,44},{16,48},{20,52},{24,56},{28,60},{32,0... | collective-permute-start | bytes 196616 | tf_op jit(solution)/shard_map/ppermute | solution.py:742
  41.7 0.2 collective-permute-start.8
  41.9 1.8 %collective-permute-start.9 = (f32[2,128,128]{2,1,0:T(8,128)S(1)}, f32[2,128,128]{2,1,0:T(8,128)S(1)}, u32[]{:S(2)}, u32[]{:S(2)}) collective-permute-start(f32[2,128,128]{2,1,0:T(8,128)S(1)} %get-tuple-element.56), channel_id=1, source_target_pairs={{0,16},{4,52},{8,24},{12,60},{16,32},{20,4},{24,40},{28,12},{32,48... | collective-permute-start | bytes 393224 | tf_op jit(solution)/shard_map/ppermute | solution.py:742
  43.7 2.8 %collective-permute-start.10 = (f32[2,128,128]{2,1,0:T(8,128)S(1)}, f32[2,128,128]{2,1,0:T(8,128)S(1)}, u32[]{:S(2)}, u32[]{:S(2)}) collective-permute-start(f32[2,128,128]{2,1,0:T(8,128)S(1)} %get-tuple-element.57), channel_id=1, source_target_pairs={{0,24},{4,44},{8,32},{12,52},{16,40},{20,60},{24,48},{28,4},{32,56... | collective-permute-start | bytes 393224 | tf_op jit(solution)/shard_map/ppermute | solution.py:742
  46.5 3.4 %own_inside.1 = (f32[768,1024]{1,0:T(8,128)S(1)}, f32[768,1024]{1,0:T(8,128)S(1)}, f32[2,8,128,128]{3,2,1,0:T(8,128)S(1)}, f32[8,128]{1,0:T(8,128)S(1)}) custom-call(f32[16]{0:T(128)S(1)} %copy-done.5, f32[24,128]{1,0:T(8,128)S(1)} %get-tuple-element.39.stats_ref, f32[256,48]{1,0:T(8,128)S(1)} %get-tuple-element.40.scale_ref, ...), custom_call_target="tpu_custom_call" | custom-call | flops 8000000000 | bytes 20000000 | tf_op jit(solution)/shard_map/own_inside/pallas_call | solution.py:744
  49.9 0.0 collective-permute-done.11.step4_ref
  49.9 0.0 collective-permute-done.8.step1_ref
  49.9 1.9 %collective-permute-done.9.step2_ref = f32[2,128,128]{2,1,0:T(8,128)S(1)} collective-permute-done((f32[2,128,128]{2,1,0:T(8,128)S(1)}, f32[2,128,128]{2,1,0:T(8,128)S(1)}, u32[]{:S(2)}, u32[]{:S(2)}) %collective-permute-start.9) | collective-permute-done | bytes 131104 | tf_op jit(solution)/shard_map/ppermute | solution.py:742
  51.9 3.0 %collective-permute-done.10.step3_ref = f32[2,128,128]{2,1,0:T(8,128)S(1)} collective-permute-done((f32[2,128,128]{2,1,0:T(8,128)S(1)}, f32[2,128,128]{2,1,0:T(8,128)S(1)}, u32[]{:S(2)}, u32[]{:S(2)}) %collective-permute-start.10) | collective-permute-done | bytes 131104 | tf_op jit(solution)/shard_map/ppermute | solution.py:742
  54.9 2.4 %collective-permute-start.12 = (f32[8,128,128]{2,1,0:T(8,128)S(1)}, f32[8,128,128]{2,1,0:T(8,128)S(1)}, u32[]{:S(2)}, u32[]{:S(2)}) collective-permute-start(f32[8,128,128]{2,1,0:T(8,128)S(1)} %pack_states.1.packed_ref), channel_id=1, source_target_pairs={{0,4},{4,0},{8,12},{12,8},{16,20},{20,16},{24,28},{28,24},{32,36},... | collective-permute-start | bytes 1572872 | tf_op jit(solution)/shard_map/ppermute | solution.py:754
  57.3 1.5 %collective-permute-done.12.swapped_ref = f32[8,128,128]{2,1,0:T(8,128)S(1)} collective-permute-done((f32[8,128,128]{2,1,0:T(8,128)S(1)}, f32[8,128,128]{2,1,0:T(8,128)S(1)}, u32[]{:S(2)}, u32[]{:S(2)}) %collective-permute-start.12) | collective-permute-done | bytes 524320 | tf_op jit(solution)/shard_map/ppermute | solution.py:754
  58.8 1.9 %outputs.1 = (f32[768,1024]{1,0:T(8,128)S(1)}, f32[768,1024]{1,0:T(8,128)S(1)}, f32[8,768]{1,0:T(8,128)S(1)}, f32[16,128,128]{2,1,0:T(8,128)S(1)}) custom-call(f32[2,128,128]{2,1,0:T(8,128)S(1)} %get-tuple-element.54.last_ref.here_ref, f32[8,128,128]{2,1,0:T(8,128)S(1)} %pack_states.1.packed_ref, f32[8,128,128]{2,1,0:T(8,128)S(1)} %collective-permute-done.12.swapped_ref, ...), custom_call_target="tpu_custom_call" | custom-call | flops 2000000 | bytes 9000 | tf_op jit(solution)/shard_map/outputs/pallas_call | solution.py:756
  60.7 2.6 %collective-permute-start.15 = (f32[8,768]{1,0:T(8,128)S(1)}, f32[8,768]{1,0:T(8,128)S(1)}, u32[]{:S(2)}, u32[]{:S(2)}) collective-permute-start(f32[8,768]{1,0:T(8,128)S(1)} %get-tuple-element.72.after_ref.sum_ref), channel_id=1, source_target_pairs={{0,3},{1,0},{2,1},{3,2},{4,7},{5,4},{6,5},{7,6},{8,11},{9,8},{10,9... | collective-permute-start | bytes 73736 | tf_op jit(solution)/shard_map/ppermute | solution.py:782
  63.3 0.5 collective-permute-start.14
  63.8 0.6 collective-permute-start.13
  64.4 2.2 %write_states.1 = (f32[3,16,128,128]{3,2,1,0:T(8,128)}, f32[8,128]{1,0:T(8,128)S(1)}) custom-call(f32[16,128,128]{2,1,0:T(8,128)S(1)} %get-tuple-element.73.first_ref, f32[2,8,128,128]{3,2,1,0:T(8,128)S(1)} %get-tuple-element.63.own_before_ref, f32[2,8,128,128]{3,2,1,0:T(8,128)S(1)} %get-tuple-element.64.away_before_ref, ...), custom_call_target="tpu_custom_call" | custom-call | flops 4000000000 | bytes 9000000 | tf_op jit(solution)/shard_map/write_states/pallas_call | solution.py:785
  66.6 0.0 collective-permute-done.15.c_ref
  66.7 0.8 %collective-permute-done.14.b_ref = f32[8,768]{1,0:T(8,128)S(1)} collective-permute-done((f32[8,768]{1,0:T(8,128)S(1)}, f32[8,768]{1,0:T(8,128)S(1)}, u32[]{:S(2)}, u32[]{:S(2)}) %collective-permute-start.14) | collective-permute-done | bytes 24608 | tf_op jit(solution)/shard_map/ppermute | solution.py:782
  67.5 0.3 collective-permute-done.13.a_ref
  67.8 0.0 copy-done.1
  67.8 2.2 %scale.1 = bf16[768,2048]{1,0:T(8,128)(2,1)} custom-call(f32[768,1024]{1,0:T(8,128)S(1)} %get-tuple-element.70.own_ref, f32[768,1024]{1,0:T(8,128)S(1)} %get-tuple-element.71.away_ref, f32[1,2048]{1,0:T(1,128)S(1)} %bitcast.2, f32[8,768]{1,0:T(8,128)S(1)} %get-tuple-element.72.after_ref.sum_ref, f32[8,768]{1,0:T(8,128)S(1)} %collective-permute-done.13.a_ref, ...), custom_call_target="tpu_custom_call" | custom-call | flops 5000000 | bytes 6500000 | tf_op jit(solution)/shard_map/scale/pallas_call | solution.py:798
  (8 shorter events, 0.1 us)
Async XLA Ops:
  4.6 4.9 %collective-permute-start = (f32[8,136,128]{2,1,0:T(8,128)S(1)}, f32[8,136,128]{2,1,0:T(8,128)S(1)}, u32[]{:S(2)}, u32[]{:S(2)}) collective-permute-start(f32[8,136,128]{2,1,0:T(8,128)S(1)} %get-tuple-element.43), channel_id=1, source_target_pairs={{0,4},{4,0},{8,12},{12,8},{16,20},{20,16},{24,28},{28,24},{32,36},... | collective-permute-start | bytes 1671176 | tf_op jit(solution)/shard_map/ppermute | solution.py:660
  7.9 11.7 %copy-start = (bf16[768,128]{1,0:T(8,128)(2,1)S(1)}, bf16[768,128]{1,0:T(8,128)(2,1)}, u32[]{:S(2)}) copy-start(bf16[768,128]{1,0:T(8,128)(2,1)} %b_ref.1) | copy-start | bytes 589828
  7.9 11.7 %copy-start.2 = (s32[16]{0:T(128)S(1)}, s32[16]{0:T(128)}, u32[]{:S(2)}) copy-start(s32[16]{0:T(128)} %doc_ref.1) | copy-start | bytes 196
  7.9 11.7 %copy-start.3 = (bf16[768,2048]{1,0:T(8,128)(2,1)S(1)}, bf16[768,2048]{1,0:T(8,128)(2,1)}, u32[]{:S(2)}) copy-start(bf16[768,2048]{1,0:T(8,128)(2,1)} %gate_ref.3) | copy-start | bytes 9437188
  7.9 11.7 %copy-start.4 = (bf16[768,128]{1,0:T(8,128)(2,1)S(1)}, bf16[768,128]{1,0:T(8,128)(2,1)}, u32[]{:S(2)}) copy-start(bf16[768,128]{1,0:T(8,128)(2,1)} %c_ref.1) | copy-start | bytes 589828
  7.9 11.7 %copy-start.5 = (f32[16]{0:T(128)S(1)}, f32[16]{0:T(128)}, u32[]{:S(2)}) copy-start(f32[16]{0:T(128)} %skip_ref.3) | copy-start | bytes 196
  9.3 19.1 %collective-permute-start.6 = (f32[8,136,128]{2,1,0:T(8,128)S(1)}, f32[8,136,128]{2,1,0:T(8,128)S(1)}, u32[]{:S(2)}, u32[]{:S(2)}) collective-permute-start(f32[8,136,128]{2,1,0:T(8,128)S(1)} %own_states.1.own_ref), channel_id=1, source_target_pairs={{0,4},{4,0},{8,12},{12,8},{16,20},{20,16},{24,28},{28,24},{32,36},... | collective-permute-start | bytes 1671176 | tf_op jit(solution)/shard_map/ppermute | solution.py:681
  9.6 14.1 %collective-permute-start.4 = (f32[1,136,128]{2,1,0:T(8,128)S(1)}, f32[1,136,128]{2,1,0:T(8,128)S(1)}, u32[]{:S(2)}, u32[]{:S(2)}) collective-permute-start(f32[1,136,128]{2,1,0:T(8,128)S(1)} %get-tuple-element.47), channel_id=1, source_target_pairs={{0,32},{4,36},{8,40},{12,44},{16,48},{20,52},{24,56},{28,60},{32,0... | collective-permute-start | bytes 208904 | tf_op jit(solution)/shard_map/ppermute | solution.py:680
  14.8 8.9 %collective-permute-start.1 = (f32[2,136,128]{2,1,0:T(8,128)S(1)}, f32[2,136,128]{2,1,0:T(8,128)S(1)}, u32[]{:S(2)}, u32[]{:S(2)}) collective-permute-start(f32[2,136,128]{2,1,0:T(8,128)S(1)} %get-tuple-element.44), channel_id=1, source_target_pairs={{0,8},{4,60},{8,16},{12,4},{16,24},{20,12},{24,32},{28,20},{32,40}... | collective-permute-start | bytes 417800 | tf_op jit(solution)/shard_map/ppermute | solution.py:680
  14.8 9.9 %collective-permute-start.2 = (f32[2,136,128]{2,1,0:T(8,128)S(1)}, f32[2,136,128]{2,1,0:T(8,128)S(1)}, u32[]{:S(2)}, u32[]{:S(2)}) collective-permute-start(f32[2,136,128]{2,1,0:T(8,128)S(1)} %get-tuple-element.45), channel_id=1, source_target_pairs={{0,16},{4,52},{8,24},{12,60},{16,32},{20,4},{24,40},{28,12},{32,48... | collective-permute-start | bytes 417800 | tf_op jit(solution)/shard_map/ppermute | solution.py:680
  14.9 13.4 %collective-permute-start.3 = (f32[2,136,128]{2,1,0:T(8,128)S(1)}, f32[2,136,128]{2,1,0:T(8,128)S(1)}, u32[]{:S(2)}, u32[]{:S(2)}) collective-permute-start(f32[2,136,128]{2,1,0:T(8,128)S(1)} %get-tuple-element.46), channel_id=1, source_target_pairs={{0,24},{4,44},{8,32},{12,52},{16,40},{20,60},{24,48},{28,4},{32,56... | collective-permute-start | bytes 417800 | tf_op jit(solution)/shard_map/ppermute | solution.py:680
  28.3 2.0 %collective-permute-start.5 = (f32[8,136,128]{2,1,0:T(8,128)S(1)}, f32[8,136,128]{2,1,0:T(8,128)S(1)}, u32[]{:S(2)}, u32[]{:S(2)}) collective-permute-start(f32[8,136,128]{2,1,0:T(8,128)S(1)} %pack_parts.1.packed_ref), channel_id=1, source_target_pairs={{0,4},{4,0},{8,12},{12,8},{16,20},{20,16},{24,28},{28,24},{32,36},... | collective-permute-start | bytes 1671176 | tf_op jit(solution)/shard_map/ppermute | solution.py:724
  30.5 6.4 %collective-permute-start.7 = (f32[2,128,128]{2,1,0:T(8,128)S(1)}, f32[2,128,128]{2,1,0:T(8,128)S(1)}, u32[]{:S(2)}, u32[]{:S(2)}) collective-permute-start(f32[2,128,128]{2,1,0:T(8,128)S(1)} %get-tuple-element.53), channel_id=1, source_target_pairs={{0,64},{4,68},{8,72},{12,76},{16,80},{20,84},{24,88},{28,92},{32,9... | collective-permute-start | bytes 393224 | tf_op jit(solution)/shard_map/ppermute | solution.py:733
  37.0 12.9 %collective-permute-start.11 = (f32[1,128,128]{2,1,0:T(8,128)S(1)}, f32[1,128,128]{2,1,0:T(8,128)S(1)}, u32[]{:S(2)}, u32[]{:S(2)}) collective-permute-start(f32[1,128,128]{2,1,0:T(8,128)S(1)} %get-tuple-element.58), channel_id=1, source_target_pairs={{0,32},{4,36},{8,40},{12,44},{16,48},{20,52},{24,56},{28,60},{32,0... | collective-permute-start | bytes 196616 | tf_op jit(solution)/shard_map/ppermute | solution.py:742
  41.7 8.2 %collective-permute-start.8 = (f32[2,128,128]{2,1,0:T(8,128)S(1)}, f32[2,128,128]{2,1,0:T(8,128)S(1)}, u32[]{:S(2)}, u32[]{:S(2)}) collective-permute-start(f32[2,128,128]{2,1,0:T(8,128)S(1)} %get-tuple-element.55), channel_id=1, source_target_pairs={{0,8},{4,60},{8,16},{12,4},{16,24},{20,12},{24,32},{28,20},{32,40}... | collective-permute-start | bytes 393224 | tf_op jit(solution)/shard_map/ppermute | solution.py:742
  41.9 10.0 %collective-permute-start.9 = (f32[2,128,128]{2,1,0:T(8,128)S(1)}, f32[2,128,128]{2,1,0:T(8,128)S(1)}, u32[]{:S(2)}, u32[]{:S(2)}) collective-permute-start(f32[2,128,128]{2,1,0:T(8,128)S(1)} %get-tuple-element.56), channel_id=1, source_target_pairs={{0,16},{4,52},{8,24},{12,60},{16,32},{20,4},{24,40},{28,12},{32,48... | collective-permute-start | bytes 393224 | tf_op jit(solution)/shard_map/ppermute | solution.py:742
  43.7 11.2 %collective-permute-start.10 = (f32[2,128,128]{2,1,0:T(8,128)S(1)}, f32[2,128,128]{2,1,0:T(8,128)S(1)}, u32[]{:S(2)}, u32[]{:S(2)}) collective-permute-start(f32[2,128,128]{2,1,0:T(8,128)S(1)} %get-tuple-element.57), channel_id=1, source_target_pairs={{0,24},{4,44},{8,32},{12,52},{16,40},{20,60},{24,48},{28,4},{32,56... | collective-permute-start | bytes 393224 | tf_op jit(solution)/shard_map/ppermute | solution.py:742
  54.9 3.9 %collective-permute-start.12 = (f32[8,128,128]{2,1,0:T(8,128)S(1)}, f32[8,128,128]{2,1,0:T(8,128)S(1)}, u32[]{:S(2)}, u32[]{:S(2)}) collective-permute-start(f32[8,128,128]{2,1,0:T(8,128)S(1)} %pack_states.1.packed_ref), channel_id=1, source_target_pairs={{0,4},{4,0},{8,12},{12,8},{16,20},{20,16},{24,28},{28,24},{32,36},... | collective-permute-start | bytes 1572872 | tf_op jit(solution)/shard_map/ppermute | solution.py:754
  60.7 5.9 %collective-permute-start.15 = (f32[8,768]{1,0:T(8,128)S(1)}, f32[8,768]{1,0:T(8,128)S(1)}, u32[]{:S(2)}, u32[]{:S(2)}) collective-permute-start(f32[8,768]{1,0:T(8,128)S(1)} %get-tuple-element.72.after_ref.sum_ref), channel_id=1, source_target_pairs={{0,3},{1,0},{2,1},{3,2},{4,7},{5,4},{6,5},{7,6},{8,11},{9,8},{10,9... | collective-permute-start | bytes 73736 | tf_op jit(solution)/shard_map/ppermute | solution.py:782
  63.3 4.2 %collective-permute-start.14 = (f32[8,768]{1,0:T(8,128)S(1)}, f32[8,768]{1,0:T(8,128)S(1)}, u32[]{:S(2)}, u32[]{:S(2)}) collective-permute-start(f32[8,768]{1,0:T(8,128)S(1)} %get-tuple-element.72.after_ref.sum_ref), channel_id=1, source_target_pairs={{0,2},{1,3},{2,0},{3,1},{4,6},{5,7},{6,4},{7,5},{8,10},{9,11},{10,... | collective-permute-start | bytes 73736 | tf_op jit(solution)/shard_map/ppermute | solution.py:782
  63.8 3.9 %collective-permute-start.13 = (f32[8,768]{1,0:T(8,128)S(1)}, f32[8,768]{1,0:T(8,128)S(1)}, u32[]{:S(2)}, u32[]{:S(2)}) collective-permute-start(f32[8,768]{1,0:T(8,128)S(1)} %get-tuple-element.72.after_ref.sum_ref), channel_id=1, source_target_pairs={{0,1},{1,2},{2,3},{3,0},{4,5},{5,6},{6,7},{7,4},{8,9},{9,10},{10,1... | collective-permute-start | bytes 73736 | tf_op jit(solution)/shard_map/ppermute | solution.py:782
  64.4 3.3 %copy-start.1 = (f32[2048]{0:T(1024)S(1)}, f32[2048]{0:T(1024)}, u32[]{:S(2)}) copy-start(f32[2048]{0:T(1024)} %param.16) | copy-start | bytes 24580

commit v4 on v3

--- a/solution.py
+++ b/solution.py
@@ -401,7 +401,7 @@
     token_ref[...] = jnp.zeros_like(token_ref)
 
 
-def pack_kernel(step1_ref, step2_ref, step3_ref, step4_ref, last_ref, after_ref, packed_ref):
+def pack_kernel(step3_ref, step2_ref, step1_ref, step4_ref, last_ref, after_ref, packed_ref):
     for step, ref in enumerate((step1_ref, step2_ref, step3_ref)):
         packed_ref[2 * step] = ref[0]
         packed_ref[2 * step + 1] = ref[1]
@@ -454,12 +454,17 @@
     token_ref[...] = jnp.zeros_like(token_ref)
 
 
+EARLY_SLOTS = (6, 7, 8, 9, 10, 11, 12, 13, 15)
+LATE_SLOTS = (0, 1, 2, 3, 4, 5, 14)
+
+
 def outputs_kernel(
-    heads,
+    slots,
+    half,
     groups,
+    last,
     here_ref,
-    packed_ref,
-    swapped_ref,
+    arrived_ref,
     own_other_ref,
     away_other_ref,
     own_before_ref,
@@ -470,59 +475,65 @@
     own_v_ref,
     away_u_ref,
     away_v_ref,
-    own_gated_ref,
-    away_gated_ref,
+    sums_ref,
+    gated_ref,
     squares_ref,
     first_ref,
 ):
     core = core_index()
-    half = heads // 2
-    for side, earlier_ref in enumerate((own_other_ref, away_other_ref)):
-        for place in range(half):
-            if place < 6:
-                chip_state = (swapped_ref, packed_ref)[side][place]
-            elif place == 6:
-                chip_state = (packed_ref, swapped_ref)[side][place]
-            else:
-                chip_state = here_ref[side]
-            joined = earlier_ref[place, N : N + 1, :] * chip_state + earlier_ref[place, 0:N, :]
-            first_ref[side * half + place] = jnp.where(core == 0, chip_state, joined)
+    sides = (
+        (own_other_ref, own_before_ref, own_u_ref, own_v_ref),
+        (away_other_ref, away_before_ref, away_u_ref, away_v_ref),
+    )
+    for index, slot in enumerate(slots):
+        side, place = slot // half, slot % half
+        earlier_ref = sides[side][0]
+        chip_state = here_ref[side] if place == half - 1 else arrived_ref[place]
+        joined = earlier_ref[place, N : N + 1, :] * chip_state + earlier_ref[place, 0:N, :]
+        first_ref[index] = jnp.where(core == 0, chip_state, joined)
 
     for group in range(groups):
         block = slice(group * Q, (group + 1) * Q)
         reach = stats_ref[16 + group : 17 + group, :]
-        squares = jnp.zeros((Q, P_SIZE), F32)
-        for side, (u_ref, v_ref, before_ref, gated_ref) in enumerate(
-            (
-                (own_u_ref, own_v_ref, own_before_ref, own_gated_ref),
-                (away_u_ref, away_v_ref, away_before_ref, away_gated_ref),
+        squares = sums_ref[block, :] if last else jnp.zeros((Q, P_SIZE), F32)
+        for start in range(0, len(slots), 2):
+            pair = range(start, min(start + 2, len(slots)))
+            states = []
+            for index in pair:
+                side, place = slots[index] // half, slots[index] % half
+                state = first_ref[index]
+                if group > 0:
+                    lane = slice(slots[index], slots[index] + 1)
+                    state = state * reach[:, lane] + sides[side][1][group - 1, place]
+                states.append(state.astype(BF16))
+            both = jnp.concatenate(states, axis=1) if len(states) > 1 else states[0]
+            carried = jnp.dot(c_ref[block, :], both, preferred_element_type=F32)
+            for part, index in enumerate(pair):
+                side, place = slots[index] // half, slots[index] % half
+                _, _, u_ref, v_ref = sides[side]
+                span = slice(place * P_SIZE, (place + 1) * P_SIZE)
+                here = slice(part * P_SIZE, (part + 1) * P_SIZE)
+                gated = u_ref[block, span] + v_ref[block, span] * carried[:, here]
+                gated_ref[block, index * P_SIZE : (index + 1) * P_SIZE] = gated
+                squares = squares + gated * gated
+        if last:
+            squares_ref[:, block] = jnp.broadcast_to(
+                jnp.sum(squares.T, axis=0, keepdims=True), (8, Q)
             )
-        ):
-            for pair in range(half // 2):
-                both = []
-                for index in (2 * pair, 2 * pair + 1):
-                    slot = side * half + index
-                    state = first_ref[slot]
-                    if group > 0:
-                        state = state * reach[:, slot : slot + 1] + before_ref[group - 1, index]
-                    both.append(state.astype(BF16))
-                carried = jnp.dot(
-                    c_ref[block, :], jnp.concatenate(both, axis=1), preferred_element_type=F32
-                )
-                span = slice(2 * pair * P_SIZE, 2 * (pair + 1) * P_SIZE)
-                gated = u_ref[block, span] + v_ref[block, span] * carried
-                gated_ref[block, span] = gated
-                square = gated * gated
-                squares = squares + square[:, 0:P_SIZE] + square[:, P_SIZE:]
-        squares_ref[:, block] = jnp.broadcast_to(
-            jnp.sum(squares.T, axis=0, keepdims=True), (8, Q)
-        )
+        else:
+            squares_ref[block, :] = squares
+
+
+def split_place(slot):
+    early = slot in EARLY_SLOTS
+    return (0, EARLY_SLOTS.index(slot)) if early else (1, LATE_SLOTS.index(slot))
 
 
 def write_states_kernel(
     heads,
     groups,
-    first_ref,
+    early_first_ref,
+    late_first_ref,
     own_before_ref,
     away_before_ref,
     stats_ref,
@@ -540,7 +551,8 @@
         for side, before_ref in enumerate((own_before_ref, away_before_ref)):
             for index in range(half):
                 slot = side * half + index
-                state = first_ref[slot]
+                which, at = split_place(slot)
+                state = (early_first_ref, late_first_ref)[which][at]
                 if group > 0:
                     state = state * reach[:, slot : slot + 1] + before_ref[group - 1, index]
                 states_ref[group, slot] = state.T
@@ -560,19 +572,20 @@
 
 
 def scale_kernel(
-    inner, heads, own_ref, away_ref, gain_ref, sum_ref, a_ref, b_ref, c_ref, after_ref, out_hbm, out_ref, sems
+    inner, heads, early_ref, late_ref, gain_ref, sum_ref, a_ref, b_ref, c_ref, after_ref, out_hbm, out_ref, sems
 ):
     mean = (sum_ref[...] + a_ref[...] + b_ref[...] + c_ref[...]) * (1.0 / inner)
     scale = lax.rsqrt(mean + 1e-05)
     half = heads // 2
     spans = head_spans(heads)
     copies = []
-    for chunk in range(own_ref.shape[0] // SCALE_ROWS):
+    for chunk in range(early_ref.shape[0] // SCALE_ROWS):
         block = slice(chunk * SCALE_ROWS, (chunk + 1) * SCALE_ROWS)
         column = jnp.broadcast_to(scale[0:1, block], (P_SIZE, SCALE_ROWS)).T
         for slot in range(heads):
-            gated_ref = own_ref if slot < half else away_ref
-            span = slice(slot % half * P_SIZE, (slot % half + 1) * P_SIZE)
+            which, at = split_place(slot)
+            gated_ref = (early_ref, late_ref)[which]
+            span = slice(at * P_SIZE, (at + 1) * P_SIZE)
             place = spans[slot]
             out_ref[block, place] = (
                 gated_ref[block, span] * column * gain_ref[:, place]
@@ -677,7 +690,8 @@
         name="join_cores",
     )(own_state, own_other)
     here_part = joined.pop()
-    arrived = [lax.ppermute(sent, "seq", pairs) for sent, pairs in zip(joined, AROUND)]
+    arrived = [lax.ppermute(joined[k], "seq", AROUND[k]) for k in (2, 1, 0, 3)]
+    arrived = [arrived[2], arrived[1], arrived[0], arrived[3]]
     away_other = lax.ppermute(own_state, "seq", CORE_SWAP)
 
     away_u, away_v, away_before, entry_c, decay, masked, away_token = pl.pallas_call(
@@ -718,7 +732,7 @@
             compiler_params=params(8),
             cost_estimate=cost(300_000, 1_100_000),
             name=name,
-        )(*states, last, after)
+        )(*states[2::-1], states[3], last, after)
 
     packed_parts = pack(arrived, here_part, away_token, "pack_parts")
     swapped_parts = lax.ppermute(packed_parts, "seq", CORE_SWAP)
@@ -739,7 +753,8 @@
         cost_estimate=cost(1_000_000, 1_100_000),
         name="entering",
     )(parts, carried)
-    returned = [lax.ppermute(sent, "seq", pairs) for sent, pairs in zip(steps, AROUND)]
+    returned = [lax.ppermute(steps[k], "seq", AROUND[k]) for k in (2, 1, 0, 3)]
+    returned = [returned[2], returned[1], returned[0], returned[3]]
 
     own_u, own_v, own_before, own_token = pl.pallas_call(
         functools.partial(own_inside_kernel, heads, groups),
@@ -753,29 +768,37 @@
     packed = pack(returned, here, own_token, "pack_states")
     swapped = lax.ppermute(packed, "seq", CORE_SWAP)
 
-    own_gated, away_gated, squares, first = pl.pallas_call(
-        functools.partial(outputs_kernel, heads, groups),
-        in_specs=[vmem] * 13,
-        out_specs=[vmem] * 4,
-        out_shape=[half_wide] * 2 + [sds((8, row_count), F32), sds((heads, N, P_SIZE), F32)],
-        compiler_params=params(30),
-        cost_estimate=cost(2_000_000, 9_000),
-        name="outputs",
-    )(
-        here,
-        packed,
-        swapped,
-        own_other,
-        away_other,
-        own_before,
-        away_before,
-        stats,
-        entry_c,
-        own_u,
-        own_v,
-        away_u,
-        away_v,
-    )
+    def outputs(slots, last, arrived_states, sums):
+        return pl.pallas_call(
+            functools.partial(outputs_kernel, slots, half, groups, last),
+            in_specs=[vmem] * 12 + [vmem if last else anywhere],
+            out_specs=[vmem] * 3,
+            out_shape=[
+                sds((row_count, len(slots) * P_SIZE), F32),
+                sds((8, row_count) if last else (row_count, P_SIZE), F32),
+                sds((len(slots), N, P_SIZE), F32),
+            ],
+            compiler_params=params(26),
+            cost_estimate=cost(2_000_000, 9_000),
+            name="late_outputs" if last else "early_outputs",
+        )(
+            here,
+            arrived_states,
+            own_other,
+            away_other,
+            own_before,
+            away_before,
+            stats,
+            entry_c,
+            own_u,
+            own_v,
+            away_u,
+            away_v,
+            sums,
+        )
+
+    early_gated, early_sums, early_first = outputs(EARLY_SLOTS, False, packed, stats)
+    late_gated, squares, late_first = outputs(LATE_SLOTS, True, swapped, early_sums)
 
     tp_size = 4
     sums = [
@@ -784,7 +807,7 @@
     ]
     group_states, states_token = pl.pallas_call(
         functools.partial(write_states_kernel, heads, groups),
-        in_specs=[vmem] * 4 + [anywhere],
+        in_specs=[vmem] * 5 + [anywhere],
         out_specs=[hbm, vmem],
         out_shape=[sds((groups, heads, P_SIZE, N), F32), token],
         scratch_shapes=[
@@ -794,7 +817,7 @@
         compiler_params=params(16),
         cost_estimate=cost(4_000_000_000, 9_000_000),
         name="write_states",
-    )(first, own_before, away_before, stats, squares)
+    )(early_first, late_first, own_before, away_before, stats, squares)
     mixed_out = pl.pallas_call(
         functools.partial(scale_kernel, width * tp_size, heads),
         in_specs=[vmem] * 7 + [anywhere],
@@ -807,7 +830,7 @@
         compiler_params=params(16),
         cost_estimate=cost(5_000_000, 6_500_000),
         name="scale",
-    )(own_gated, away_gated, gain, squares, *sums, states_token)
+    )(early_gated, late_gated, gain, squares, *sums, states_token)
     return (mixed_out, group_states)
 
 

time: 70.2 us -> 68.3 us (0.973)
  starting transfers between devices: 30.5 us -> 29.5 us
  waiting for transfers between devices: 19.2 us -> 18.3 us
    ppermute x8, starting transfers between devices: 19.5 us -> 17.2 us  [the longest x4 10 us: local(): arrived = [lax.ppermute(joined[k], 'seq', AROUND[k]) for k in (2, 1, 0, 3)]]
    ppermute x1, starting transfers between devices: 0.11 us -> 1.42 us  [local(): swapped_parts = lax.ppermute(packed_parts, 'seq', CORE_SWAP)]
    ppermute x1, waiting for transfers between devices: 1.54 us -> 0.51 us  [local(): swapped = lax.ppermute(packed, 'seq', CORE_SWAP)]
    ppermute x8, waiting for transfers between devices: 9.5 us -> 10.2 us  [the longest x4 5.12 us: local(): arrived = [lax.ppermute(joined[k], 'seq', AROUND[k]) for k in (2, 1, 0, 3)]]
    pallas_call x1 -> x2, Pallas kernels: 1.9 us -> 1.98 us  [outputs(): pl.pallas_call(functools.partial(outputs_kernel, slots, half, groups, las...]
  transfers between devices with their start and end apart: 16 -> 16, of which waited for: 10 -> 11; matrix products, arithmetic and copies ran while one was open for 0% -> 0% of each run, Pallas kernels for 16% -> 18%
where the time goes in v4:
time: 68.3 us; the launch traced here: 68.2 us
  starting transfers between devices  29.5 us (43%)
  Pallas kernels  19.4 us (28%)
  waiting for transfers between devices  18.3 us (27%)
  between operations  0.92 us (1%)
    ppermute x4, starting transfers between devices, local(): arrived = [lax.ppermute(joined[k], 'seq', AROUND[k]) for k in (2, 1, 0, 3)]  10 us
    ppermute x4, starting transfers between devices, local(): returned = [lax.ppermute(steps[k], 'seq', AROUND[k]) for k in (2, 1, 0, 3)]  7.14 us
    ppermute x4, waiting for transfers between devices, local(): arrived = [lax.ppermute(joined[k], 'seq', AROUND[k]) for k in (2, 1, 0, 3)]  5.12 us
    ppermute x4, waiting for transfers between devices, local(): returned = [lax.ppermute(steps[k], 'seq', AROUND[k]) for k in (2, 1, 0, 3)]  5.1 us
    ppermute x1, waiting for transfers between devices, local(): carried = lax.ppermute(total, 'seq', NEXT_ROW)  4.76 us
    pallas_call x1, Pallas kernels, local(): pl.pallas_call(functools.partial(away_inside_kernel, heads, groups), in_s...  4.02 us
    pallas_call x1, Pallas kernels, local(): pl.pallas_call(functools.partial(away_states_kernel, heads, groups), in_s...  3.95 us
    ppermute x3, starting transfers between devices, local(): lax.ppermute(squares, 'tp', [(i, (i + k) % tp_size) for i in range(tp_siz...  3.64 us
  transfers between devices with their start and end apart: 16, of which 11 were waited for; matrix products, arithmetic and copies ran while one was open for 0% of the time, Pallas kernels for 18%

profile of v4, /device:TPU:1, one launch (start us, length us, event | category | flops | bytes accessed | tf_op | source)
XLA Modules:
  0.0 68.2 jit_solution(5607059491157006968)
XLA Ops:
  0.6 3.9 %away_states.1 = (f32[8,136,128]{2,1,0:T(8,128)S(1)}, f32[24,128]{1,0:T(8,128)S(1)}, f32[256,48]{1,0:T(8,128)S(1)}, bf16[3,128,256]{2,1,0:T(8,128)(2,1)S(1)}, f3...) custom-call(s32[16]{0:T(128)} %doc_ref.1, f32[16]{0:T(128)} %rate_hbm.1, f32[16,768]{1,0:T(8,128)} %bitcast.3, ...), custom_call_target="tpu_custom_call" | custom-call | flops 200000000 | bytes 4000000 | tf_op jit(solution)/shard_map/away_states/pallas_call | solution.py:649
  4.6 3.3 %collective-permute-start = (f32[8,136,128]{2,1,0:T(8,128)S(1)}, f32[8,136,128]{2,1,0:T(8,128)S(1)}, u32[]{:S(2)}, u32[]{:S(2)}) collective-permute-start(f32[8,136,128]{2,1,0:T(8,128)S(1)} %get-tuple-element.45), channel_id=1, source_target_pairs={{0,4},{4,0},{8,12},{12,8},{16,20},{20,16},{24,28},{28,24},{32,36},... | collective-permute-start | bytes 1671176 | tf_op jit(solution)/shard_map/ppermute | solution.py:673
  7.9 0.0 copy-start.5
  7.9 1.3 %own_states.1.own_ref = f32[8,136,128]{2,1,0:T(8,128)S(1)} custom-call(f32[24,128]{1,0:T(8,128)S(1)} %get-tuple-element.41.stats_ref.sums_ref, f32[256,48]{1,0:T(8,128)S(1)} %get-tuple-element.42.scale_ref, bf16[3,128,256]{2,1,0:T(8,128)(2,1)S(1)} %get-tuple-element.43.tail_ref, bf16[768,2048]{1,0:T(8,128)(2,1)S(1)} %get-tuple-element.44.x_ref), custom_call_target="tpu_custom_call" | custom-call | flops 2000000000 | bytes 4000000 | tf_op jit(solution)/shard_map/own_states/pallas_call | solution.py:675
  9.3 0.1 collective-permute-start.6
  9.4 0.1 collective-permute-done.other_ref.own_other_ref
  9.5 0.1 join_cores.1
  9.6 5.2 %collective-permute-start.4 = (f32[1,136,128]{2,1,0:T(8,128)S(1)}, f32[1,136,128]{2,1,0:T(8,128)S(1)}, u32[]{:S(2)}, u32[]{:S(2)}) collective-permute-start(f32[1,136,128]{2,1,0:T(8,128)S(1)} %get-tuple-element.49), channel_id=1, source_target_pairs={{0,32},{4,36},{8,40},{12,44},{16,48},{20,52},{24,56},{28,60},{32,0... | collective-permute-start | bytes 208904 | tf_op jit(solution)/shard_map/ppermute | solution.py:693
  14.8 0.0 collective-permute-start.1
  14.8 4.1 %collective-permute-start.2 = (f32[2,136,128]{2,1,0:T(8,128)S(1)}, f32[2,136,128]{2,1,0:T(8,128)S(1)}, u32[]{:S(2)}, u32[]{:S(2)}) collective-permute-start(f32[2,136,128]{2,1,0:T(8,128)S(1)} %get-tuple-element.47), channel_id=1, source_target_pairs={{0,16},{4,52},{8,24},{12,60},{16,32},{20,4},{24,40},{28,12},{32,48... | collective-permute-start | bytes 417800 | tf_op jit(solution)/shard_map/ppermute | solution.py:693
  18.9 0.7 %collective-permute-start.3 = (f32[2,136,128]{2,1,0:T(8,128)S(1)}, f32[2,136,128]{2,1,0:T(8,128)S(1)}, u32[]{:S(2)}, u32[]{:S(2)}) collective-permute-start(f32[2,136,128]{2,1,0:T(8,128)S(1)} %get-tuple-element.48), channel_id=1, source_target_pairs={{0,8},{4,60},{8,16},{12,4},{16,24},{20,12},{24,32},{28,20},{32,40}... | collective-permute-start | bytes 417800 | tf_op jit(solution)/shard_map/ppermute | solution.py:693
  19.6 0.0 copy-done
  19.6 0.0 copy-done.2
  19.6 0.0 copy-done.3
  19.6 0.0 copy-done.5
  19.6 4.0 %away_inside.1 = (f32[768,1024]{1,0:T(8,128)S(1)}, f32[768,1024]{1,0:T(8,128)S(1)}, f32[2,8,128,128]{3,2,1,0:T(8,128)S(1)}, bf16[768,128]{1,0:T(8,128)(2,1)S(1)}...) custom-call(s32[16]{0:T(128)S(1)} %copy-done.2, f32[16]{0:T(128)S(1)} %copy-done.5, ...), custom_call_target="tpu_custom_call" | custom-call | flops 8000000000 | bytes 20000000 | tf_op jit(solution)/shard_map/away_inside/pallas_call | solution.py:697
  23.7 0.0 collective-permute-done.4.step4_ref
  23.7 0.0 collective-permute-done.1.step3_ref
  23.7 3.1 %collective-permute-done.2.step2_ref = f32[2,136,128]{2,1,0:T(8,128)S(1)} collective-permute-done((f32[2,136,128]{2,1,0:T(8,128)S(1)}, f32[2,136,128]{2,1,0:T(8,128)S(1)}, u32[]{:S(2)}, u32[]{:S(2)}) %collective-permute-start.2) | collective-permute-done | bytes 139296 | tf_op jit(solution)/shard_map/ppermute | solution.py:693
  26.8 2.0 %collective-permute-done.3.step1_ref = f32[2,136,128]{2,1,0:T(8,128)S(1)} collective-permute-done((f32[2,136,128]{2,1,0:T(8,128)S(1)}, f32[2,136,128]{2,1,0:T(8,128)S(1)}, u32[]{:S(2)}, u32[]{:S(2)}) %collective-permute-start.3) | collective-permute-done | bytes 139296 | tf_op jit(solution)/shard_map/ppermute | solution.py:693
  28.8 1.4 %collective-permute-start.5 = (f32[8,136,128]{2,1,0:T(8,128)S(1)}, f32[8,136,128]{2,1,0:T(8,128)S(1)}, u32[]{:S(2)}, u32[]{:S(2)}) collective-permute-start(f32[8,136,128]{2,1,0:T(8,128)S(1)} %pack_parts.1.packed_ref), channel_id=1, source_target_pairs={{0,4},{4,0},{8,12},{12,8},{16,20},{20,16},{24,28},{28,24},{32,36},... | collective-permute-start | bytes 1671176 | tf_op jit(solution)/shard_map/ppermute | solution.py:738
  30.3 0.0 collective-permute-done.6.after_ref.away_other_ref
  30.3 1.6 %collective-permute-done.5.swapped_ref = f32[8,136,128]{2,1,0:T(8,128)S(1)} collective-permute-done((f32[8,136,128]{2,1,0:T(8,128)S(1)}, f32[8,136,128]{2,1,0:T(8,128)S(1)}, u32[]{:S(2)}, u32[]{:S(2)}) %collective-permute-start.5) | collective-permute-done | bytes 557088 | tf_op jit(solution)/shard_map/ppermute | solution.py:738
  31.9 0.2 row_total.1
  32.0 1.4 %collective-permute-start.7 = (f32[2,128,128]{2,1,0:T(8,128)S(1)}, f32[2,128,128]{2,1,0:T(8,128)S(1)}, u32[]{:S(2)}, u32[]{:S(2)}) collective-permute-start(f32[2,128,128]{2,1,0:T(8,128)S(1)} %get-tuple-element.55), channel_id=1, source_target_pairs={{0,64},{4,68},{8,72},{12,76},{16,80},{20,84},{24,88},{28,92},{32,9... | collective-permute-start | bytes 393224 | tf_op jit(solution)/shard_map/ppermute | solution.py:747
  33.4 4.8 %collective-permute-done.7.carried_ref = f32[2,128,128]{2,1,0:T(8,128)S(1)} collective-permute-done((f32[2,128,128]{2,1,0:T(8,128)S(1)}, f32[2,128,128]{2,1,0:T(8,128)S(1)}, u32[]{:S(2)}, u32[]{:S(2)}) %collective-permute-start.7) | collective-permute-done | bytes 131104 | tf_op jit(solution)/shard_map/ppermute | solution.py:747
  38.2 0.1 entering.1
  38.3 3.0 %collective-permute-start.11 = (f32[1,128,128]{2,1,0:T(8,128)S(1)}, f32[1,128,128]{2,1,0:T(8,128)S(1)}, u32[]{:S(2)}, u32[]{:S(2)}) collective-permute-start(f32[1,128,128]{2,1,0:T(8,128)S(1)} %get-tuple-element.60), channel_id=1, source_target_pairs={{0,32},{4,36},{8,40},{12,44},{16,48},{20,52},{24,56},{28,60},{32,0... | collective-permute-start | bytes 196616 | tf_op jit(solution)/shard_map/ppermute | solution.py:756
  41.3 1.1 %collective-permute-start.8 = (f32[2,128,128]{2,1,0:T(8,128)S(1)}, f32[2,128,128]{2,1,0:T(8,128)S(1)}, u32[]{:S(2)}, u32[]{:S(2)}) collective-permute-start(f32[2,128,128]{2,1,0:T(8,128)S(1)} %get-tuple-element.57), channel_id=1, source_target_pairs={{0,24},{4,44},{8,32},{12,52},{16,40},{20,60},{24,48},{28,4},{32,56... | collective-permute-start | bytes 393224 | tf_op jit(solution)/shard_map/ppermute | solution.py:756
  42.4 2.4 %collective-permute-start.9 = (f32[2,128,128]{2,1,0:T(8,128)S(1)}, f32[2,128,128]{2,1,0:T(8,128)S(1)}, u32[]{:S(2)}, u32[]{:S(2)}) collective-permute-start(f32[2,128,128]{2,1,0:T(8,128)S(1)} %get-tuple-element.58), channel_id=1, source_target_pairs={{0,16},{4,52},{8,24},{12,60},{16,32},{20,4},{24,40},{28,12},{32,48... | collective-permute-start | bytes 393224 | tf_op jit(solution)/shard_map/ppermute | solution.py:756
  44.8 0.6 collective-permute-start.10
  45.4 3.4 %own_inside.1 = (f32[768,1024]{1,0:T(8,128)S(1)}, f32[768,1024]{1,0:T(8,128)S(1)}, f32[2,8,128,128]{3,2,1,0:T(8,128)S(1)}, f32[8,128]{1,0:T(8,128)S(1)}) custom-call(f32[16]{0:T(128)S(1)} %copy-done.5, f32[24,128]{1,0:T(8,128)S(1)} %get-tuple-element.41.stats_ref.sums_ref, f32[256,48]{1,0:T(8,128)S(1)} %get-tuple-element.42.scale_ref, ...), custom_call_target="tpu_custom_call" | custom-call | flops 8000000000 | bytes 20000000 | tf_op jit(solution)/shard_map/own_inside/pallas_call | solution.py:759
  48.8 0.0 collective-permute-done.11.step4_ref
  48.8 1.2 %collective-permute-done.8.step3_ref = f32[2,128,128]{2,1,0:T(8,128)S(1)} collective-permute-done((f32[2,128,128]{2,1,0:T(8,128)S(1)}, f32[2,128,128]{2,1,0:T(8,128)S(1)}, u32[]{:S(2)}, u32[]{:S(2)}) %collective-permute-start.8) | collective-permute-done | bytes 131104 | tf_op jit(solution)/shard_map/ppermute | solution.py:756
  50.0 3.8 %collective-permute-done.9.step2_ref = f32[2,128,128]{2,1,0:T(8,128)S(1)} collective-permute-done((f32[2,128,128]{2,1,0:T(8,128)S(1)}, f32[2,128,128]{2,1,0:T(8,128)S(1)}, u32[]{:S(2)}, u32[]{:S(2)}) %collective-permute-start.9) | collective-permute-done | bytes 131104 | tf_op jit(solution)/shard_map/ppermute | solution.py:756
  53.8 0.2 collective-permute-done.10.step1_ref
  54.0 2.5 %collective-permute-start.12 = (f32[8,128,128]{2,1,0:T(8,128)S(1)}, f32[8,128,128]{2,1,0:T(8,128)S(1)}, u32[]{:S(2)}, u32[]{:S(2)}) collective-permute-start(f32[8,128,128]{2,1,0:T(8,128)S(1)} %pack_states.1.arrived_ref), channel_id=1, source_target_pairs={{0,4},{4,0},{8,12},{12,8},{16,20},{20,16},{24,28},{28,24},{32,36},... | collective-permute-start | bytes 1572872 | tf_op jit(solution)/shard_map/ppermute | solution.py:769
  56.5 1.0 %early_outputs.1 = (f32[768,1152]{1,0:T(8,128)S(1)}, f32[768,128]{1,0:T(8,128)S(1)}, f32[9,128,128]{2,1,0:T(8,128)S(1)}) custom-call(f32[2,128,128]{2,1,0:T(8,128)S(1)} %get-tuple-element.56.last_ref.here_ref, f32[8,128,128]{2,1,0:T(8,128)S(1)} %pack_states.1.arrived_ref, f32[8,136,128]{2,1,0:T(8,128)S(1)} %collective-permute-done.other_ref.own_other_ref, ...), custom_call_target="tpu_custom_call" | custom-call | flops 2000000 | bytes 9000 | tf_op jit(solution)/shard_map/early_outputs/pallas_call | solution.py:772
  57.5 0.5 collective-permute-done.12.arrived_ref
  58.0 1.0 %late_outputs.1 = (f32[768,896]{1,0:T(8,128)S(1)}, f32[8,768]{1,0:T(8,128)S(1)}, f32[7,128,128]{2,1,0:T(8,128)S(1)}) custom-call(f32[2,128,128]{2,1,0:T(8,128)S(1)} %get-tuple-element.56.last_ref.here_ref, f32[8,128,128]{2,1,0:T(8,128)S(1)} %collective-permute-done.12.arrived_ref, f32[8,136,128]{2,1,0:T(8,128)S(1)} %collective-permute-done.other_ref.own_other_ref, ...), custom_call_target="tpu_custom_call" | custom-call | flops 2000000 | bytes 9000 | tf_op jit(solution)/shard_map/late_outputs/pallas_call | solution.py:772
  58.9 2.5 %collective-permute-start.15 = (f32[8,768]{1,0:T(8,128)S(1)}, f32[8,768]{1,0:T(8,128)S(1)}, u32[]{:S(2)}, u32[]{:S(2)}) collective-permute-start(f32[8,768]{1,0:T(8,128)S(1)} %get-tuple-element.75.after_ref.sum_ref), channel_id=1, source_target_pairs={{0,3},{1,0},{2,1},{3,2},{4,7},{5,4},{6,5},{7,6},{8,11},{9,8},{10,9... | collective-permute-start | bytes 73736 | tf_op jit(solution)/shard_map/ppermute | solution.py:805
  61.5 0.5 collective-permute-start.14
  62.0 0.6 collective-permute-start.13
  62.6 2.2 %write_states.1 = (f32[3,16,128,128]{3,2,1,0:T(8,128)}, f32[8,128]{1,0:T(8,128)S(1)}) custom-call(f32[9,128,128]{2,1,0:T(8,128)S(1)} %get-tuple-element.76.early_first_ref, f32[7,128,128]{2,1,0:T(8,128)S(1)} %get-tuple-element.77.late_first_ref, f32[2,8,128,128]{3,2,1,0:T(8,128)S(1)} %get-tuple-element.65.own_before_ref, ...), custom_call_target="tpu_custom_call" | custom-call | flops 4000000000 | bytes 9000000 | tf_op jit(solution)/shard_map/write_states/pallas_call | solution.py:808
  64.8 0.0 collective-permute-done.15.c_ref
  64.8 0.8 %collective-permute-done.14.b_ref = f32[8,768]{1,0:T(8,128)S(1)} collective-permute-done((f32[8,768]{1,0:T(8,128)S(1)}, f32[8,768]{1,0:T(8,128)S(1)}, u32[]{:S(2)}, u32[]{:S(2)}) %collective-permute-start.14) | collective-permute-done | bytes 24608 | tf_op jit(solution)/shard_map/ppermute | solution.py:805
  65.6 0.3 collective-permute-done.13.a_ref
  65.9 2.1 %scale.1 = bf16[768,2048]{1,0:T(8,128)(2,1)} custom-call(f32[768,1152]{1,0:T(8,128)S(1)} %get-tuple-element.72.early_ref, f32[768,896]{1,0:T(8,128)S(1)} %get-tuple-element.74.late_ref, f32[1,2048]{1,0:T(1,128)S(1)} %bitcast.2, f32[8,768]{1,0:T(8,128)S(1)} %get-tuple-element.75.after_ref.sum_ref, f32[8,768]{1,0:T(8,128)S(1)} %collective-permute-done.13.a_ref, ...), custom_call_target="tpu_custom_call" | custom-call | flops 5000000 | bytes 6500000 | tf_op jit(solution)/shard_map/scale/pallas_call | solution.py:821
  (9 shorter events, 0.1 us)
Async XLA Ops:
  4.6 4.9 %collective-permute-start = (f32[8,136,128]{2,1,0:T(8,128)S(1)}, f32[8,136,128]{2,1,0:T(8,128)S(1)}, u32[]{:S(2)}, u32[]{:S(2)}) collective-permute-start(f32[8,136,128]{2,1,0:T(8,128)S(1)} %get-tuple-element.45), channel_id=1, source_target_pairs={{0,4},{4,0},{8,12},{12,8},{16,20},{20,16},{24,28},{28,24},{32,36},... | collective-permute-start | bytes 1671176 | tf_op jit(solution)/shard_map/ppermute | solution.py:673
  7.9 11.7 %copy-start = (bf16[768,128]{1,0:T(8,128)(2,1)S(1)}, bf16[768,128]{1,0:T(8,128)(2,1)}, u32[]{:S(2)}) copy-start(bf16[768,128]{1,0:T(8,128)(2,1)} %b_ref.1) | copy-start | bytes 589828
  7.9 11.7 %copy-start.2 = (s32[16]{0:T(128)S(1)}, s32[16]{0:T(128)}, u32[]{:S(2)}) copy-start(s32[16]{0:T(128)} %doc_ref.1) | copy-start | bytes 196
  7.9 11.7 %copy-start.3 = (bf16[768,2048]{1,0:T(8,128)(2,1)S(1)}, bf16[768,2048]{1,0:T(8,128)(2,1)}, u32[]{:S(2)}) copy-start(bf16[768,2048]{1,0:T(8,128)(2,1)} %gate_ref.3) | copy-start | bytes 9437188
  7.9 11.7 %copy-start.4 = (bf16[768,128]{1,0:T(8,128)(2,1)S(1)}, bf16[768,128]{1,0:T(8,128)(2,1)}, u32[]{:S(2)}) copy-start(bf16[768,128]{1,0:T(8,128)(2,1)} %c_ref.1) | copy-start | bytes 589828
  7.9 11.7 %copy-start.5 = (f32[16]{0:T(128)S(1)}, f32[16]{0:T(128)}, u32[]{:S(2)}) copy-start(f32[16]{0:T(128)} %skip_ref.3) | copy-start | bytes 196
  9.3 21.0 %collective-permute-start.6 = (f32[8,136,128]{2,1,0:T(8,128)S(1)}, f32[8,136,128]{2,1,0:T(8,128)S(1)}, u32[]{:S(2)}, u32[]{:S(2)}) collective-permute-start(f32[8,136,128]{2,1,0:T(8,128)S(1)} %own_states.1.own_ref), channel_id=1, source_target_pairs={{0,4},{4,0},{8,12},{12,8},{16,20},{20,16},{24,28},{28,24},{32,36},... | collective-permute-start | bytes 1671176 | tf_op jit(solution)/shard_map/ppermute | solution.py:695
  9.6 14.1 %collective-permute-start.4 = (f32[1,136,128]{2,1,0:T(8,128)S(1)}, f32[1,136,128]{2,1,0:T(8,128)S(1)}, u32[]{:S(2)}, u32[]{:S(2)}) collective-permute-start(f32[1,136,128]{2,1,0:T(8,128)S(1)} %get-tuple-element.49), channel_id=1, source_target_pairs={{0,32},{4,36},{8,40},{12,44},{16,48},{20,52},{24,56},{28,60},{32,0... | collective-permute-start | bytes 208904 | tf_op jit(solution)/shard_map/ppermute | solution.py:693
  14.8 8.8 %collective-permute-start.1 = (f32[2,136,128]{2,1,0:T(8,128)S(1)}, f32[2,136,128]{2,1,0:T(8,128)S(1)}, u32[]{:S(2)}, u32[]{:S(2)}) collective-permute-start(f32[2,136,128]{2,1,0:T(8,128)S(1)} %get-tuple-element.46), channel_id=1, source_target_pairs={{0,24},{4,44},{8,32},{12,52},{16,40},{20,60},{24,48},{28,4},{32,56... | collective-permute-start | bytes 417800 | tf_op jit(solution)/shard_map/ppermute | solution.py:693
  14.8 12.0 %collective-permute-start.2 = (f32[2,136,128]{2,1,0:T(8,128)S(1)}, f32[2,136,128]{2,1,0:T(8,128)S(1)}, u32[]{:S(2)}, u32[]{:S(2)}) collective-permute-start(f32[2,136,128]{2,1,0:T(8,128)S(1)} %get-tuple-element.47), channel_id=1, source_target_pairs={{0,16},{4,52},{8,24},{12,60},{16,32},{20,4},{24,40},{28,12},{32,48... | collective-permute-start | bytes 417800 | tf_op jit(solution)/shard_map/ppermute | solution.py:693
  18.9 9.9 %collective-permute-start.3 = (f32[2,136,128]{2,1,0:T(8,128)S(1)}, f32[2,136,128]{2,1,0:T(8,128)S(1)}, u32[]{:S(2)}, u32[]{:S(2)}) collective-permute-start(f32[2,136,128]{2,1,0:T(8,128)S(1)} %get-tuple-element.48), channel_id=1, source_target_pairs={{0,8},{4,60},{8,16},{12,4},{16,24},{20,12},{24,32},{28,20},{32,40}... | collective-permute-start | bytes 417800 | tf_op jit(solution)/shard_map/ppermute | solution.py:693
  28.8 3.0 %collective-permute-start.5 = (f32[8,136,128]{2,1,0:T(8,128)S(1)}, f32[8,136,128]{2,1,0:T(8,128)S(1)}, u32[]{:S(2)}, u32[]{:S(2)}) collective-permute-start(f32[8,136,128]{2,1,0:T(8,128)S(1)} %pack_parts.1.packed_ref), channel_id=1, source_target_pairs={{0,4},{4,0},{8,12},{12,8},{16,20},{20,16},{24,28},{28,24},{32,36},... | collective-permute-start | bytes 1671176 | tf_op jit(solution)/shard_map/ppermute | solution.py:738
  32.0 6.1 %collective-permute-start.7 = (f32[2,128,128]{2,1,0:T(8,128)S(1)}, f32[2,128,128]{2,1,0:T(8,128)S(1)}, u32[]{:S(2)}, u32[]{:S(2)}) collective-permute-start(f32[2,128,128]{2,1,0:T(8,128)S(1)} %get-tuple-element.55), channel_id=1, source_target_pairs={{0,64},{4,68},{8,72},{12,76},{16,80},{20,84},{24,88},{28,92},{32,9... | collective-permute-start | bytes 393224 | tf_op jit(solution)/shard_map/ppermute | solution.py:747
  38.3 10.5 %collective-permute-start.11 = (f32[1,128,128]{2,1,0:T(8,128)S(1)}, f32[1,128,128]{2,1,0:T(8,128)S(1)}, u32[]{:S(2)}, u32[]{:S(2)}) collective-permute-start(f32[1,128,128]{2,1,0:T(8,128)S(1)} %get-tuple-element.60), channel_id=1, source_target_pairs={{0,32},{4,36},{8,40},{12,44},{16,48},{20,52},{24,56},{28,60},{32,0... | collective-permute-start | bytes 196616 | tf_op jit(solution)/shard_map/ppermute | solution.py:756
  41.3 8.7 %collective-permute-start.8 = (f32[2,128,128]{2,1,0:T(8,128)S(1)}, f32[2,128,128]{2,1,0:T(8,128)S(1)}, u32[]{:S(2)}, u32[]{:S(2)}) collective-permute-start(f32[2,128,128]{2,1,0:T(8,128)S(1)} %get-tuple-element.57), channel_id=1, source_target_pairs={{0,24},{4,44},{8,32},{12,52},{16,40},{20,60},{24,48},{28,4},{32,56... | collective-permute-start | bytes 393224 | tf_op jit(solution)/shard_map/ppermute | solution.py:756
  42.4 11.3 %collective-permute-start.9 = (f32[2,128,128]{2,1,0:T(8,128)S(1)}, f32[2,128,128]{2,1,0:T(8,128)S(1)}, u32[]{:S(2)}, u32[]{:S(2)}) collective-permute-start(f32[2,128,128]{2,1,0:T(8,128)S(1)} %get-tuple-element.58), channel_id=1, source_target_pairs={{0,16},{4,52},{8,24},{12,60},{16,32},{20,4},{24,40},{28,12},{32,48... | collective-permute-start | bytes 393224 | tf_op jit(solution)/shard_map/ppermute | solution.py:756
  44.8 9.1 %collective-permute-start.10 = (f32[2,128,128]{2,1,0:T(8,128)S(1)}, f32[2,128,128]{2,1,0:T(8,128)S(1)}, u32[]{:S(2)}, u32[]{:S(2)}) collective-permute-start(f32[2,128,128]{2,1,0:T(8,128)S(1)} %get-tuple-element.59), channel_id=1, source_target_pairs={{0,8},{4,60},{8,16},{12,4},{16,24},{20,12},{24,32},{28,20},{32,40}... | collective-permute-start | bytes 393224 | tf_op jit(solution)/shard_map/ppermute | solution.py:756
  54.0 4.0 %collective-permute-start.12 = (f32[8,128,128]{2,1,0:T(8,128)S(1)}, f32[8,128,128]{2,1,0:T(8,128)S(1)}, u32[]{:S(2)}, u32[]{:S(2)}) collective-permute-start(f32[8,128,128]{2,1,0:T(8,128)S(1)} %pack_states.1.arrived_ref), channel_id=1, source_target_pairs={{0,4},{4,0},{8,12},{12,8},{16,20},{20,16},{24,28},{28,24},{32,36},... | collective-permute-start | bytes 1572872 | tf_op jit(solution)/shard_map/ppermute | solution.py:769
  58.9 5.9 %collective-permute-start.15 = (f32[8,768]{1,0:T(8,128)S(1)}, f32[8,768]{1,0:T(8,128)S(1)}, u32[]{:S(2)}, u32[]{:S(2)}) collective-permute-start(f32[8,768]{1,0:T(8,128)S(1)} %get-tuple-element.75.after_ref.sum_ref), channel_id=1, source_target_pairs={{0,3},{1,0},{2,1},{3,2},{4,7},{5,4},{6,5},{7,6},{8,11},{9,8},{10,9... | collective-permute-start | bytes 73736 | tf_op jit(solution)/shard_map/ppermute | solution.py:805
  61.5 4.2 %collective-permute-start.14 = (f32[8,768]{1,0:T(8,128)S(1)}, f32[8,768]{1,0:T(8,128)S(1)}, u32[]{:S(2)}, u32[]{:S(2)}) collective-permute-start(f32[8,768]{1,0:T(8,128)S(1)} %get-tuple-element.75.after_ref.sum_ref), channel_id=1, source_target_pairs={{0,2},{1,3},{2,0},{3,1},{4,6},{5,7},{6,4},{7,5},{8,10},{9,11},{10,... | collective-permute-start | bytes 73736 | tf_op jit(solution)/shard_map/ppermute | solution.py:805
  62.0 3.9 %collective-permute-start.13 = (f32[8,768]{1,0:T(8,128)S(1)}, f32[8,768]{1,0:T(8,128)S(1)}, u32[]{:S(2)}, u32[]{:S(2)}) collective-permute-start(f32[8,768]{1,0:T(8,128)S(1)} %get-tuple-element.75.after_ref.sum_ref), channel_id=1, source_target_pairs={{0,1},{1,2},{2,3},{3,0},{4,5},{5,6},{6,7},{7,4},{8,9},{9,10},{10,1... | collective-permute-start | bytes 73736 | tf_op jit(solution)/shard_map/ppermute | solution.py:805
  62.6 3.3 %copy-start.1 = (f32[2048]{0:T(1024)S(1)}, f32[2048]{0:T(1024)}, u32[]{:S(2)}) copy-start(f32[2048]{0:T(1024)} %param.16) | copy-start | bytes 24580

commit v5 on v4

--- a/solution.py
+++ b/solution.py
@@ -97,14 +97,11 @@
     return jnp.concatenate([rows[:, g * Q : (g + 1) * Q] for g in range(groups)], axis=0)
 
 
-def column_logs(step, rate_ref, heads):
+def column_logs(step, rate_ref, lower, heads):
     head_rows = lax.rem(lax.broadcasted_iota(jnp.int32, step.shape, 0), heads)
     rates = jnp.zeros_like(step)
     for slot in range(heads):
         rates = jnp.where(head_rows == slot, -rate_ref[head_of(slot, heads)], rates)
-    rows = lax.broadcasted_iota(jnp.int32, (Q, Q), 0)
-    cols = lax.broadcasted_iota(jnp.int32, (Q, Q), 1)
-    lower = jnp.where(cols <= rows, 1.0, 0.0).astype(BF16)
     return sum(
         lax.dot_general(lower, part, NT, preferred_element_type=F32)
         for part in split3(rates * step)
@@ -189,17 +186,22 @@
     ]
     for copy in small + wide:
         copy.start()
-    for copy in small:
+    stats_ref[...] = jnp.zeros_like(stats_ref)
+    rows = lax.broadcasted_iota(jnp.int32, (Q, Q), 0)
+    cols = lax.broadcasted_iota(jnp.int32, (Q, Q), 1)
+    lower = jnp.where(cols <= rows, 1.0, 0.0).astype(BF16)
+    for copy in small[:2]:
         copy.wait()
-    stats_ref[...] = jnp.zeros_like(stats_ref)
     base = lax.axis_index("seq") * (groups * Q)
     reach = jnp.ones((1, heads), F32)
     stats_ref[16:17, 0:heads] = reach
     step = stacked_groups(slot_rows(step_ref))
-    logs = column_logs(step, rate_ref, heads)
+    logs = column_logs(step, rate_ref, lower, heads)
     logs_ref[...] = logs
     scale_ref[...] = jnp.exp(-logs) * step.T
     finals = jnp.exp(logs[Q - 1 : Q, :])
+    for copy in small[2:]:
+        copy.wait()
     for group in range(groups):
         start = base + group * Q
         doc_first, next_end = group_bounds(doc_ref, start)

time: 68.3 us -> 67.9 us (level)
  no operation moved by 1% of the time
where the time goes in v5:
time: 67.9 us
  starting transfers between devices  29.5 us (43%)
  Pallas kernels  19.1 us (28%)
  waiting for transfers between devices  18.3 us (27%)
  between operations  0.92 us (1%)
    ppermute x4, starting transfers between devices, local(): arrived = [lax.ppermute(joined[k], 'seq', AROUND[k]) for k in (2, 1, 0, 3)]  10 us
    ppermute x4, starting transfers between devices, local(): returned = [lax.ppermute(steps[k], 'seq', AROUND[k]) for k in (2, 1, 0, 3)]  7.13 us
    ppermute x4, waiting for transfers between devices, local(): returned = [lax.ppermute(steps[k], 'seq', AROUND[k]) for k in (2, 1, 0, 3)]  5.12 us
    ppermute x4, waiting for transfers between devices, local(): arrived = [lax.ppermute(joined[k], 'seq', AROUND[k]) for k in (2, 1, 0, 3)]  5.11 us
    ppermute x1, waiting for transfers between devices, local(): carried = lax.ppermute(total, 'seq', NEXT_ROW)  4.75 us
    pallas_call x1, Pallas kernels, local(): pl.pallas_call(functools.partial(away_inside_kernel, heads, groups), in_s...  4.03 us
    ppermute x3, starting transfers between devices, local(): lax.ppermute(squares, 'tp', [(i, (i + k) % tp_size) for i in range(tp_siz...  3.65 us
    pallas_call x1, Pallas kernels, local(): pl.pallas_call(functools.partial(away_states_kernel, heads, groups), in_s...  3.59 us
  transfers between devices with their start and end apart: 16, of which 11 were waited for; matrix products, arithmetic and copies ran while one was open for 0% of the time, Pallas kernels for 18%

profile of v5, /device:TPU:1, one launch (start us, length us, event | category | flops | bytes accessed | tf_op | source)
XLA Modules:
  0.0 67.9 jit_solution(13113251160969112338)
XLA Ops:
  0.6 3.6 %away_states.1 = (f32[8,136,128]{2,1,0:T(8,128)S(1)}, f32[24,128]{1,0:T(8,128)S(1)}, f32[256,48]{1,0:T(8,128)S(1)}, bf16[3,128,256]{2,1,0:T(8,128)(2,1)S(1)}, f3...) custom-call(s32[16]{0:T(128)} %doc_ref.1, f32[16]{0:T(128)} %rate_hbm.1, f32[16,768]{1,0:T(8,128)} %bitcast.3, ...), custom_call_target="tpu_custom_call" | custom-call | flops 200000000 | bytes 4000000 | tf_op jit(solution)/shard_map/away_states/pallas_call | solution.py:651
  4.2 3.3 %collective-permute-start = (f32[8,136,128]{2,1,0:T(8,128)S(1)}, f32[8,136,128]{2,1,0:T(8,128)S(1)}, u32[]{:S(2)}, u32[]{:S(2)}) collective-permute-start(f32[8,136,128]{2,1,0:T(8,128)S(1)} %get-tuple-element.45), channel_id=1, source_target_pairs={{0,4},{4,0},{8,12},{12,8},{16,20},{20,16},{24,28},{28,24},{32,36},... | collective-permute-start | bytes 1671176 | tf_op jit(solution)/shard_map/ppermute | solution.py:675
  7.6 0.0 copy-start.5
  7.6 1.3 %own_states.1.own_ref = f32[8,136,128]{2,1,0:T(8,128)S(1)} custom-call(f32[24,128]{1,0:T(8,128)S(1)} %get-tuple-element.41.stats_ref.sums_ref, f32[256,48]{1,0:T(8,128)S(1)} %get-tuple-element.42.scale_ref, bf16[3,128,256]{2,1,0:T(8,128)(2,1)S(1)} %get-tuple-element.43.tail_ref, bf16[768,2048]{1,0:T(8,128)(2,1)S(1)} %get-tuple-element.44.x_ref), custom_call_target="tpu_custom_call" | custom-call | flops 2000000000 | bytes 4000000 | tf_op jit(solution)/shard_map/own_states/pallas_call | solution.py:677
  8.9 0.1 collective-permute-start.6
  9.0 0.1 collective-permute-done.other_ref.own_other_ref
  9.1 0.1 join_cores.1
  9.2 5.2 %collective-permute-start.4 = (f32[1,136,128]{2,1,0:T(8,128)S(1)}, f32[1,136,128]{2,1,0:T(8,128)S(1)}, u32[]{:S(2)}, u32[]{:S(2)}) collective-permute-start(f32[1,136,128]{2,1,0:T(8,128)S(1)} %get-tuple-element.49), channel_id=1, source_target_pairs={{0,32},{4,36},{8,40},{12,44},{16,48},{20,52},{24,56},{28,60},{32,0... | collective-permute-start | bytes 208904 | tf_op jit(solution)/shard_map/ppermute | solution.py:695
  14.5 0.0 collective-permute-start.1
  14.5 4.1 %collective-permute-start.2 = (f32[2,136,128]{2,1,0:T(8,128)S(1)}, f32[2,136,128]{2,1,0:T(8,128)S(1)}, u32[]{:S(2)}, u32[]{:S(2)}) collective-permute-start(f32[2,136,128]{2,1,0:T(8,128)S(1)} %get-tuple-element.47), channel_id=1, source_target_pairs={{0,16},{4,52},{8,24},{12,60},{16,32},{20,4},{24,40},{28,12},{32,48... | collective-permute-start | bytes 417800 | tf_op jit(solution)/shard_map/ppermute | solution.py:695
  18.5 0.7 %collective-permute-start.3 = (f32[2,136,128]{2,1,0:T(8,128)S(1)}, f32[2,136,128]{2,1,0:T(8,128)S(1)}, u32[]{:S(2)}, u32[]{:S(2)}) collective-permute-start(f32[2,136,128]{2,1,0:T(8,128)S(1)} %get-tuple-element.48), channel_id=1, source_target_pairs={{0,8},{4,60},{8,16},{12,4},{16,24},{20,12},{24,32},{28,20},{32,40}... | collective-permute-start | bytes 417800 | tf_op jit(solution)/shard_map/ppermute | solution.py:695
  19.3 0.0 copy-done
  19.3 0.0 copy-done.2
  19.3 0.0 copy-done.3
  19.3 0.0 copy-done.4
  19.3 4.0 %away_inside.1 = (f32[768,1024]{1,0:T(8,128)S(1)}, f32[768,1024]{1,0:T(8,128)S(1)}, f32[2,8,128,128]{3,2,1,0:T(8,128)S(1)}, bf16[768,128]{1,0:T(8,128)(2,1)S(1)}...) custom-call(s32[16]{0:T(128)S(1)} %copy-done.2, f32[16]{0:T(128)S(1)} %copy-done.5, ...), custom_call_target="tpu_custom_call" | custom-call | flops 8000000000 | bytes 20000000 | tf_op jit(solution)/shard_map/away_inside/pallas_call | solution.py:699
  23.3 0.0 collective-permute-done.4.step4_ref
  23.3 0.0 collective-permute-done.1.step3_ref
  23.3 3.1 %collective-permute-done.2.step2_ref = f32[2,136,128]{2,1,0:T(8,128)S(1)} collective-permute-done((f32[2,136,128]{2,1,0:T(8,128)S(1)}, f32[2,136,128]{2,1,0:T(8,128)S(1)}, u32[]{:S(2)}, u32[]{:S(2)}) %collective-permute-start.2) | collective-permute-done | bytes 139296 | tf_op jit(solution)/shard_map/ppermute | solution.py:695
  26.5 2.0 %collective-permute-done.3.step1_ref = f32[2,136,128]{2,1,0:T(8,128)S(1)} collective-permute-done((f32[2,136,128]{2,1,0:T(8,128)S(1)}, f32[2,136,128]{2,1,0:T(8,128)S(1)}, u32[]{:S(2)}, u32[]{:S(2)}) %collective-permute-start.3) | collective-permute-done | bytes 139296 | tf_op jit(solution)/shard_map/ppermute | solution.py:695
  28.5 1.4 %collective-permute-start.5 = (f32[8,136,128]{2,1,0:T(8,128)S(1)}, f32[8,136,128]{2,1,0:T(8,128)S(1)}, u32[]{:S(2)}, u32[]{:S(2)}) collective-permute-start(f32[8,136,128]{2,1,0:T(8,128)S(1)} %pack_parts.1.packed_ref), channel_id=1, source_target_pairs={{0,4},{4,0},{8,12},{12,8},{16,20},{20,16},{24,28},{28,24},{32,36},... | collective-permute-start | bytes 1671176 | tf_op jit(solution)/shard_map/ppermute | solution.py:740
  29.9 0.0 collective-permute-done.6.after_ref.away_other_ref
  29.9 1.6 %collective-permute-done.5.swapped_ref = f32[8,136,128]{2,1,0:T(8,128)S(1)} collective-permute-done((f32[8,136,128]{2,1,0:T(8,128)S(1)}, f32[8,136,128]{2,1,0:T(8,128)S(1)}, u32[]{:S(2)}, u32[]{:S(2)}) %collective-permute-start.5) | collective-permute-done | bytes 557088 | tf_op jit(solution)/shard_map/ppermute | solution.py:740
  31.5 0.2 row_total.1
  31.7 1.4 %collective-permute-start.7 = (f32[2,128,128]{2,1,0:T(8,128)S(1)}, f32[2,128,128]{2,1,0:T(8,128)S(1)}, u32[]{:S(2)}, u32[]{:S(2)}) collective-permute-start(f32[2,128,128]{2,1,0:T(8,128)S(1)} %get-tuple-element.55), channel_id=1, source_target_pairs={{0,64},{4,68},{8,72},{12,76},{16,80},{20,84},{24,88},{28,92},{32,9... | collective-permute-start | bytes 393224 | tf_op jit(solution)/shard_map/ppermute | solution.py:749
  33.0 4.8 %collective-permute-done.7.carried_ref = f32[2,128,128]{2,1,0:T(8,128)S(1)} collective-permute-done((f32[2,128,128]{2,1,0:T(8,128)S(1)}, f32[2,128,128]{2,1,0:T(8,128)S(1)}, u32[]{:S(2)}, u32[]{:S(2)}) %collective-permute-start.7) | collective-permute-done | bytes 131104 | tf_op jit(solution)/shard_map/ppermute | solution.py:749
  37.8 0.1 entering.1
  37.9 3.0 %collective-permute-start.11 = (f32[1,128,128]{2,1,0:T(8,128)S(1)}, f32[1,128,128]{2,1,0:T(8,128)S(1)}, u32[]{:S(2)}, u32[]{:S(2)}) collective-permute-start(f32[1,128,128]{2,1,0:T(8,128)S(1)} %get-tuple-element.60), channel_id=1, source_target_pairs={{0,32},{4,36},{8,40},{12,44},{16,48},{20,52},{24,56},{28,60},{32,0... | collective-permute-start | bytes 196616 | tf_op jit(solution)/shard_map/ppermute | solution.py:758
  41.0 1.1 %collective-permute-start.8 = (f32[2,128,128]{2,1,0:T(8,128)S(1)}, f32[2,128,128]{2,1,0:T(8,128)S(1)}, u32[]{:S(2)}, u32[]{:S(2)}) collective-permute-start(f32[2,128,128]{2,1,0:T(8,128)S(1)} %get-tuple-element.57), channel_id=1, source_target_pairs={{0,24},{4,44},{8,32},{12,52},{16,40},{20,60},{24,48},{28,4},{32,56... | collective-permute-start | bytes 393224 | tf_op jit(solution)/shard_map/ppermute | solution.py:758
  42.1 2.4 %collective-permute-start.9 = (f32[2,128,128]{2,1,0:T(8,128)S(1)}, f32[2,128,128]{2,1,0:T(8,128)S(1)}, u32[]{:S(2)}, u32[]{:S(2)}) collective-permute-start(f32[2,128,128]{2,1,0:T(8,128)S(1)} %get-tuple-element.58), channel_id=1, source_target_pairs={{0,16},{4,52},{8,24},{12,60},{16,32},{20,4},{24,40},{28,12},{32,48... | collective-permute-start | bytes 393224 | tf_op jit(solution)/shard_map/ppermute | solution.py:758
  44.5 0.6 collective-permute-start.10
  45.1 3.4 %own_inside.1 = (f32[768,1024]{1,0:T(8,128)S(1)}, f32[768,1024]{1,0:T(8,128)S(1)}, f32[2,8,128,128]{3,2,1,0:T(8,128)S(1)}, f32[8,128]{1,0:T(8,128)S(1)}) custom-call(f32[16]{0:T(128)S(1)} %copy-done.5, f32[24,128]{1,0:T(8,128)S(1)} %get-tuple-element.41.stats_ref.sums_ref, f32[256,48]{1,0:T(8,128)S(1)} %get-tuple-element.42.scale_ref, ...), custom_call_target="tpu_custom_call" | custom-call | flops 8000000000 | bytes 20000000 | tf_op jit(solution)/shard_map/own_inside/pallas_call | solution.py:761
  48.5 0.0 collective-permute-done.11.step4_ref
  48.5 1.2 %collective-permute-done.8.step3_ref = f32[2,128,128]{2,1,0:T(8,128)S(1)} collective-permute-done((f32[2,128,128]{2,1,0:T(8,128)S(1)}, f32[2,128,128]{2,1,0:T(8,128)S(1)}, u32[]{:S(2)}, u32[]{:S(2)}) %collective-permute-start.8) | collective-permute-done | bytes 131104 | tf_op jit(solution)/shard_map/ppermute | solution.py:758
  49.7 3.8 %collective-permute-done.9.step2_ref = f32[2,128,128]{2,1,0:T(8,128)S(1)} collective-permute-done((f32[2,128,128]{2,1,0:T(8,128)S(1)}, f32[2,128,128]{2,1,0:T(8,128)S(1)}, u32[]{:S(2)}, u32[]{:S(2)}) %collective-permute-start.9) | collective-permute-done | bytes 131104 | tf_op jit(solution)/shard_map/ppermute | solution.py:758
  53.4 0.2 collective-permute-done.10.step1_ref
  53.6 2.4 %collective-permute-start.12 = (f32[8,128,128]{2,1,0:T(8,128)S(1)}, f32[8,128,128]{2,1,0:T(8,128)S(1)}, u32[]{:S(2)}, u32[]{:S(2)}) collective-permute-start(f32[8,128,128]{2,1,0:T(8,128)S(1)} %pack_states.1.arrived_ref), channel_id=1, source_target_pairs={{0,4},{4,0},{8,12},{12,8},{16,20},{20,16},{24,28},{28,24},{32,36},... | collective-permute-start | bytes 1572872 | tf_op jit(solution)/shard_map/ppermute | solution.py:771
  56.1 1.0 %early_outputs.1 = (f32[768,1152]{1,0:T(8,128)S(1)}, f32[768,128]{1,0:T(8,128)S(1)}, f32[9,128,128]{2,1,0:T(8,128)S(1)}) custom-call(f32[2,128,128]{2,1,0:T(8,128)S(1)} %get-tuple-element.56.last_ref.here_ref, f32[8,128,128]{2,1,0:T(8,128)S(1)} %pack_states.1.arrived_ref, f32[8,136,128]{2,1,0:T(8,128)S(1)} %collective-permute-done.other_ref.own_other_ref, ...), custom_call_target="tpu_custom_call" | custom-call | flops 2000000 | bytes 9000 | tf_op jit(solution)/shard_map/early_outputs/pallas_call | solution.py:774
  57.1 0.5 collective-permute-done.12.arrived_ref
  57.6 0.9 %late_outputs.1 = (f32[768,896]{1,0:T(8,128)S(1)}, f32[8,768]{1,0:T(8,128)S(1)}, f32[7,128,128]{2,1,0:T(8,128)S(1)}) custom-call(f32[2,128,128]{2,1,0:T(8,128)S(1)} %get-tuple-element.56.last_ref.here_ref, f32[8,128,128]{2,1,0:T(8,128)S(1)} %collective-permute-done.12.arrived_ref, f32[8,136,128]{2,1,0:T(8,128)S(1)} %collective-permute-done.other_ref.own_other_ref, ...), custom_call_target="tpu_custom_call" | custom-call | flops 2000000 | bytes 9000 | tf_op jit(solution)/shard_map/late_outputs/pallas_call | solution.py:774
  58.6 2.5 %collective-permute-start.15 = (f32[8,768]{1,0:T(8,128)S(1)}, f32[8,768]{1,0:T(8,128)S(1)}, u32[]{:S(2)}, u32[]{:S(2)}) collective-permute-start(f32[8,768]{1,0:T(8,128)S(1)} %get-tuple-element.75.after_ref.sum_ref), channel_id=1, source_target_pairs={{0,3},{1,0},{2,1},{3,2},{4,7},{5,4},{6,5},{7,6},{8,11},{9,8},{10,9... | collective-permute-start | bytes 73736 | tf_op jit(solution)/shard_map/ppermute | solution.py:807
  61.1 0.5 collective-permute-start.14
  61.6 0.6 collective-permute-start.13
  62.2 2.2 %write_states.1 = (f32[3,16,128,128]{3,2,1,0:T(8,128)}, f32[8,128]{1,0:T(8,128)S(1)}) custom-call(f32[9,128,128]{2,1,0:T(8,128)S(1)} %get-tuple-element.76.early_first_ref, f32[7,128,128]{2,1,0:T(8,128)S(1)} %get-tuple-element.77.late_first_ref, f32[2,8,128,128]{3,2,1,0:T(8,128)S(1)} %get-tuple-element.65.own_before_ref, ...), custom_call_target="tpu_custom_call" | custom-call | flops 4000000000 | bytes 9000000 | tf_op jit(solution)/shard_map/write_states/pallas_call | solution.py:810
  64.4 0.0 collective-permute-done.15.c_ref
  64.4 0.8 %collective-permute-done.14.b_ref = f32[8,768]{1,0:T(8,128)S(1)} collective-permute-done((f32[8,768]{1,0:T(8,128)S(1)}, f32[8,768]{1,0:T(8,128)S(1)}, u32[]{:S(2)}, u32[]{:S(2)}) %collective-permute-start.14) | collective-permute-done | bytes 24608 | tf_op jit(solution)/shard_map/ppermute | solution.py:807
  65.3 0.3 collective-permute-done.13.a_ref
  65.6 2.1 %scale.1 = bf16[768,2048]{1,0:T(8,128)(2,1)} custom-call(f32[768,1152]{1,0:T(8,128)S(1)} %get-tuple-element.72.early_ref, f32[768,896]{1,0:T(8,128)S(1)} %get-tuple-element.74.late_ref, f32[1,2048]{1,0:T(1,128)S(1)} %bitcast.2, f32[8,768]{1,0:T(8,128)S(1)} %get-tuple-element.75.after_ref.sum_ref, f32[8,768]{1,0:T(8,128)S(1)} %collective-permute-done.13.a_ref, ...), custom_call_target="tpu_custom_call" | custom-call | flops 5000000 | bytes 6500000 | tf_op jit(solution)/shard_map/scale/pallas_call | solution.py:823
  (9 shorter events, 0.1 us)
Async XLA Ops:
  4.2 4.9 %collective-permute-start = (f32[8,136,128]{2,1,0:T(8,128)S(1)}, f32[8,136,128]{2,1,0:T(8,128)S(1)}, u32[]{:S(2)}, u32[]{:S(2)}) collective-permute-start(f32[8,136,128]{2,1,0:T(8,128)S(1)} %get-tuple-element.45), channel_id=1, source_target_pairs={{0,4},{4,0},{8,12},{12,8},{16,20},{20,16},{24,28},{28,24},{32,36},... | collective-permute-start | bytes 1671176 | tf_op jit(solution)/shard_map/ppermute | solution.py:675
  7.6 11.7 %copy-start = (bf16[768,128]{1,0:T(8,128)(2,1)S(1)}, bf16[768,128]{1,0:T(8,128)(2,1)}, u32[]{:S(2)}) copy-start(bf16[768,128]{1,0:T(8,128)(2,1)} %b_ref.1) | copy-start | bytes 589828
  7.6 11.7 %copy-start.2 = (s32[16]{0:T(128)S(1)}, s32[16]{0:T(128)}, u32[]{:S(2)}) copy-start(s32[16]{0:T(128)} %doc_ref.1) | copy-start | bytes 196
  7.6 11.7 %copy-start.3 = (bf16[768,2048]{1,0:T(8,128)(2,1)S(1)}, bf16[768,2048]{1,0:T(8,128)(2,1)}, u32[]{:S(2)}) copy-start(bf16[768,2048]{1,0:T(8,128)(2,1)} %gate_ref.3) | copy-start | bytes 9437188
  7.6 11.7 %copy-start.4 = (bf16[768,128]{1,0:T(8,128)(2,1)S(1)}, bf16[768,128]{1,0:T(8,128)(2,1)}, u32[]{:S(2)}) copy-start(bf16[768,128]{1,0:T(8,128)(2,1)} %c_ref.1) | copy-start | bytes 589828
  7.6 11.7 %copy-start.5 = (f32[16]{0:T(128)S(1)}, f32[16]{0:T(128)}, u32[]{:S(2)}) copy-start(f32[16]{0:T(128)} %skip_ref.3) | copy-start | bytes 196
  8.9 21.0 %collective-permute-start.6 = (f32[8,136,128]{2,1,0:T(8,128)S(1)}, f32[8,136,128]{2,1,0:T(8,128)S(1)}, u32[]{:S(2)}, u32[]{:S(2)}) collective-permute-start(f32[8,136,128]{2,1,0:T(8,128)S(1)} %own_states.1.own_ref), channel_id=1, source_target_pairs={{0,4},{4,0},{8,12},{12,8},{16,20},{20,16},{24,28},{28,24},{32,36},... | collective-permute-start | bytes 1671176 | tf_op jit(solution)/shard_map/ppermute | solution.py:697
  9.2 14.1 %collective-permute-start.4 = (f32[1,136,128]{2,1,0:T(8,128)S(1)}, f32[1,136,128]{2,1,0:T(8,128)S(1)}, u32[]{:S(2)}, u32[]{:S(2)}) collective-permute-start(f32[1,136,128]{2,1,0:T(8,128)S(1)} %get-tuple-element.49), channel_id=1, source_target_pairs={{0,32},{4,36},{8,40},{12,44},{16,48},{20,52},{24,56},{28,60},{32,0... | collective-permute-start | bytes 208904 | tf_op jit(solution)/shard_map/ppermute | solution.py:695
  14.5 8.9 %collective-permute-start.1 = (f32[2,136,128]{2,1,0:T(8,128)S(1)}, f32[2,136,128]{2,1,0:T(8,128)S(1)}, u32[]{:S(2)}, u32[]{:S(2)}) collective-permute-start(f32[2,136,128]{2,1,0:T(8,128)S(1)} %get-tuple-element.46), channel_id=1, source_target_pairs={{0,24},{4,44},{8,32},{12,52},{16,40},{20,60},{24,48},{28,4},{32,56... | collective-permute-start | bytes 417800 | tf_op jit(solution)/shard_map/ppermute | solution.py:695
  14.5 12.0 %collective-permute-start.2 = (f32[2,136,128]{2,1,0:T(8,128)S(1)}, f32[2,136,128]{2,1,0:T(8,128)S(1)}, u32[]{:S(2)}, u32[]{:S(2)}) collective-permute-start(f32[2,136,128]{2,1,0:T(8,128)S(1)} %get-tuple-element.47), channel_id=1, source_target_pairs={{0,16},{4,52},{8,24},{12,60},{16,32},{20,4},{24,40},{28,12},{32,48... | collective-permute-start | bytes 417800 | tf_op jit(solution)/shard_map/ppermute | solution.py:695
  18.5 9.9 %collective-permute-start.3 = (f32[2,136,128]{2,1,0:T(8,128)S(1)}, f32[2,136,128]{2,1,0:T(8,128)S(1)}, u32[]{:S(2)}, u32[]{:S(2)}) collective-permute-start(f32[2,136,128]{2,1,0:T(8,128)S(1)} %get-tuple-element.48), channel_id=1, source_target_pairs={{0,8},{4,60},{8,16},{12,4},{16,24},{20,12},{24,32},{28,20},{32,40}... | collective-permute-start | bytes 417800 | tf_op jit(solution)/shard_map/ppermute | solution.py:695
  28.5 3.0 %collective-permute-start.5 = (f32[8,136,128]{2,1,0:T(8,128)S(1)}, f32[8,136,128]{2,1,0:T(8,128)S(1)}, u32[]{:S(2)}, u32[]{:S(2)}) collective-permute-start(f32[8,136,128]{2,1,0:T(8,128)S(1)} %pack_parts.1.packed_ref), channel_id=1, source_target_pairs={{0,4},{4,0},{8,12},{12,8},{16,20},{20,16},{24,28},{28,24},{32,36},... | collective-permute-start | bytes 1671176 | tf_op jit(solution)/shard_map/ppermute | solution.py:740
  31.7 6.1 %collective-permute-start.7 = (f32[2,128,128]{2,1,0:T(8,128)S(1)}, f32[2,128,128]{2,1,0:T(8,128)S(1)}, u32[]{:S(2)}, u32[]{:S(2)}) collective-permute-start(f32[2,128,128]{2,1,0:T(8,128)S(1)} %get-tuple-element.55), channel_id=1, source_target_pairs={{0,64},{4,68},{8,72},{12,76},{16,80},{20,84},{24,88},{28,92},{32,9... | collective-permute-start | bytes 393224 | tf_op jit(solution)/shard_map/ppermute | solution.py:749
  37.9 10.5 %collective-permute-start.11 = (f32[1,128,128]{2,1,0:T(8,128)S(1)}, f32[1,128,128]{2,1,0:T(8,128)S(1)}, u32[]{:S(2)}, u32[]{:S(2)}) collective-permute-start(f32[1,128,128]{2,1,0:T(8,128)S(1)} %get-tuple-element.60), channel_id=1, source_target_pairs={{0,32},{4,36},{8,40},{12,44},{16,48},{20,52},{24,56},{28,60},{32,0... | collective-permute-start | bytes 196616 | tf_op jit(solution)/shard_map/ppermute | solution.py:758
  41.0 8.7 %collective-permute-start.8 = (f32[2,128,128]{2,1,0:T(8,128)S(1)}, f32[2,128,128]{2,1,0:T(8,128)S(1)}, u32[]{:S(2)}, u32[]{:S(2)}) collective-permute-start(f32[2,128,128]{2,1,0:T(8,128)S(1)} %get-tuple-element.57), channel_id=1, source_target_pairs={{0,24},{4,44},{8,32},{12,52},{16,40},{20,60},{24,48},{28,4},{32,56... | collective-permute-start | bytes 393224 | tf_op jit(solution)/shard_map/ppermute | solution.py:758
  42.1 11.3 %collective-permute-start.9 = (f32[2,128,128]{2,1,0:T(8,128)S(1)}, f32[2,128,128]{2,1,0:T(8,128)S(1)}, u32[]{:S(2)}, u32[]{:S(2)}) collective-permute-start(f32[2,128,128]{2,1,0:T(8,128)S(1)} %get-tuple-element.58), channel_id=1, source_target_pairs={{0,16},{4,52},{8,24},{12,60},{16,32},{20,4},{24,40},{28,12},{32,48... | collective-permute-start | bytes 393224 | tf_op jit(solution)/shard_map/ppermute | solution.py:758
  44.5 9.1 %collective-permute-start.10 = (f32[2,128,128]{2,1,0:T(8,128)S(1)}, f32[2,128,128]{2,1,0:T(8,128)S(1)}, u32[]{:S(2)}, u32[]{:S(2)}) collective-permute-start(f32[2,128,128]{2,1,0:T(8,128)S(1)} %get-tuple-element.59), channel_id=1, source_target_pairs={{0,8},{4,60},{8,16},{12,4},{16,24},{20,12},{24,32},{28,20},{32,40}... | collective-permute-start | bytes 393224 | tf_op jit(solution)/shard_map/ppermute | solution.py:758
  53.6 4.0 %collective-permute-start.12 = (f32[8,128,128]{2,1,0:T(8,128)S(1)}, f32[8,128,128]{2,1,0:T(8,128)S(1)}, u32[]{:S(2)}, u32[]{:S(2)}) collective-permute-start(f32[8,128,128]{2,1,0:T(8,128)S(1)} %pack_states.1.arrived_ref), channel_id=1, source_target_pairs={{0,4},{4,0},{8,12},{12,8},{16,20},{20,16},{24,28},{28,24},{32,36},... | collective-permute-start | bytes 1572872 | tf_op jit(solution)/shard_map/ppermute | solution.py:771
  58.6 5.9 %collective-permute-start.15 = (f32[8,768]{1,0:T(8,128)S(1)}, f32[8,768]{1,0:T(8,128)S(1)}, u32[]{:S(2)}, u32[]{:S(2)}) collective-permute-start(f32[8,768]{1,0:T(8,128)S(1)} %get-tuple-element.75.after_ref.sum_ref), channel_id=1, source_target_pairs={{0,3},{1,0},{2,1},{3,2},{4,7},{5,4},{6,5},{7,6},{8,11},{9,8},{10,9... | collective-permute-start | bytes 73736 | tf_op jit(solution)/shard_map/ppermute | solution.py:807
  61.1 4.2 %collective-permute-start.14 = (f32[8,768]{1,0:T(8,128)S(1)}, f32[8,768]{1,0:T(8,128)S(1)}, u32[]{:S(2)}, u32[]{:S(2)}) collective-permute-start(f32[8,768]{1,0:T(8,128)S(1)} %get-tuple-element.75.after_ref.sum_ref), channel_id=1, source_target_pairs={{0,2},{1,3},{2,0},{3,1},{4,6},{5,7},{6,4},{7,5},{8,10},{9,11},{10,... | collective-permute-start | bytes 73736 | tf_op jit(solution)/shard_map/ppermute | solution.py:807
  61.6 3.9 %collective-permute-start.13 = (f32[8,768]{1,0:T(8,128)S(1)}, f32[8,768]{1,0:T(8,128)S(1)}, u32[]{:S(2)}, u32[]{:S(2)}) collective-permute-start(f32[8,768]{1,0:T(8,128)S(1)} %get-tuple-element.75.after_ref.sum_ref), channel_id=1, source_target_pairs={{0,1},{1,2},{2,3},{3,0},{4,5},{5,6},{6,7},{7,4},{8,9},{9,10},{10,1... | collective-permute-start | bytes 73736 | tf_op jit(solution)/shard_map/ppermute | solution.py:807
  62.2 3.3 %copy-start.1 = (f32[2048]{0:T(1024)S(1)}, f32[2048]{0:T(1024)}, u32[]{:S(2)}) copy-start(f32[2048]{0:T(1024)} %param.16) | copy-start | bytes 24580
